TPU v7x, 256 devices: a whole 4x4x8 slice. The times are simulated.
256 devices in a mesh: head: 4 (over x_hi, core), inner: 8 (over z), outer: 8 (over y, x_lo).
Axes of the slice: x: 4 (x_hi: 2, x_lo: 2; x = x_hi * 2 + x_lo), y: 4, z: 8, core: 2. Of those that a mesh axis runs over, the one named last changes fastest.
Arguments:
- query: bfloat16 [32768, 4096], P(('head', 'inner', 'outer')), may hold values from -4.5 to 4.5, as said below
- key_value: bfloat16 [32768, 1024], P(('head', 'inner', 'outer')), may hold values from -4.5 to 4.5
- grad_out: bfloat16 [32768, 4096], P(('head', 'inner', 'outer')), may hold values from -6 to 6
- positions: int32 [32768], P(('head', 'inner', 'outer')), may hold values from 0 to 32767, as said below
Outputs:
- attn_out: bfloat16 [32768, 4096], P(('head', 'inner', 'outer'))
- grad_query: bfloat16 [32768, 4096], P(('head', 'inner', 'outer'))
- grad_kv: float32 [32768, 1024], P(('head', 'inner', 'outer'))
Inputs may be any that keep to these rules, and one draw needn't show every extreme that they name: `query`: every entry lies within the range; entries of one row may be alike in size or sign across heads. A permutation of 0 to 32767. Number the rows i = h * 64 * 128 + g * 128 + r with r below 128, and take the rows of one g in the order of h and then r: the first 256 of them hold consecutive positions from b * 256 on, the last 256 consecutive positions from (127 - b) * 256 on, for a b that differs from g to g.
All inputs are finite; a program needn't handle non-finite values.
Results may differ from a plain program's by a relative error of at most 0.022.
Values may be sent and summed in bfloat16 or wider, within the bound.
No kernel may reach another device: no remote copies, remote signals or barrier semaphores. Data moves between devices by JAX's collectives and lax.ppermute only.
A program may use at most 128 MiB of HBM per device.

v0:
```python
import functools
import math

import jax
import jax.numpy as jnp
from jax import lax
from jax.experimental import pallas as pl
from jax.experimental.pallas import tpu as pltpu
from jax.sharding import PartitionSpec as P

D = 128
PIECE = 128
HALF = 256
ROWS = 512
HEADER = 16
BLOCKS = 128
SCALE = 1.0 / math.sqrt(D)
EXP2_SCALE = SCALE * math.log2(math.e)
VMEM_LIMIT = 48 * 2**20
f32, bf16 = jnp.float32, jnp.bfloat16
NT = (((1,), (1,)), ((), ()))
NN = (((1,), (0,)), ((), ()))
SUMS = 16


def dot(a, b, dims):
    return lax.dot_general(a, b, dims, preferred_element_type=f32)


def place(h, ref):
    b = jnp.max(ref[ROWS : ROWS + HEADER, :].astype(f32)).astype(jnp.int32)
    swapped = jnp.where(b < BLOCKS // 2, 0, 1) ^ (h // 2)
    early = pl.multiple_of(swapped * HALF, HALF)
    return jnp.minimum(b, BLOCKS - 1 - b), early, pl.multiple_of(HALF - early, HALF)


def causal(h):
    def position(axis):
        row = lax.broadcasted_iota(jnp.int32, (HALF, HALF), axis)
        return jnp.where(h % 2 == 0, row, (row + PIECE) % HALF)

    return position(0) <= position(1)


class Layout:
    def __init__(self, h, own_ref, windows, with_own):
        self.b, self.q_early, self.q_late = place(h, own_ref)
        self.blocks, self.spots = [], []
        if with_own:
            self.spots += [(0, 0), (0, 1), (0, 2)]
            self.blocks += [
                (own_ref, self.q_early, self.q_early, True, True),
                (own_ref, self.q_early, self.q_late, False, False),
                (own_ref, self.q_late, self.q_late, False, True),
            ]
        for group, ref in enumerate(windows):
            self.spots += [(group + with_own, 0), (group + with_own, 1)]
            b, k_early, k_late = place(h, ref)
            first = b < self.b
            key_row = pl.multiple_of(jnp.where(first, k_early, k_late), HALF)
            query_row = pl.multiple_of(jnp.where(first, self.q_early, self.q_late), HALF)
            self.blocks += [
                (ref, k_early, self.q_late, False, False),
                (ref, key_row, query_row, first, False),
            ]


def split(flag, x):
    if flag is True:
        return x, None
    if flag is False:
        return None, x
    return jnp.where(flag, x, 0.0), jnp.where(flag, 0.0, x)


def add(total, x):
    return total if x is None else x if total is None else total + x


STRIP = 64


def at(refs, layout, a, n):
    group, index = layout.spots[n]
    return refs[group].at[a, index]


def cols(ref, row, n, head):
    return ref[pl.ds(row, n), head * D : (head + 1) * D]


def weigh_blocks(layout, heads, q_ref, mask, vt_ref, s_ref, w_refs, old):
    tops = [[None, None] if old is None else list(old[a]) for a in range(heads)]
    for a in range(heads):
        for n, (keys, key_row, query_row, first, masked) in enumerate(layout.blocks):
            s = dot(keys[pl.ds(key_row, HALF), :D], cols(q_ref, query_row, HALF, a), NT)
            if masked:
                s = jnp.where(mask, s, -1e30)
            s_ref[a, n] = s
            top = jnp.max(s, axis=0, keepdims=True)
            for half in range(2):
                if first is (half == 1):
                    continue
                t = top
                if first is not True and first is not False:
                    t = jnp.where(first if half == 0 else jnp.logical_not(first), top, -1e30)
                tops[a][half] = t if tops[a][half] is None else jnp.maximum(tops[a][half], t)
    acc = [[None, None] for _ in range(heads)]
    for a in range(heads):
        for n, (keys, key_row, query_row, first, masked) in enumerate(layout.blocks):
            if first is True:
                m = tops[a][0]
            elif first is False:
                m = tops[a][1]
            else:
                m = jnp.where(first, tops[a][0], tops[a][1])
            w_ref = at(w_refs, layout, a, n)
            for r in range(0, HALF, STRIP):
                x = s_ref[a, n, r : r + STRIP, :]
                w_ref[r : r + STRIP, :] = jnp.exp2((x - m) * EXP2_SCALE).astype(bf16)
            for half, x in enumerate(split(first, dot(vt_ref[n], w_ref[...], NN))):
                acc[a][half] = add(acc[a][half], x)
    return tops, acc


def load_vt(layout, vt_ref):
    @pl.when(pl.program_id(0) == 0)
    def _():
        for n, (keys, key_row, *_) in enumerate(layout.blocks):
            vt_ref[n, :D, :] = jnp.transpose(keys[pl.ds(key_row, HALF), D:], (1, 0))
            vt_ref[n, D:, :] = jnp.ones((SUMS, HALF), bf16)


def fwd_first_kernel(heads, h_ref, q0, q1, q2, q3, own, *refs):
    n_win = (len(refs) - 6) // 2
    windows, refs = refs[:n_win], refs[n_win:]
    w_refs = refs[3 : 4 + n_win]
    q_out, state_ref, top_ref = refs[:3]
    vt_ref, s_ref = refs[4 + n_win :]
    h = h_ref[0]
    layout = Layout(h, own, windows, True)
    load_vt(layout, vt_ref)
    for k, piece in enumerate((q0, q1, q2, q3)):
        q_out[k * PIECE : (k + 1) * PIECE, :] = piece[...]
    tops, acc = weigh_blocks(layout, heads, q_out, causal(h), vt_ref, s_ref, w_refs, None)
    for a in range(heads):
        for half in range(2):
            state_ref[a, half] = acc[a][half]
            top_ref[a, half] = jnp.broadcast_to(tops[a][half], (8, HALF))


def fwd_last_kernel(heads, h_ref, q_ref, g0, g1, g2, g3, own, win, state_in, top_in,
                    o0, o1, o2, o3, g_out, gb_out, w_ref, vt_ref, s_ref, g_ref, o_ref):
    h = h_ref[0]
    layout = Layout(h, own, [win], False)
    load_vt(layout, vt_ref)
    for k, piece in enumerate((g0, g1, g2, g3)):
        g_ref[k * PIECE : (k + 1) * PIECE, :] = piece[...]
    old = [[top_in[a, half, :1, :] for half in range(2)] for a in range(heads)]
    tops, acc = weigh_blocks(layout, heads, q_ref, None, vt_ref, s_ref, [w_ref], old)
    for a in range(heads):
        for half, row in enumerate((layout.q_early, layout.q_late)):
            shrink = jnp.exp2((old[a][half] - tops[a][half]) * EXP2_SCALE)
            t = state_in[a, half] * shrink + acc[a][half]
            r = 1.0 / t[D : D + 1]
            out = jnp.transpose(t[:D] * r, (1, 0)).astype(bf16)
            o_ref[pl.ds(row, HALF), a * D : (a + 1) * D] = out
            g = cols(g_ref, row, HALF, a).astype(f32)
            for ref, factor in ((g_out, r * shrink), (gb_out, r)):
                scaled = g * jnp.transpose(jnp.broadcast_to(factor, (D, HALF)), (1, 0))
                ref[pl.ds(row, HALF), 2 * a * D : (2 * a + 1) * D] = scaled.astype(bf16)
                ref[pl.ds(row, HALF), (2 * a + 1) * D : (2 * a + 2) * D] = (
                    -scaled * out.astype(f32)).astype(bf16)
    for k, ref in enumerate((o0, o1, o2, o3)):
        ref[...] = o_ref[k * PIECE : (k + 1) * PIECE, :]


PAY_SPEC = pl.BlockSpec((ROWS + HEADER, 2 * D), lambda j, h: (0, 0))


def piece_spec(heads):
    return pl.BlockSpec((PIECE, heads * D), lambda j, h: (0, j))


def rows_spec(heads):
    return pl.BlockSpec((ROWS, heads * D), lambda j, h: (0, j))


def w_spec(heads, n):
    return pl.BlockSpec((heads, n, HALF, HALF), lambda j, h: (j, 0, 0, 0))


def half_spec(heads, n):
    return pl.BlockSpec((heads, 2, n, HALF), lambda j, h: (j, 0, 0, 0))


def call(kernel, name, steps, ins, in_specs, outs, out_specs, scratch, flops, exps=0):
    return pl.pallas_call(
        kernel,
        grid_spec=pltpu.PrefetchScalarGridSpec(
            num_scalar_prefetch=1, grid=(steps,), in_specs=in_specs, out_specs=out_specs,
            scratch_shapes=scratch),
        out_shape=outs,
        compiler_params=pltpu.CompilerParams(vmem_limit_bytes=VMEM_LIMIT),
        cost_estimate=pl.CostEstimate(flops=flops, bytes_accessed=8 * 2**20, transcendentals=exps),
        name=name,
    )(*ins)


def shape(*dims, dtype=bf16):
    return jax.ShapeDtypeStruct(dims, dtype)


STEP_FIRST, STEP_LAST, STEP_A, STEP_B, STEP_C = 2, 4, 8, 2, 2


def forward_first(h, q, own, windows):
    heads = q[0].shape[1] // D
    n = 3 + 2 * len(windows)
    e = STEP_FIRST
    return call(
        functools.partial(fwd_first_kernel, e), "forward_first", heads // e, (h, *q, own, *windows),
        [piece_spec(e)] * 4 + [PAY_SPEC] * (1 + len(windows)),
        [shape(ROWS, heads * D), shape(heads, 2, D + SUMS, HALF, dtype=f32),
         shape(heads, 2, 8, HALF, dtype=f32), shape(heads, 3, HALF, HALF)]
        + [shape(heads, 2, HALF, HALF)] * len(windows),
        [rows_spec(e), half_spec(e, D + SUMS), half_spec(e, 8), w_spec(e, 3)]
        + [w_spec(e, 2)] * len(windows),
        [pltpu.VMEM((n, D + SUMS, HALF), bf16), pltpu.VMEM((e, n, HALF, HALF), f32)],
        heads * n * 4 * HALF * HALF * D, heads * n * HALF * HALF)


def forward_last(h, q_rows, g, own, window, state, top):
    heads = q_rows.shape[1] // D
    e = STEP_LAST
    return call(
        functools.partial(fwd_last_kernel, e), "forward_last", heads // e,
        (h, q_rows, *g, own, window, state, top),
        [rows_spec(e)] + [piece_spec(e)] * 4 + [PAY_SPEC] * 2 + [half_spec(e, D + SUMS), half_spec(e, 8)],
        [shape(PIECE, heads * D)] * 4 + [shape(ROWS, heads * 2 * D)] * 2 + [shape(heads, 2, HALF, HALF)],
        [piece_spec(e)] * 4 + [rows_spec(2 * e)] * 2 + [w_spec(e, 2)],
        [pltpu.VMEM((2, D + SUMS, HALF), bf16), pltpu.VMEM((e, 2, HALF, HALF), f32),
         pltpu.VMEM((ROWS, e * D), bf16), pltpu.VMEM((ROWS, e * D), bf16)],
        heads * 2 * 4 * HALF * HALF * D, heads * 2 * HALF * HALF)


def bwd_kernel(heads, n_win, with_own, first, last, h_ref, q_ref, ga_ref, own, *refs):
    windows, refs = refs[:n_win], refs[n_win:]
    n_terms = n_win + with_own
    w_refs, refs = refs[:n_terms], refs[n_terms:]
    if not first:
        d_in, refs = refs[0], refs[1:]
    if last:
        d_outs, refs = refs[:4], refs[4:]
    else:
        d_out, refs = refs[0], refs[1:]
    terms, refs = refs[:n_terms], refs[n_terms:]
    kt_ref, va_ref, acc_ref, ds_ref = refs[:4]
    h = h_ref[0]
    layout = Layout(h, own, windows, with_own)
    j = pl.program_id(0)

    @pl.when(j == 0)
    def _():
        for n, (keys, key_row, *_) in enumerate(layout.blocks):
            kt_ref[n] = jnp.transpose(keys[pl.ds(key_row, HALF), :D], (1, 0))
            va_ref[n, :, :D] = keys[pl.ds(key_row, HALF), D:]
            va_ref[n, :, D:] = jnp.ones((HALF, D), bf16)
        acc_ref[...] = jnp.zeros_like(acc_ref)

    total = [[None, None] if first else [d_in[a, 0], d_in[a, 1]] for a in range(heads)]

    def grads(row, a, width):
        return ga_ref[pl.ds(row, HALF), 2 * a * D : (2 * a + width) * D]

    for n, (keys, key_row, query_row, early, masked) in enumerate(layout.blocks):
        for a in range(heads):
            dp = dot(va_ref[n], grads(query_row, a, 2), NT)
            ds_ref[a, n] = (at(w_refs, layout, a, n)[...].astype(f32) * dp).astype(bf16)
    for n, (keys, key_row, query_row, early, masked) in enumerate(layout.blocks):
        value_sum = key_sum = None
        for a in range(heads):
            value_sum = add(value_sum, dot(at(w_refs, layout, a, n)[...], grads(query_row, a, 1), NN))
            key_sum = add(key_sum, dot(ds_ref[a, n], cols(q_ref, query_row, HALF, a), NN))
            for half, x in enumerate(split(early, dot(kt_ref[n], ds_ref[a, n], NN))):
                total[a][half] = add(total[a][half], x)
        acc_ref[n, :, D:] += value_sum
        acc_ref[n, :, :D] += key_sum
    if last:
        d_ref = refs[4]
        for a in range(heads):
            for row, d in ((layout.q_early, total[a][0]), (layout.q_late, total[a][1])):
                d_ref[pl.ds(row, HALF), a * D : (a + 1) * D] = jnp.transpose(d * SCALE, (1, 0)).astype(bf16)
        for k, ref in enumerate(d_outs):
            ref[...] = d_ref[k * PIECE : (k + 1) * PIECE, :]
    else:
        for a in range(heads):
            for half in range(2):
                d_out[a, half] = total[a][half]

    @pl.when(j == pl.num_programs(0) - 1)
    def _():
        n = 0
        for term in terms:
            if with_own and n == 0:
                parts = [(layout.q_early, acc_ref[0] + acc_ref[1]), (layout.q_late, acc_ref[2])]
                n = 3
            else:
                flag = layout.blocks[n + 1][3]
                k_early = layout.blocks[n][1]
                x, y = acc_ref[n], acc_ref[n + 1]
                parts = [
                    (k_early, x + jnp.where(flag, y, 0.0)),
                    (pl.multiple_of(HALF - k_early, HALF), jnp.where(flag, 0.0, y)),
                ]
                n += 2
            for row, x in parts:
                term[pl.ds(row, HALF), :D] = (x[:, :D] * SCALE).astype(bf16)
                term[pl.ds(row, HALF), D:] = x[:, D:].astype(bf16)


def backward(name, e, h, q_rows, ga, own, windows, w, d=None, with_own=False, last=False):
    heads = q_rows.shape[1] // D
    n = 3 * with_own + 2 * len(windows)
    n_terms = with_own + len(windows)
    first = d is None
    return call(
        functools.partial(bwd_kernel, e, len(windows), with_own, first, last), name, heads // e,
        (h, q_rows, ga, own, *windows, *w) + (() if first else (d,)),
        [rows_spec(e), rows_spec(2 * e)] + [PAY_SPEC] * (1 + len(windows))
        + [w_spec(e, 3)] * with_own + [w_spec(e, 2)] * len(windows)
        + ([] if first else [half_spec(e, D)]),
        ([shape(PIECE, heads * D)] * 4 if last else [shape(heads, 2, D, HALF, dtype=f32)])
        + [shape(ROWS, 2 * D)] * n_terms,
        ([piece_spec(e)] * 4 if last else [half_spec(e, D)])
        + [pl.BlockSpec((ROWS, 2 * D), lambda j, h: (0, 0))] * n_terms,
        [pltpu.VMEM((n, D, HALF), bf16), pltpu.VMEM((n, HALF, 2 * D), bf16),
         pltpu.VMEM((n, HALF, 2 * D), f32), pltpu.VMEM((e, n, HALF, HALF), bf16)]
        + ([pltpu.VMEM((ROWS, e * D), bf16)] if last else []),
        heads * n * 8 * HALF * HALF * D)


def place_kernel(h_ref, p0, p1, p2, p3, out):
    width = p0.shape[1]
    for k, piece in enumerate((p0, p1, p2, p3)):
        column = pl.multiple_of((h_ref[0] ^ k) * width, width)
        out[:, pl.ds(column, width)] = piece[...].astype(out.dtype)


def placed(h, pieces, dtype=bf16):
    rows, width = pieces[0].shape
    return pl.pallas_call(
        place_kernel,
        in_specs=[pl.BlockSpec(memory_space=pltpu.SMEM)] + [pl.BlockSpec(memory_space=pltpu.VMEM)] * 4,
        out_specs=pl.BlockSpec(memory_space=pltpu.VMEM),
        out_shape=shape(rows, 4 * width, dtype=dtype),
        cost_estimate=pl.CostEstimate(flops=0, bytes_accessed=16 * rows * width, transcendentals=0),
        name="placed",
    )(h, *pieces)


def after(x, earlier):
    return lax.optimization_barrier((x, earlier))[0]


def swap(x, k):
    return lax.ppermute(x, "head", [(i, i ^ k) for i in range(4)])


def along(x, axis, distance):
    n = lax.axis_size(axis)
    return lax.ppermute(x, axis, [(i, (i + distance) % n) for i in range(n)])


def columns(h, x, k):
    width = x.shape[1] // 4
    return lax.dynamic_slice(x, (0, (h ^ k) * width), (x.shape[0], width))


def to_heads(h, x, earlier=None):
    pieces = [columns(h, x, k) for k in range(4)]
    if earlier is not None:
        pieces = pieces[:1] + [after(pieces[k], earlier[k]) for k in (1, 2, 3)]
    return from_heads(pieces)


def from_heads(pieces):
    return [pieces[0]] + [swap(pieces[k], k) for k in (1, 2, 3)]


def plus(x, y):
    return (x.astype(f32) + y.astype(f32)).astype(bf16)


def local(query, key_value, grad_out, positions):
    h = lax.axis_index("head")
    h_arg = jnp.full((1,), h, jnp.int32)
    block = positions[0] // HALF
    b = jnp.where(h < 2, block, BLOCKS - 1 - block)
    header = jnp.broadcast_to(b.astype(bf16), (HEADER, 2 * D))
    kv = to_heads(h, key_value)
    own = jnp.concatenate(kv + [header], axis=0)
    q = to_heads(h, query, kv)
    g = to_heads(h, grad_out, q)
    before = along(own, ("inner", "outer"), 1)
    w1 = along(own, "inner", 1)
    w2 = along(w1, "inner", 1)
    w3 = along(w2, "inner", 1)
    q_rows, state, top, wo, ww2, wwb, ww1 = forward_first(h_arg, q, own, [w2, before, w1])
    *out, ga, gb, ww3 = forward_last(h_arg, q_rows, g, own, w3, state, top)
    out = from_heads(out)
    d, t3 = backward("backward_a", STEP_A, h_arg, q_rows, gb, own, [w3], [ww3])
    s2 = along(t3, "inner", -1)
    d, t2, tb = backward("backward_b", STEP_B, h_arg, q_rows, ga, own, [w2, before], [ww2, wwb], d)
    s1 = along(plus(t2, s2), "inner", -1)
    back = along(tb, ("inner", "outer"), -1)
    *dq, t0, t1 = backward(
        "backward_c", STEP_C, h_arg, q_rows, ga, own, [w1], [wo, ww1], d, with_own=True, last=True)
    s0 = along(plus(t1, s1), "inner", -1)
    dq = from_heads(dq[:1] + [after(dq[k], out[k]) for k in (1, 2, 3)])
    dkv = (t0.astype(f32) + s0.astype(f32) + back.astype(f32)).astype(bf16)
    dkv = from_heads([dkv[k * PIECE : (k + 1) * PIECE] for k in range(4)])
    return placed(h_arg, out), placed(h_arg, dq), placed(h_arg, dkv, f32)


def solution(mesh):
    spec = P(("head", "inner", "outer"), None)
    return jax.shard_map(
        local,
        mesh=mesh,
        in_specs=(spec, spec, spec, P(("head", "inner", "outer"))),
        out_specs=(spec, spec, spec),
        check_vma=False,
    )
```

profile of v0, /device:TPU:1, one launch (start us, length us, event | category | flops | bytes accessed | tf_op | source)
XLA Modules:
  0.0 129.2 jit_solution(11441878347616614533)
XLA Ops:
  0.7 1.0 dynamic-slice_dynamic-update-slice_fusion
  1.7 3.3 %collective-permute-start = (bf16[128,256]{1,0:T(8,128)(2,1)S(1)}, bf16[128,256]{1,0:T(8,128)(2,1)S(1)}, u32[]{:S(2)}, u32[]{:S(2)}) collective-permute-start(bf16[128,256]{1,0:T(8,128)(2,1)S(1)} %get-tuple-element.85), channel_id=1, source_target_pairs={{0,64},{64,0},{128,192},{192,128},{1,65},{65,1},{129,193},{193,129... | collective-permute-start | bytes 196616 | tf_op jit(solution)/shard_map/ppermute | solution.py:367
  5.0 1.0 collective-permute-start.2
  6.1 2.2 %collective-permute-start.4 = (bf16[128,256]{1,0:T(8,128)(2,1)S(1)}, bf16[128,256]{1,0:T(8,128)(2,1)S(1)}, u32[]{:S(2)}, u32[]{:S(2)}) collective-permute-start(bf16[128,256]{1,0:T(8,128)(2,1)S(1)} %get-tuple-element.86), channel_id=1, source_target_pairs={{0,192},{64,128},{128,64},{192,0},{1,193},{65,129},{129,65},{193,1... | collective-permute-start | bytes 196616 | tf_op jit(solution)/shard_map/ppermute | solution.py:367
  10.9 0.9 collective-permute-done.4
  11.9 1.5 %collective-permute-start.6 = (bf16[528,256]{1,0:T(8,128)(2,1)S(1)}, bf16[528,256]{1,0:T(8,128)(2,1)S(1)}, u32[]{:S(2)}, u32[]{:S(2)}) collective-permute-start(bf16[528,256]{1,0:T(8,128)(2,1)S(1)} %constant_dynamic-update-slice_fusion.own), channel_id=1, source_target_pairs={{0,8},{8,16},{16,24},{24,32},{32,40},{40,48},{48,56},{56,0},{1,9},... | collective-permute-start | bytes 811016 | tf_op jit(solution)/shard_map/ppermute | solution.py:372
  13.4 10.5 %collective-permute-done.6.refs_2_.refs_0_ = bf16[528,256]{1,0:T(8,128)(2,1)S(1)} collective-permute-done((bf16[528,256]{1,0:T(8,128)(2,1)S(1)}, bf16[528,256]{1,0:T(8,128)(2,1)S(1)}, u32[]{:S(2)}, u32[]{:S(2)}) %collective-permute-start.6) | collective-permute-done | bytes 270368 | tf_op jit(solution)/shard_map/ppermute | solution.py:372
  23.9 0.0 collective-permute-start.7
  23.9 1.3 constant_dynamic-slice_fusion.5
  25.1 2.0 %collective-permute-start.5 = (bf16[128,1024]{1,0:T(8,128)(2,1)S(1)}, bf16[128,1024]{1,0:T(8,128)(2,1)S(1)}, u32[]{:S(2)}, u32[]{:S(2)}) collective-permute-start(bf16[128,1024]{1,0:T(8,128)(2,1)S(1)} %get-tuple-element.39), channel_id=1, source_target_pairs={{0,192},{64,128},{128,64},{192,0},{1,193},{65,129},{129,65},{193,1... | collective-permute-start | bytes 786440 | tf_op jit(solution)/shard_map/ppermute | solution.py:367
  27.1 1.8 %collective-permute-start.3 = (bf16[128,1024]{1,0:T(8,128)(2,1)S(1)}, bf16[128,1024]{1,0:T(8,128)(2,1)S(1)}, u32[]{:S(2)}, u32[]{:S(2)}) collective-permute-start(bf16[128,1024]{1,0:T(8,128)(2,1)S(1)} %get-tuple-element.38), channel_id=1, source_target_pairs={{0,128},{64,192},{128,0},{192,64},{1,129},{65,193},{129,1},{193,65... | collective-permute-start | bytes 786440 | tf_op jit(solution)/shard_map/ppermute | solution.py:367
  28.9 0.3 collective-permute-start.8
  29.3 2.9 %collective-permute-done.7.refs_0_ = bf16[528,256]{1,0:T(8,128)(2,1)S(1)} collective-permute-done((bf16[528,256]{1,0:T(8,128)(2,1)S(1)}, bf16[528,256]{1,0:T(8,128)(2,1)S(1)}, u32[]{:S(2)}, u32[]{:S(2)}) %collective-permute-start.7) | collective-permute-done | bytes 270368 | tf_op jit(solution)/shard_map/ppermute | solution.py:372
  32.2 0.0 collective-permute-start.12
  32.2 0.1 constant_dynamic-slice_fusion
  32.3 3.1 %collective-permute-done.5.q3 = bf16[128,1024]{1,0:T(8,128)(2,1)S(1)} collective-permute-done((bf16[128,1024]{1,0:T(8,128)(2,1)S(1)}, bf16[128,1024]{1,0:T(8,128)(2,1)S(1)}, u32[]{:S(2)}, u32[]{:S(2)}) %collective-permute-start.5) | collective-permute-done | bytes 262176 | tf_op jit(solution)/shard_map/ppermute | solution.py:367
  35.4 0.0 collective-permute-done.1.q1
  35.4 6.0 %collective-permute-done.3.q2 = bf16[128,1024]{1,0:T(8,128)(2,1)S(1)} collective-permute-done((bf16[128,1024]{1,0:T(8,128)(2,1)S(1)}, bf16[128,1024]{1,0:T(8,128)(2,1)S(1)}, u32[]{:S(2)}, u32[]{:S(2)}) %collective-permute-start.3) | collective-permute-done | bytes 262176 | tf_op jit(solution)/shard_map/ppermute | solution.py:367
  41.4 1.2 collective-permute-start.10
  42.6 0.6 collective-permute-start.9
  43.2 1.6 %collective-permute-start.11 = (bf16[128,1024]{1,0:T(8,128)(2,1)S(1)}, bf16[128,1024]{1,0:T(8,128)(2,1)S(1)}, u32[]{:S(2)}, u32[]{:S(2)}) collective-permute-start(bf16[128,1024]{1,0:T(8,128)(2,1)S(1)} %get-tuple-element.43), channel_id=1, source_target_pairs={{0,192},{64,128},{128,64},{192,0},{1,193},{65,129},{129,65},{193,1... | collective-permute-start | bytes 786440 | tf_op jit(solution)/shard_map/ppermute | solution.py:367
  44.8 10.8 %forward_first.1 = (bf16[512,1024]{1,0:T(8,128)(2,1)S(1)}, f32[8,2,144,256]{3,2,1,0:T(8,128)}, f32[8,2,8,256]{3,2,1,0:T(8,128)S(1)}, bf16[8,3,256,256]{3,2,1,0:T...) custom-call(s32[1]{0:T(128)} %bitcast.h_ref, ...), custom_call_target="tpu_custom_call" | custom-call | flops 2415919104 | bytes 8388608 | tf_op jit(solution)/shard_map/forward_first/pallas_call | solution.py:198
  55.6 1.3 %copy-done.3 = bf16[8,2,256,256]{3,2,1,0:T(8,128)(2,1)} copy-done((bf16[8,2,256,256]{3,2,1,0:T(8,128)(2,1)}, bf16[8,2,256,256]{3,2,1,0:T(8,128)(2,1)S(1)}, u32[]{:S(2)}) %copy-start.3) | copy-done | bytes 2097176
  56.9 0.0 collective-permute-done.9.g1
  56.9 1.2 collective-permute-done.11.g3
  58.1 0.0 collective-permute-done.12.win.refs_0_
  58.1 7.1 %forward_last.1 = (bf16[128,1024]{1,0:T(8,128)(2,1)S(1)}, bf16[128,1024]{1,0:T(8,128)(2,1)S(1)}, bf16[128,1024]{1,0:T(8,128)(2,1)S(1)}, bf16[128,1024]{1,0:T(8,1...) custom-call(s32[1]{0:T(128)} %bitcast.h_ref, ...), custom_call_target="tpu_custom_call" | custom-call | flops 536870912 | bytes 8388608 | tf_op jit(solution)/shard_map/forward_last/pallas_call | solution.py:198
  65.2 1.4 %copy-done = bf16[512,2048]{1,0:T(8,128)(2,1)} copy-done((bf16[512,2048]{1,0:T(8,128)(2,1)}, bf16[512,2048]{1,0:T(8,128)(2,1)S(1)}, u32[]{:S(2)}) %copy-start) | copy-done | bytes 2097176
  66.5 0.7 copy-done.6
  67.2 1.6 %copy-done.2 = bf16[512,2048]{1,0:T(8,128)(2,1)S(1)} copy-done((bf16[512,2048]{1,0:T(8,128)(2,1)S(1)}, bf16[512,2048]{1,0:T(8,128)(2,1)}, u32[]{:S(2)}) %copy-start.2) | copy-done | bytes 2097176
  68.8 4.0 %backward_a.1 = (f32[8,2,128,256]{3,2,1,0:T(8,128)S(1)}, bf16[512,256]{1,0:T(8,128)(2,1)S(1)}) custom-call(s32[1]{0:T(128)} %bitcast.h_ref, bf16[512,1024]{1,0:T(8,128)(2,1)S(1)} %get-tuple-element.40.q_ref, bf16[512,2048]{1,0:T(8,128)(2,1)S(1)} %copy-done.2, bf16[528,256]{1,0:T(8,128)(2,1)S(1)} %constant_dynamic-update-slice_fusion.own, ...), custom_call_target="tpu_custom_call" | custom-call | flops 1073741824 | bytes 8388608 | tf_op jit(solution)/shard_map/backward_a/pallas_call | solution.py:198
  72.8 1.3 %copy-done.5 = f32[8,2,128,256]{3,2,1,0:T(8,128)} copy-done((f32[8,2,128,256]{3,2,1,0:T(8,128)}, f32[8,2,128,256]{3,2,1,0:T(8,128)S(1)}, u32[]{:S(2)}) %copy-start.5) | copy-done | bytes 2097176
  74.1 2.5 %collective-permute-start.19 = (bf16[512,256]{1,0:T(8,128)(2,1)S(1)}, bf16[512,256]{1,0:T(8,128)(2,1)S(1)}, u32[]{:S(2)}, u32[]{:S(2)}) collective-permute-start(bf16[512,256]{1,0:T(8,128)(2,1)S(1)} %get-tuple-element.69), channel_id=1, source_target_pairs={{0,56},{8,0},{16,8},{24,16},{32,24},{40,32},{48,40},{56,48},{1,57}... | collective-permute-start | bytes 786440 | tf_op jit(solution)/shard_map/ppermute | solution.py:372
  76.6 7.6 %backward_b.1 = (f32[8,2,128,256]{3,2,1,0:T(8,128)S(1)}, bf16[512,256]{1,0:T(8,128)(2,1)S(1)}, bf16[512,256]{1,0:T(8,128)(2,1)S(1)}) custom-call(s32[1]{0:T(128)} %bitcast.h_ref, bf16[512,1024]{1,0:T(8,128)(2,1)S(1)} %get-tuple-element.40.q_ref, bf16[512,2048]{1,0:T(8,128)(2,1)} %copy-done, bf16[528,256]{1,0:T(8,128)(2,1)S(1)} %constant_dynamic-update-slice_fusion.own, ...), custom_call_target="tpu_custom_call" | custom-call | flops 2147483648 | bytes 8388608 | tf_op jit(solution)/shard_map/backward_b/pallas_call | solution.py:198
  84.2 1.3 %copy-done.4 = f32[8,2,128,256]{3,2,1,0:T(8,128)} copy-done((f32[8,2,128,256]{3,2,1,0:T(8,128)}, f32[8,2,128,256]{3,2,1,0:T(8,128)S(1)}, u32[]{:S(2)}) %copy-start.4) | copy-done | bytes 2097176
  85.6 0.0 collective-permute-done.19
  85.6 0.1 add_convert_fusion.2
  85.6 0.1 collective-permute-start.20
  85.7 1.3 collective-permute-start.13
  87.0 1.4 %collective-permute-start.14 = (bf16[128,1024]{1,0:T(8,128)(2,1)S(1)}, bf16[128,1024]{1,0:T(8,128)(2,1)S(1)}, u32[]{:S(2)}, u32[]{:S(2)}) collective-permute-start(bf16[128,1024]{1,0:T(8,128)(2,1)S(1)} %get-tuple-element.48), channel_id=1, source_target_pairs={{0,128},{64,192},{128,0},{192,64},{1,129},{65,193},{129,1},{193,65... | collective-permute-start | bytes 786440 | tf_op jit(solution)/shard_map/ppermute | solution.py:367
  88.4 1.7 %collective-permute-start.15 = (bf16[128,1024]{1,0:T(8,128)(2,1)S(1)}, bf16[128,1024]{1,0:T(8,128)(2,1)S(1)}, u32[]{:S(2)}, u32[]{:S(2)}) collective-permute-start(bf16[128,1024]{1,0:T(8,128)(2,1)S(1)} %get-tuple-element.49), channel_id=1, source_target_pairs={{0,192},{64,128},{128,64},{192,0},{1,193},{65,129},{129,65},{193,1... | collective-permute-start | bytes 786440 | tf_op jit(solution)/shard_map/ppermute | solution.py:367
  90.1 7.0 %collective-permute-start.22 = (bf16[512,256]{1,0:T(8,128)(2,1)S(1)}, bf16[512,256]{1,0:T(8,128)(2,1)S(1)}, u32[]{:S(2)}, u32[]{:S(2)}) collective-permute-start(bf16[512,256]{1,0:T(8,128)(2,1)S(1)} %get-tuple-element.70), channel_id=1, source_target_pairs={{0,63},{1,0},{2,1},{3,2},{4,3},{5,4},{6,5},{7,6},{8,7},{9,8},{10,9... | collective-permute-start | bytes 786440 | tf_op jit(solution)/shard_map/ppermute | solution.py:372
  97.1 8.8 %backward_c.1 = (bf16[128,1024]{1,0:T(8,128)(2,1)S(1)}, bf16[128,1024]{1,0:T(8,128)(2,1)S(1)}, bf16[128,1024]{1,0:T(8,128)(2,1)S(1)}, bf16[128,1024]{1,0:T(8,128...) custom-call(s32[1]{0:T(128)} %bitcast.h_ref, bf16[512,1024]{1,0:T(8,128)(2,1)S(1)} %get-tuple-element.40.q_ref, ...), custom_call_target="tpu_custom_call" | custom-call | flops 2684354560 | bytes 8388608 | tf_op jit(solution)/shard_map/backward_c/pallas_call | solution.py:198
  106.0 0.1 add_convert_fusion.1
  106.1 1.6 %collective-permute-start.21 = (bf16[512,256]{1,0:T(8,128)(2,1)S(1)}, bf16[512,256]{1,0:T(8,128)(2,1)S(1)}, u32[]{:S(2)}, u32[]{:S(2)}) collective-permute-start(bf16[512,256]{1,0:T(8,128)(2,1)S(1)} %add_convert_fusion.1), channel_id=1, source_target_pairs={{0,56},{8,0},{16,8},{24,16},{32,24},{40,32},{48,40},{56,48},{1,57}... | collective-permute-start | bytes 786440 | tf_op jit(solution)/shard_map/ppermute | solution.py:372
  107.7 0.0 collective-permute-done.13.p1
  107.7 0.1 collective-permute-done.15.p3
  107.8 2.4 %collective-permute-start.18 = (bf16[128,1024]{1,0:T(8,128)(2,1)S(1)}, bf16[128,1024]{1,0:T(8,128)(2,1)S(1)}, u32[]{:S(2)}, u32[]{:S(2)}) collective-permute-start(bf16[128,1024]{1,0:T(8,128)(2,1)S(1)} %get-tuple-element.65), channel_id=1, source_target_pairs={{0,192},{64,128},{128,64},{192,0},{1,193},{65,129},{129,65},{193,1... | collective-permute-start | bytes 786440 | tf_op jit(solution)/shard_map/ppermute | solution.py:367
  110.2 1.3 collective-permute-start.17
  111.5 2.1 %collective-permute-done.21 = bf16[512,256]{1,0:T(8,128)(2,1)S(1)} collective-permute-done((bf16[512,256]{1,0:T(8,128)(2,1)S(1)}, bf16[512,256]{1,0:T(8,128)(2,1)S(1)}, u32[]{:S(2)}, u32[]{:S(2)}) %collective-permute-start.21) | collective-permute-done | bytes 262176 | tf_op jit(solution)/shard_map/ppermute | solution.py:372
  113.5 0.1 add_convert_fusion
  113.6 0.6 fusion
  114.3 2.9 %collective-permute-start.25 = (bf16[128,256]{1,0:T(8,128)(2,1)S(1)}, bf16[128,256]{1,0:T(8,128)(2,1)S(1)}, u32[]{:S(2)}, u32[]{:S(2)}) collective-permute-start(bf16[128,256]{1,0:T(8,128)(2,1)S(1)} %get-tuple-element.79), channel_id=1, source_target_pairs={{0,192},{64,128},{128,64},{192,0},{1,193},{65,129},{129,65},{193,1... | collective-permute-start | bytes 196616 | tf_op jit(solution)/shard_map/ppermute | solution.py:367
  117.2 1.3 collective-permute-start.24
  118.5 0.2 collective-permute-start.23
  118.7 2.2 %placed.3 = bf16[128,4096]{1,0:T(8,128)(2,1)} custom-call(s32[1]{0:T(128)} %bitcast.h_ref, bf16[128,1024]{1,0:T(8,128)(2,1)} %copy-done.6, bf16[128,1024]{1,0:T(8,128)(2,1)} %copy-done.9, bf16[128,1024]{1,0:T(8,128)(2,1)} %copy-done.10, bf16[128,1024]{1,0:T(8,128)(2,1)} %copy-done.11), custom_call_target="tpu_custom_call" | custom-call | bytes 2097152 | tf_op jit(solution)/shard_map/placed/pallas_call | solution.py:352
  120.9 2.8 %collective-permute-done.17.p2 = bf16[128,1024]{1,0:T(8,128)(2,1)S(1)} collective-permute-done((bf16[128,1024]{1,0:T(8,128)(2,1)S(1)}, bf16[128,1024]{1,0:T(8,128)(2,1)S(1)}, u32[]{:S(2)}, u32[]{:S(2)}) %collective-permute-start.17) | collective-permute-done | bytes 262176 | tf_op jit(solution)/shard_map/ppermute | solution.py:367
  123.7 0.7 copy-done.13
  124.4 0.1 copy-done.14
  124.5 2.2 %placed.4 = bf16[128,4096]{1,0:T(8,128)(2,1)} custom-call(s32[1]{0:T(128)} %bitcast.h_ref, bf16[128,1024]{1,0:T(8,128)(2,1)} %copy-done.7, bf16[128,1024]{1,0:T(8,128)(2,1)} %copy-done.14, bf16[128,1024]{1,0:T(8,128)(2,1)} %copy-done.13, bf16[128,1024]{1,0:T(8,128)(2,1)} %copy-done.12), custom_call_target="tpu_custom_call" | custom-call | bytes 2097152 | tf_op jit(solution)/shard_map/placed/pallas_call | solution.py:352
  126.8 0.6 copy-done.15
  127.4 0.0 copy-done.16
  127.4 0.0 copy-done.17
  127.4 1.8 %placed.5 = f32[128,1024]{1,0:T(8,128)} custom-call(s32[1]{0:T(128)} %bitcast.h_ref, bf16[128,256]{1,0:T(8,128)(2,1)} %get-tuple-element.82.p0, bf16[128,256]{1,0:T(8,128)(2,1)} %copy-done.17, bf16[128,256]{1,0:T(8,128)(2,1)} %copy-done.16, bf16[128,256]{1,0:T(8,128)(2,1)} %copy-done.15), custom_call_target="tpu_custom_call" | custom-call | bytes 524288 | tf_op jit(solution)/shard_map/placed/pallas_call | solution.py:352
  (43 shorter events, 0.1 us)
Async XLA Ops:
  0.6 31.6 %copy-start.8 = (bf16[128,4096]{1,0:T(8,128)(2,1)S(1)}, bf16[128,4096]{1,0:T(8,128)(2,1)}, u32[]{:S(2)}) copy-start(bf16[128,4096]{1,0:T(8,128)(2,1)} %param.6) | copy-start | bytes 3145732
  1.7 9.2 %collective-permute-start = (bf16[128,256]{1,0:T(8,128)(2,1)S(1)}, bf16[128,256]{1,0:T(8,128)(2,1)S(1)}, u32[]{:S(2)}, u32[]{:S(2)}) collective-permute-start(bf16[128,256]{1,0:T(8,128)(2,1)S(1)} %get-tuple-element.85), channel_id=1, source_target_pairs={{0,64},{64,0},{128,192},{192,128},{1,65},{65,1},{129,193},{193,129... | collective-permute-start | bytes 196616 | tf_op jit(solution)/shard_map/ppermute | solution.py:367
  5.0 5.9 %collective-permute-start.2 = (bf16[128,256]{1,0:T(8,128)(2,1)S(1)}, bf16[128,256]{1,0:T(8,128)(2,1)S(1)}, u32[]{:S(2)}, u32[]{:S(2)}) collective-permute-start(bf16[128,256]{1,0:T(8,128)(2,1)S(1)} %get-tuple-element.84), channel_id=1, source_target_pairs={{0,128},{64,192},{128,0},{192,64},{1,129},{65,193},{129,1},{193,65... | collective-permute-start | bytes 196616 | tf_op jit(solution)/shard_map/ppermute | solution.py:367
  6.1 5.8 %collective-permute-start.4 = (bf16[128,256]{1,0:T(8,128)(2,1)S(1)}, bf16[128,256]{1,0:T(8,128)(2,1)S(1)}, u32[]{:S(2)}, u32[]{:S(2)}) collective-permute-start(bf16[128,256]{1,0:T(8,128)(2,1)S(1)} %get-tuple-element.86), channel_id=1, source_target_pairs={{0,192},{64,128},{128,64},{192,0},{1,193},{65,129},{129,65},{193,1... | collective-permute-start | bytes 196616 | tf_op jit(solution)/shard_map/ppermute | solution.py:367
  11.9 12.0 %collective-permute-start.6 = (bf16[528,256]{1,0:T(8,128)(2,1)S(1)}, bf16[528,256]{1,0:T(8,128)(2,1)S(1)}, u32[]{:S(2)}, u32[]{:S(2)}) collective-permute-start(bf16[528,256]{1,0:T(8,128)(2,1)S(1)} %constant_dynamic-update-slice_fusion.own), channel_id=1, source_target_pairs={{0,8},{8,16},{16,24},{24,32},{32,40},{40,48},{48,56},{56,0},{1,9},... | collective-permute-start | bytes 811016 | tf_op jit(solution)/shard_map/ppermute | solution.py:372
  23.9 8.3 %collective-permute-start.7 = (bf16[528,256]{1,0:T(8,128)(2,1)S(1)}, bf16[528,256]{1,0:T(8,128)(2,1)S(1)}, u32[]{:S(2)}, u32[]{:S(2)}) collective-permute-start(bf16[528,256]{1,0:T(8,128)(2,1)S(1)} %collective-permute-done.6.refs_2_.refs_0_), channel_id=1, source_target_pairs={{0,8},{8,16},{16,24},{24,32},{32,40},{40,48},{48,56},{56,0},{1,9},... | collective-permute-start | bytes 811016 | tf_op jit(solution)/shard_map/ppermute | solution.py:372
  25.1 10.3 %collective-permute-start.5 = (bf16[128,1024]{1,0:T(8,128)(2,1)S(1)}, bf16[128,1024]{1,0:T(8,128)(2,1)S(1)}, u32[]{:S(2)}, u32[]{:S(2)}) collective-permute-start(bf16[128,1024]{1,0:T(8,128)(2,1)S(1)} %get-tuple-element.39), channel_id=1, source_target_pairs={{0,192},{64,128},{128,64},{192,0},{1,193},{65,129},{129,65},{193,1... | collective-permute-start | bytes 786440 | tf_op jit(solution)/shard_map/ppermute | solution.py:367
  27.1 8.3 %collective-permute-start.1 = (bf16[128,1024]{1,0:T(8,128)(2,1)S(1)}, bf16[128,1024]{1,0:T(8,128)(2,1)S(1)}, u32[]{:S(2)}, u32[]{:S(2)}) collective-permute-start(bf16[128,1024]{1,0:T(8,128)(2,1)S(1)} %get-tuple-element.37), channel_id=1, source_target_pairs={{0,64},{64,0},{128,192},{192,128},{1,65},{65,1},{129,193},{193,129... | collective-permute-start | bytes 786440 | tf_op jit(solution)/shard_map/ppermute | solution.py:367
  27.1 14.3 %collective-permute-start.3 = (bf16[128,1024]{1,0:T(8,128)(2,1)S(1)}, bf16[128,1024]{1,0:T(8,128)(2,1)S(1)}, u32[]{:S(2)}, u32[]{:S(2)}) collective-permute-start(bf16[128,1024]{1,0:T(8,128)(2,1)S(1)} %get-tuple-element.38), channel_id=1, source_target_pairs={{0,128},{64,192},{128,0},{192,64},{1,129},{65,193},{129,1},{193,65... | collective-permute-start | bytes 786440 | tf_op jit(solution)/shard_map/ppermute | solution.py:367
  28.9 15.8 %collective-permute-start.8 = (bf16[528,256]{1,0:T(8,128)(2,1)S(1)}, bf16[528,256]{1,0:T(8,128)(2,1)S(1)}, u32[]{:S(2)}, u32[]{:S(2)}) collective-permute-start(bf16[528,256]{1,0:T(8,128)(2,1)S(1)} %constant_dynamic-update-slice_fusion.own), channel_id=1, source_target_pairs={{0,1},{1,2},{2,3},{3,4},{4,5},{5,6},{6,7},{7,8},{8,9},{9,10},{10,1... | collective-permute-start | bytes 811016 | tf_op jit(solution)/shard_map/ppermute | solution.py:372
  32.2 25.9 %collective-permute-start.12 = (bf16[528,256]{1,0:T(8,128)(2,1)S(1)}, bf16[528,256]{1,0:T(8,128)(2,1)S(1)}, u32[]{:S(2)}, u32[]{:S(2)}) collective-permute-start(bf16[528,256]{1,0:T(8,128)(2,1)S(1)} %collective-permute-done.7.refs_0_), channel_id=1, source_target_pairs={{0,8},{8,16},{16,24},{24,32},{32,40},{40,48},{48,56},{56,0},{1,9},... | collective-permute-start | bytes 811016 | tf_op jit(solution)/shard_map/ppermute | solution.py:372
  41.4 15.5 %collective-permute-start.10 = (bf16[128,1024]{1,0:T(8,128)(2,1)S(1)}, bf16[128,1024]{1,0:T(8,128)(2,1)S(1)}, u32[]{:S(2)}, u32[]{:S(2)}) collective-permute-start(bf16[128,1024]{1,0:T(8,128)(2,1)S(1)} %get-tuple-element.42), channel_id=1, source_target_pairs={{0,128},{64,192},{128,0},{192,64},{1,129},{65,193},{129,1},{193,65... | collective-permute-start | bytes 786440 | tf_op jit(solution)/shard_map/ppermute | solution.py:367
  42.6 14.3 %collective-permute-start.9 = (bf16[128,1024]{1,0:T(8,128)(2,1)S(1)}, bf16[128,1024]{1,0:T(8,128)(2,1)S(1)}, u32[]{:S(2)}, u32[]{:S(2)}) collective-permute-start(bf16[128,1024]{1,0:T(8,128)(2,1)S(1)} %get-tuple-element.41), channel_id=1, source_target_pairs={{0,64},{64,0},{128,192},{192,128},{1,65},{65,1},{129,193},{193,129... | collective-permute-start | bytes 786440 | tf_op jit(solution)/shard_map/ppermute | solution.py:367
  43.2 14.9 %collective-permute-start.11 = (bf16[128,1024]{1,0:T(8,128)(2,1)S(1)}, bf16[128,1024]{1,0:T(8,128)(2,1)S(1)}, u32[]{:S(2)}, u32[]{:S(2)}) collective-permute-start(bf16[128,1024]{1,0:T(8,128)(2,1)S(1)} %get-tuple-element.43), channel_id=1, source_target_pairs={{0,192},{64,128},{128,64},{192,0},{1,193},{65,129},{129,65},{193,1... | collective-permute-start | bytes 786440 | tf_op jit(solution)/shard_map/ppermute | solution.py:367
  55.6 1.3 %copy-start.3 = (bf16[8,2,256,256]{3,2,1,0:T(8,128)(2,1)}, bf16[8,2,256,256]{3,2,1,0:T(8,128)(2,1)S(1)}, u32[]{:S(2)}) copy-start(bf16[8,2,256,256]{3,2,1,0:T(8,128)(2,1)S(1)} %get-tuple-element.53.refs_2_) | copy-start | bytes 6291460
  65.2 1.4 %copy-start = (bf16[512,2048]{1,0:T(8,128)(2,1)}, bf16[512,2048]{1,0:T(8,128)(2,1)S(1)}, u32[]{:S(2)}) copy-start(bf16[512,2048]{1,0:T(8,128)(2,1)S(1)} %get-tuple-element.50.ga_ref) | copy-start | bytes 6291460
  66.5 0.7 copy-start.6
  67.2 1.6 %copy-start.2 = (bf16[512,2048]{1,0:T(8,128)(2,1)S(1)}, bf16[512,2048]{1,0:T(8,128)(2,1)}, u32[]{:S(2)}) copy-start(bf16[512,2048]{1,0:T(8,128)(2,1)} %get-tuple-element.55.ga_ref) | copy-start | bytes 6291460
  72.8 1.3 %copy-start.5 = (f32[8,2,128,256]{3,2,1,0:T(8,128)}, f32[8,2,128,256]{3,2,1,0:T(8,128)S(1)}, u32[]{:S(2)}) copy-start(f32[8,2,128,256]{3,2,1,0:T(8,128)S(1)} %get-tuple-element.57.refs_4_) | copy-start | bytes 6291460
  74.1 11.4 %collective-permute-start.19 = (bf16[512,256]{1,0:T(8,128)(2,1)S(1)}, bf16[512,256]{1,0:T(8,128)(2,1)S(1)}, u32[]{:S(2)}, u32[]{:S(2)}) collective-permute-start(bf16[512,256]{1,0:T(8,128)(2,1)S(1)} %get-tuple-element.69), channel_id=1, source_target_pairs={{0,56},{8,0},{16,8},{24,16},{32,24},{40,32},{48,40},{56,48},{1,57}... | collective-permute-start | bytes 786440 | tf_op jit(solution)/shard_map/ppermute | solution.py:372
  76.6 20.5 %copy-start.1 = (bf16[512,2048]{1,0:T(8,128)(2,1)S(1)}, bf16[512,2048]{1,0:T(8,128)(2,1)}, u32[]{:S(2)}) copy-start(bf16[512,2048]{1,0:T(8,128)(2,1)} %copy-done) | copy-start | bytes 6291460
  84.2 1.4 %copy-start.4 = (f32[8,2,128,256]{3,2,1,0:T(8,128)}, f32[8,2,128,256]{3,2,1,0:T(8,128)S(1)}, u32[]{:S(2)}) copy-start(f32[8,2,128,256]{3,2,1,0:T(8,128)S(1)} %get-tuple-element.58.refs_3_) | copy-start | bytes 6291460
  85.6 20.3 %collective-permute-start.20 = (bf16[512,256]{1,0:T(8,128)(2,1)S(1)}, bf16[512,256]{1,0:T(8,128)(2,1)S(1)}, u32[]{:S(2)}, u32[]{:S(2)}) collective-permute-start(bf16[512,256]{1,0:T(8,128)(2,1)S(1)} %add_convert_fusion.2), channel_id=1, source_target_pairs={{0,56},{8,0},{16,8},{24,16},{32,24},{40,32},{48,40},{56,48},{1,57}... | collective-permute-start | bytes 786440 | tf_op jit(solution)/shard_map/ppermute | solution.py:372
  85.7 21.9 %collective-permute-start.13 = (bf16[128,1024]{1,0:T(8,128)(2,1)S(1)}, bf16[128,1024]{1,0:T(8,128)(2,1)S(1)}, u32[]{:S(2)}, u32[]{:S(2)}) collective-permute-start(bf16[128,1024]{1,0:T(8,128)(2,1)S(1)} %get-tuple-element.47), channel_id=1, source_target_pairs={{0,64},{64,0},{128,192},{192,128},{1,65},{65,1},{129,193},{193,129... | collective-permute-start | bytes 786440 | tf_op jit(solution)/shard_map/ppermute | solution.py:367
  87.0 20.7 %collective-permute-start.14 = (bf16[128,1024]{1,0:T(8,128)(2,1)S(1)}, bf16[128,1024]{1,0:T(8,128)(2,1)S(1)}, u32[]{:S(2)}, u32[]{:S(2)}) collective-permute-start(bf16[128,1024]{1,0:T(8,128)(2,1)S(1)} %get-tuple-element.48), channel_id=1, source_target_pairs={{0,128},{64,192},{128,0},{192,64},{1,129},{65,193},{129,1},{193,65... | collective-permute-start | bytes 786440 | tf_op jit(solution)/shard_map/ppermute | solution.py:367
  88.4 19.4 %collective-permute-start.15 = (bf16[128,1024]{1,0:T(8,128)(2,1)S(1)}, bf16[128,1024]{1,0:T(8,128)(2,1)S(1)}, u32[]{:S(2)}, u32[]{:S(2)}) collective-permute-start(bf16[128,1024]{1,0:T(8,128)(2,1)S(1)} %get-tuple-element.49), channel_id=1, source_target_pairs={{0,192},{64,128},{128,64},{192,0},{1,193},{65,129},{129,65},{193,1... | collective-permute-start | bytes 786440 | tf_op jit(solution)/shard_map/ppermute | solution.py:367
  90.1 21.3 %collective-permute-start.22 = (bf16[512,256]{1,0:T(8,128)(2,1)S(1)}, bf16[512,256]{1,0:T(8,128)(2,1)S(1)}, u32[]{:S(2)}, u32[]{:S(2)}) collective-permute-start(bf16[512,256]{1,0:T(8,128)(2,1)S(1)} %get-tuple-element.70), channel_id=1, source_target_pairs={{0,63},{1,0},{2,1},{3,2},{4,3},{5,4},{6,5},{7,6},{8,7},{9,8},{10,9... | collective-permute-start | bytes 786440 | tf_op jit(solution)/shard_map/ppermute | solution.py:372
  106.0 15.0 %copy-start.7 = (bf16[128,1024]{1,0:T(8,128)(2,1)}, bf16[128,1024]{1,0:T(8,128)(2,1)S(1)}, u32[]{:S(2)}) copy-start(bf16[128,1024]{1,0:T(8,128)(2,1)S(1)} %get-tuple-element.59.p0) | copy-start | bytes 786436
  106.1 7.4 %collective-permute-start.21 = (bf16[512,256]{1,0:T(8,128)(2,1)S(1)}, bf16[512,256]{1,0:T(8,128)(2,1)S(1)}, u32[]{:S(2)}, u32[]{:S(2)}) collective-permute-start(bf16[512,256]{1,0:T(8,128)(2,1)S(1)} %add_convert_fusion.1), channel_id=1, source_target_pairs={{0,56},{8,0},{16,8},{24,16},{32,24},{40,32},{48,40},{56,48},{1,57}... | collective-permute-start | bytes 786440 | tf_op jit(solution)/shard_map/ppermute | solution.py:372
  107.7 11.0 %copy-start.9 = (bf16[128,1024]{1,0:T(8,128)(2,1)}, bf16[128,1024]{1,0:T(8,128)(2,1)S(1)}, u32[]{:S(2)}) copy-start(bf16[128,1024]{1,0:T(8,128)(2,1)S(1)} %collective-permute-done.13.p1) | copy-start | bytes 786436
  107.7 11.0 %copy-start.10 = (bf16[128,1024]{1,0:T(8,128)(2,1)}, bf16[128,1024]{1,0:T(8,128)(2,1)S(1)}, u32[]{:S(2)}) copy-start(bf16[128,1024]{1,0:T(8,128)(2,1)S(1)} %collective-permute-done.14.p2) | copy-start | bytes 786436
  107.8 10.9 %copy-start.11 = (bf16[128,1024]{1,0:T(8,128)(2,1)}, bf16[128,1024]{1,0:T(8,128)(2,1)S(1)}, u32[]{:S(2)}) copy-start(bf16[128,1024]{1,0:T(8,128)(2,1)S(1)} %collective-permute-done.15.p3) | copy-start | bytes 786436
  107.8 10.7 %collective-permute-start.18 = (bf16[128,1024]{1,0:T(8,128)(2,1)S(1)}, bf16[128,1024]{1,0:T(8,128)(2,1)S(1)}, u32[]{:S(2)}, u32[]{:S(2)}) collective-permute-start(bf16[128,1024]{1,0:T(8,128)(2,1)S(1)} %get-tuple-element.65), channel_id=1, source_target_pairs={{0,192},{64,128},{128,64},{192,0},{1,193},{65,129},{129,65},{193,1... | collective-permute-start | bytes 786440 | tf_op jit(solution)/shard_map/ppermute | solution.py:367
  110.2 13.6 %collective-permute-start.17 = (bf16[128,1024]{1,0:T(8,128)(2,1)S(1)}, bf16[128,1024]{1,0:T(8,128)(2,1)S(1)}, u32[]{:S(2)}, u32[]{:S(2)}) collective-permute-start(bf16[128,1024]{1,0:T(8,128)(2,1)S(1)} %get-tuple-element.63), channel_id=1, source_target_pairs={{0,128},{64,192},{128,0},{192,64},{1,129},{65,193},{129,1},{193,65... | collective-permute-start | bytes 786440 | tf_op jit(solution)/shard_map/ppermute | solution.py:367
  111.5 12.3 %collective-permute-start.16 = (bf16[128,1024]{1,0:T(8,128)(2,1)S(1)}, bf16[128,1024]{1,0:T(8,128)(2,1)S(1)}, u32[]{:S(2)}, u32[]{:S(2)}) collective-permute-start(bf16[128,1024]{1,0:T(8,128)(2,1)S(1)} %get-tuple-element.61), channel_id=1, source_target_pairs={{0,64},{64,0},{128,192},{192,128},{1,65},{65,1},{129,193},{193,129... | collective-permute-start | bytes 786440 | tf_op jit(solution)/shard_map/ppermute | solution.py:367
  114.3 12.5 %collective-permute-start.25 = (bf16[128,256]{1,0:T(8,128)(2,1)S(1)}, bf16[128,256]{1,0:T(8,128)(2,1)S(1)}, u32[]{:S(2)}, u32[]{:S(2)}) collective-permute-start(bf16[128,256]{1,0:T(8,128)(2,1)S(1)} %get-tuple-element.79), channel_id=1, source_target_pairs={{0,192},{64,128},{128,64},{192,0},{1,193},{65,129},{129,65},{193,1... | collective-permute-start | bytes 196616 | tf_op jit(solution)/shard_map/ppermute | solution.py:367
  117.2 9.5 %collective-permute-start.24 = (bf16[128,256]{1,0:T(8,128)(2,1)S(1)}, bf16[128,256]{1,0:T(8,128)(2,1)S(1)}, u32[]{:S(2)}, u32[]{:S(2)}) collective-permute-start(bf16[128,256]{1,0:T(8,128)(2,1)S(1)} %get-tuple-element.80), channel_id=1, source_target_pairs={{0,128},{64,192},{128,0},{192,64},{1,129},{65,193},{129,1},{193,65... | collective-permute-start | bytes 196616 | tf_op jit(solution)/shard_map/ppermute | solution.py:367
  118.5 5.2 %copy-start.12 = (bf16[128,1024]{1,0:T(8,128)(2,1)}, bf16[128,1024]{1,0:T(8,128)(2,1)S(1)}, u32[]{:S(2)}) copy-start(bf16[128,1024]{1,0:T(8,128)(2,1)S(1)} %collective-permute-done.18.p3) | copy-start | bytes 786436
  118.5 8.3 %collective-permute-start.23 = (bf16[128,256]{1,0:T(8,128)(2,1)S(1)}, bf16[128,256]{1,0:T(8,128)(2,1)S(1)}, u32[]{:S(2)}, u32[]{:S(2)}) collective-permute-start(bf16[128,256]{1,0:T(8,128)(2,1)S(1)} %get-tuple-element.81), channel_id=1, source_target_pairs={{0,64},{64,0},{128,192},{192,128},{1,65},{65,1},{129,193},{193,129... | collective-permute-start | bytes 196616 | tf_op jit(solution)/shard_map/ppermute | solution.py:367
  123.7 0.7 copy-start.13
  123.7 0.8 copy-start.14
  126.7 0.6 copy-start.15
  126.7 0.7 copy-start.16
  126.8 0.6 copy-start.17
where the time goes:
time: 130 us; the launch traced here: 129 us
  Pallas kernels  44.5 us (34%)
  starting transfers between devices  39.2 us (30%)
  waiting for transfers between devices  29.7 us (23%)
  local copies, waits for them, and re-layouts  12.1 us (9%)
  between operations  3.47 us (3%)
    pallas_call x5, Pallas kernels, call(): pl.pallas_call(kernel, grid_spec=pltpu.PrefetchScalarGridSpec(num_scalar_...  38.3 us
    ppermute x18, starting transfers between devices, swap(): return lax.ppermute(x, 'head', [(i, i ^ k) for i in range(4)])  26.2 us
    ppermute x8, waiting for transfers between devices, along(): return lax.ppermute(x, axis, [(i, (i + distance) % n) for i in range(n)])  15.5 us
    ppermute x18, waiting for transfers between devices, swap(): return lax.ppermute(x, 'head', [(i, i ^ k) for i in range(4)])  14.1 us
    ppermute x8, starting transfers between devices, along(): return lax.ppermute(x, axis, [(i, (i + distance) % n) for i in range(n)])  13 us
    unnamed x40, local copies, waits for them, and re-layouts  10.1 us
    pallas_call x3, Pallas kernels, placed(): pl.pallas_call(place_kernel, in_specs=[pl.BlockSpec(memory_space=pltpu.SM...  6.21 us
  transfers between devices with their start and end apart: 26, of which 9 were waited for; matrix products, arithmetic and copies ran while one was open for 2% of the time, Pallas kernels for 25%

commit v1 on v0

--- a/solution.py
+++ b/solution.py
@@ -16,7 +16,7 @@
 BLOCKS = 128
 SCALE = 1.0 / math.sqrt(D)
 EXP2_SCALE = SCALE * math.log2(math.e)
-VMEM_LIMIT = 48 * 2**20
+VMEM_LIMIT = 26 * 2**20
 f32, bf16 = jnp.float32, jnp.bfloat16
 NT = (((1,), (1,)), ((), ()))
 NN = (((1,), (0,)), ((), ()))
@@ -149,30 +149,41 @@
             top_ref[a, half] = jnp.broadcast_to(tops[a][half], (8, HALF))
 
 
-def fwd_last_kernel(heads, h_ref, q_ref, g0, g1, g2, g3, own, win, state_in, top_in,
-                    o0, o1, o2, o3, g_out, gb_out, w_ref, vt_ref, s_ref, g_ref, o_ref):
+def fwd_last_kernel(heads, n_win, h_ref, q_ref, own, *refs):
+    windows, (state_in, top_in), refs = refs[:n_win], refs[n_win : n_win + 2], refs[n_win + 2 :]
+    o0, o1, o2, factor_ref = refs[:4]
+    w_refs = refs[4 : 4 + n_win]
+    vt_ref, s_ref, o_ref = refs[4 + n_win :]
     h = h_ref[0]
-    layout = Layout(h, own, [win], False)
+    layout = Layout(h, own, windows, False)
     load_vt(layout, vt_ref)
-    for k, piece in enumerate((g0, g1, g2, g3)):
-        g_ref[k * PIECE : (k + 1) * PIECE, :] = piece[...]
     old = [[top_in[a, half, :1, :] for half in range(2)] for a in range(heads)]
-    tops, acc = weigh_blocks(layout, heads, q_ref, None, vt_ref, s_ref, [w_ref], old)
+    tops, acc = weigh_blocks(layout, heads, q_ref, None, vt_ref, s_ref, w_refs, old)
     for a in range(heads):
         for half, row in enumerate((layout.q_early, layout.q_late)):
             shrink = jnp.exp2((old[a][half] - tops[a][half]) * EXP2_SCALE)
             t = state_in[a, half] * shrink + acc[a][half]
             r = 1.0 / t[D : D + 1]
-            out = jnp.transpose(t[:D] * r, (1, 0)).astype(bf16)
-            o_ref[pl.ds(row, HALF), a * D : (a + 1) * D] = out
+            o_ref[pl.ds(row, HALF), a * D : (a + 1) * D] = jnp.transpose(t[:D] * r, (1, 0)).astype(bf16)
+            factor_ref[a, half, 0:8] = jnp.broadcast_to(r * shrink, (8, HALF))
+            factor_ref[a, half, 8:16] = jnp.broadcast_to(r, (8, HALF))
+    for row, ref in ((0, o0), (PIECE, o1), (HALF, o2)):
+        ref[...] = o_ref[row : row + ref.shape[0], :]
+
+
+def scaled_kernel_part(heads, layout, g_pieces, o_pieces, factor_ref, g_ref, o_ref, ga_refs):
+    for row, g, o in zip((0, PIECE, HALF), g_pieces, o_pieces):
+        g_ref[row : row + g.shape[0], :] = g[...]
+        o_ref[row : row + o.shape[0], :] = o[...]
+    for a in range(heads):
+        for half, row in enumerate((layout.q_early, layout.q_late)):
             g = cols(g_ref, row, HALF, a).astype(f32)
-            for ref, factor in ((g_out, r * shrink), (gb_out, r)):
-                scaled = g * jnp.transpose(jnp.broadcast_to(factor, (D, HALF)), (1, 0))
+            out = cols(o_ref, row, HALF, a).astype(f32)
+            for i, ref in enumerate(ga_refs):
+                factor = jnp.broadcast_to(factor_ref[a, half, 8 * i : 8 * i + 1], (D, HALF))
+                scaled = g * jnp.transpose(factor, (1, 0))
                 ref[pl.ds(row, HALF), 2 * a * D : (2 * a + 1) * D] = scaled.astype(bf16)
-                ref[pl.ds(row, HALF), (2 * a + 1) * D : (2 * a + 2) * D] = (
-                    -scaled * out.astype(f32)).astype(bf16)
-    for k, ref in enumerate((o0, o1, o2, o3)):
-        ref[...] = o_ref[k * PIECE : (k + 1) * PIECE, :]
+                ref[pl.ds(row, HALF), (2 * a + 1) * D : (2 * a + 2) * D] = (-scaled * out).astype(bf16)
 
 
 PAY_SPEC = pl.BlockSpec((ROWS + HEADER, 2 * D), lambda j, h: (0, 0))
@@ -182,6 +193,10 @@
     return pl.BlockSpec((PIECE, heads * D), lambda j, h: (0, j))
 
 
+def pieces_spec(heads):
+    return [piece_spec(heads)] * 2 + [pl.BlockSpec((HALF, heads * D), lambda j, h: (0, j))]
+
+
 def rows_spec(heads):
     return pl.BlockSpec((ROWS, heads * D), lambda j, h: (0, j))
 
@@ -194,15 +209,23 @@
     return pl.BlockSpec((heads, 2, n, HALF), lambda j, h: (j, 0, 0, 0))
 
 
-def call(kernel, name, steps, ins, in_specs, outs, out_specs, scratch, flops, exps=0):
+def call(kernel, name, steps, ins, in_specs, outs, out_specs, scratch, flops, exps=0, token=None):
+    tokens = () if token is None else (token,)
+    n = len(tokens)
+
+    def body(h_ref, *refs):
+        kernel(h_ref, *refs[n:])
+
+    ins = (ins[0], *tokens, *ins[1:])
+    in_specs = [pl.BlockSpec(memory_space=pl.ANY)] * n + in_specs
     return pl.pallas_call(
-        kernel,
+        body,
         grid_spec=pltpu.PrefetchScalarGridSpec(
             num_scalar_prefetch=1, grid=(steps,), in_specs=in_specs, out_specs=out_specs,
             scratch_shapes=scratch),
         out_shape=outs,
         compiler_params=pltpu.CompilerParams(vmem_limit_bytes=VMEM_LIMIT),
-        cost_estimate=pl.CostEstimate(flops=flops, bytes_accessed=8 * 2**20, transcendentals=exps),
+        cost_estimate=pl.CostEstimate(flops=flops, bytes_accessed=2**16, transcendentals=0),
         name=name,
     )(*ins)
 
@@ -211,10 +234,10 @@
     return jax.ShapeDtypeStruct(dims, dtype)
 
 
-STEP_FIRST, STEP_LAST, STEP_A, STEP_B, STEP_C = 2, 4, 8, 2, 2
-
-
-def forward_first(h, q, own, windows):
+STEP_FIRST, STEP_LAST, STEP_A, STEP_C = 2, 4, 2, 2
+
+
+def forward_first(h, q, own, windows, token=None):
     heads = q[0].shape[1] // D
     n = 3 + 2 * len(windows)
     e = STEP_FIRST
@@ -227,38 +250,49 @@
         [rows_spec(e), half_spec(e, D + SUMS), half_spec(e, 8), w_spec(e, 3)]
         + [w_spec(e, 2)] * len(windows),
         [pltpu.VMEM((n, D + SUMS, HALF), bf16), pltpu.VMEM((e, n, HALF, HALF), f32)],
-        heads * n * 4 * HALF * HALF * D, heads * n * HALF * HALF)
-
-
-def forward_last(h, q_rows, g, own, window, state, top):
+        int(heads * n * 1 * HALF * HALF * D), heads * n * HALF * HALF, token)
+
+
+def forward_last(h, q_rows, own, windows, state, top):
     heads = q_rows.shape[1] // D
     e = STEP_LAST
+    n_win = len(windows)
+    n = 2 * n_win
     return call(
-        functools.partial(fwd_last_kernel, e), "forward_last", heads // e,
-        (h, q_rows, *g, own, window, state, top),
-        [rows_spec(e)] + [piece_spec(e)] * 4 + [PAY_SPEC] * 2 + [half_spec(e, D + SUMS), half_spec(e, 8)],
-        [shape(PIECE, heads * D)] * 4 + [shape(ROWS, heads * 2 * D)] * 2 + [shape(heads, 2, HALF, HALF)],
-        [piece_spec(e)] * 4 + [rows_spec(2 * e)] * 2 + [w_spec(e, 2)],
-        [pltpu.VMEM((2, D + SUMS, HALF), bf16), pltpu.VMEM((e, 2, HALF, HALF), f32),
-         pltpu.VMEM((ROWS, e * D), bf16), pltpu.VMEM((ROWS, e * D), bf16)],
-        heads * 2 * 4 * HALF * HALF * D, heads * 2 * HALF * HALF)
-
-
-def bwd_kernel(heads, n_win, with_own, first, last, h_ref, q_ref, ga_ref, own, *refs):
+        functools.partial(fwd_last_kernel, e, n_win), "forward_last", heads // e,
+        (h, q_rows, own, *windows, state, top),
+        [rows_spec(e)] + [PAY_SPEC] * (1 + n_win) + [half_spec(e, D + SUMS), half_spec(e, 8)],
+        [shape(PIECE, heads * D)] * 2 + [shape(HALF, heads * D), shape(heads, 2, 16, HALF, dtype=f32)]
+        + [shape(heads, 2, HALF, HALF)] * n_win,
+        pieces_spec(e) + [half_spec(e, 16)] + [w_spec(e, 2)] * n_win,
+        [pltpu.VMEM((n, D + SUMS, HALF), bf16), pltpu.VMEM((e, n, HALF, HALF), f32),
+         pltpu.VMEM((ROWS, e * D), bf16)],
+        int(heads * n * 1 * HALF * HALF * D), heads * n * HALF * HALF)
+
+
+def bwd_kernel(heads, n_win, with_own, first, last, which, h_ref, q_ref, own, *refs):
+    if first:
+        g_pieces, o_pieces, factor_ref, refs = refs[:3], refs[3:6], refs[6], refs[7:]
+    else:
+        ga_refs, refs = refs[:1], refs[1:]
     windows, refs = refs[:n_win], refs[n_win:]
     n_terms = n_win + with_own
     w_refs, refs = refs[:n_terms], refs[n_terms:]
     if not first:
         d_in, refs = refs[0], refs[1:]
     if last:
-        d_outs, refs = refs[:4], refs[4:]
+        d_outs, refs = refs[:3], refs[3:]
     else:
-        d_out, refs = refs[0], refs[1:]
+        d_out, ga_out, refs = refs[0], refs[1], refs[2:]
     terms, refs = refs[:n_terms], refs[n_terms:]
     kt_ref, va_ref, acc_ref, ds_ref = refs[:4]
     h = h_ref[0]
     layout = Layout(h, own, windows, with_own)
     j = pl.program_id(0)
+    if first:
+        g_ref, o_ref, gb_ref = refs[4:]
+        ga_refs = (ga_out, gb_ref)
+        scaled_kernel_part(heads, layout, g_pieces, o_pieces, factor_ref, g_ref, o_ref, ga_refs)
 
     @pl.when(j == 0)
     def _():
@@ -270,17 +304,18 @@
 
     total = [[None, None] if first else [d_in[a, 0], d_in[a, 1]] for a in range(heads)]
 
-    def grads(row, a, width):
+    def grads(n, row, a, width):
+        ga_ref = ga_refs[which[layout.spots[n][0]]]
         return ga_ref[pl.ds(row, HALF), 2 * a * D : (2 * a + width) * D]
 
     for n, (keys, key_row, query_row, early, masked) in enumerate(layout.blocks):
         for a in range(heads):
-            dp = dot(va_ref[n], grads(query_row, a, 2), NT)
+            dp = dot(va_ref[n], grads(n, query_row, a, 2), NT)
             ds_ref[a, n] = (at(w_refs, layout, a, n)[...].astype(f32) * dp).astype(bf16)
     for n, (keys, key_row, query_row, early, masked) in enumerate(layout.blocks):
         value_sum = key_sum = None
         for a in range(heads):
-            value_sum = add(value_sum, dot(at(w_refs, layout, a, n)[...], grads(query_row, a, 1), NN))
+            value_sum = add(value_sum, dot(at(w_refs, layout, a, n)[...], grads(n, query_row, a, 1), NN))
             key_sum = add(key_sum, dot(ds_ref[a, n], cols(q_ref, query_row, HALF, a), NN))
             for half, x in enumerate(split(early, dot(kt_ref[n], ds_ref[a, n], NN))):
                 total[a][half] = add(total[a][half], x)
@@ -291,8 +326,8 @@
         for a in range(heads):
             for row, d in ((layout.q_early, total[a][0]), (layout.q_late, total[a][1])):
                 d_ref[pl.ds(row, HALF), a * D : (a + 1) * D] = jnp.transpose(d * SCALE, (1, 0)).astype(bf16)
-        for k, ref in enumerate(d_outs):
-            ref[...] = d_ref[k * PIECE : (k + 1) * PIECE, :]
+        for row, ref in zip((0, PIECE, HALF), d_outs):
+            ref[...] = d_ref[row : row + ref.shape[0], :]
     else:
         for a in range(heads):
             for half in range(2):
@@ -319,57 +354,96 @@
                 term[pl.ds(row, HALF), D:] = x[:, D:].astype(bf16)
 
 
-def backward(name, e, h, q_rows, ga, own, windows, w, d=None, with_own=False, last=False):
+def backward(name, e, h, q_rows, cotangents, which, own, windows, w, d=None, with_own=False):
     heads = q_rows.shape[1] // D
     n = 3 * with_own + 2 * len(windows)
     n_terms = with_own + len(windows)
     first = d is None
+    if first:
+        specs = pieces_spec(e) * 2 + [half_spec(e, 16)]
+        outs = [shape(heads, 2, D, HALF, dtype=f32), shape(ROWS, heads * 2 * D)]
+        out_specs = [half_spec(e, D), rows_spec(2 * e)]
+        scratch = [pltpu.VMEM((ROWS, e * D), bf16)] * 2 + [pltpu.VMEM((ROWS, 2 * e * D), bf16)]
+    else:
+        specs = [rows_spec(2 * e)]
+        outs = [shape(PIECE, heads * D)] * 2 + [shape(HALF, heads * D)]
+        out_specs = pieces_spec(e)
+        scratch = [pltpu.VMEM((ROWS, e * D), bf16)]
     return call(
-        functools.partial(bwd_kernel, e, len(windows), with_own, first, last), name, heads // e,
-        (h, q_rows, ga, own, *windows, *w) + (() if first else (d,)),
-        [rows_spec(e), rows_spec(2 * e)] + [PAY_SPEC] * (1 + len(windows))
+        functools.partial(bwd_kernel, e, len(windows), with_own, first, not first, which),
+        name, heads // e,
+        (h, q_rows, own, *cotangents, *windows, *w) + (() if first else (d,)),
+        [rows_spec(e), PAY_SPEC] + specs + [PAY_SPEC] * len(windows)
         + [w_spec(e, 3)] * with_own + [w_spec(e, 2)] * len(windows)
         + ([] if first else [half_spec(e, D)]),
-        ([shape(PIECE, heads * D)] * 4 if last else [shape(heads, 2, D, HALF, dtype=f32)])
-        + [shape(ROWS, 2 * D)] * n_terms,
-        ([piece_spec(e)] * 4 if last else [half_spec(e, D)])
-        + [pl.BlockSpec((ROWS, 2 * D), lambda j, h: (0, 0))] * n_terms,
+        outs + [shape(ROWS, 2 * D)] * n_terms,
+        out_specs + [pl.BlockSpec((ROWS, 2 * D), lambda j, h: (0, 0))] * n_terms,
         [pltpu.VMEM((n, D, HALF), bf16), pltpu.VMEM((n, HALF, 2 * D), bf16),
-         pltpu.VMEM((n, HALF, 2 * D), f32), pltpu.VMEM((e, n, HALF, HALF), bf16)]
-        + ([pltpu.VMEM((ROWS, e * D), bf16)] if last else []),
-        heads * n * 8 * HALF * HALF * D)
-
-
-def place_kernel(h_ref, p0, p1, p2, p3, out):
-    width = p0.shape[1]
-    for k, piece in enumerate((p0, p1, p2, p3)):
-        column = pl.multiple_of((h_ref[0] ^ k) * width, width)
-        out[:, pl.ds(column, width)] = piece[...].astype(out.dtype)
-
-
-def placed(h, pieces, dtype=bf16):
-    rows, width = pieces[0].shape
+         pltpu.VMEM((n, HALF, 2 * D), f32), pltpu.VMEM((e, n, HALF, HALF), bf16)] + scratch,
+        int(heads * n * 2 * HALF * HALF * D))
+
+
+def place_kernel(n, h_ref, *refs):
+    pieces, outs, held, sems = refs[: 4 * n], refs[4 * n : 5 * n], refs[5 * n : -1], refs[-1]
+    copies = []
+    for i, out in enumerate(outs):
+        width = pieces[4 * i].shape[1]
+        for k in range(4):
+            piece = pieces[4 * i + k]
+            if out.dtype != bf16:
+                held[0][k] = piece[...].astype(out.dtype)
+                piece = held[0].at[k]
+            column = pl.multiple_of((h_ref[0] ^ k) * width, width)
+            copy = pltpu.make_async_copy(piece, out.at[:, pl.ds(column, width)], sems.at[4 * i + k])
+            copy.start()
+            copies.append(copy)
+    for copy in copies:
+        copy.wait()
+
+
+def placed(h, *arrays):
+    ins, outs, held = [], [], []
+    for pieces, dtype in arrays:
+        rows, width = pieces[0].shape
+        ins += pieces
+        outs.append(shape(rows, 4 * width, dtype=dtype))
+        if dtype != bf16:
+            held = [pltpu.VMEM((4, rows, width), dtype)]
     return pl.pallas_call(
-        place_kernel,
-        in_specs=[pl.BlockSpec(memory_space=pltpu.SMEM)] + [pl.BlockSpec(memory_space=pltpu.VMEM)] * 4,
-        out_specs=pl.BlockSpec(memory_space=pltpu.VMEM),
-        out_shape=shape(rows, 4 * width, dtype=dtype),
-        cost_estimate=pl.CostEstimate(flops=0, bytes_accessed=16 * rows * width, transcendentals=0),
+        functools.partial(place_kernel, len(arrays)),
+        in_specs=[pl.BlockSpec(memory_space=pltpu.SMEM)]
+        + [pl.BlockSpec(memory_space=pltpu.VMEM)] * len(ins),
+        out_specs=[pl.BlockSpec(memory_space=pl.ANY)] * len(outs),
+        out_shape=outs,
+        scratch_shapes=held + [pltpu.SemaphoreType.DMA((len(ins),))],
+        cost_estimate=pl.CostEstimate(flops=0, bytes_accessed=2**21, transcendentals=0),
         name="placed",
-    )(h, *pieces)
-
-
-def after(x, earlier):
-    return lax.optimization_barrier((x, earlier))[0]
-
-
-def swap(x, k):
-    return lax.ppermute(x, "head", [(i, i ^ k) for i in range(4)])
-
-
-def along(x, axis, distance):
+    )(h, *ins)
+
+
+def small(*arrays):
+    return sum(a[:16, :D] for a in arrays)
+
+
+def token(x, stages, name):
+    for _ in range(stages):
+        x = swap(x + 1, 1, name)
+    return x
+
+
+def together(*arrays):
+    return lax.optimization_barrier(arrays)
+
+
+def swap(x, k, name):
+    with jax.named_scope(f"{name}_{k}"):
+        return lax.ppermute(x, "head", [(i, i ^ k) for i in range(4)])
+
+
+def along(x, axis, distance, name):
     n = lax.axis_size(axis)
-    return lax.ppermute(x, axis, [(i, (i + distance) % n) for i in range(n)])
+    with jax.named_scope(name):
+        return lax.ppermute(x, axis, [(i, (i + distance) % n) for i in range(n)])
 
 
 def columns(h, x, k):
@@ -377,15 +451,26 @@
     return lax.dynamic_slice(x, (0, (h ^ k) * width), (x.shape[0], width))
 
 
-def to_heads(h, x, earlier=None):
-    pieces = [columns(h, x, k) for k in range(4)]
-    if earlier is not None:
-        pieces = pieces[:1] + [after(pieces[k], earlier[k]) for k in (1, 2, 3)]
-    return from_heads(pieces)
-
-
-def from_heads(pieces):
-    return [pieces[0]] + [swap(pieces[k], k) for k in (1, 2, 3)]
+def to_heads(h, x, name):
+    return from_heads([columns(h, x, k) for k in range(4)], name)
+
+
+def to_heads_by_two(h, x, name, earlier=()):
+    near = swap(jnp.concatenate([columns(h, x, 1), columns(h, x, 3)], axis=0), 1, name)
+    far = jnp.concatenate([columns(h, x, 2), near[PIECE:]], axis=0)
+    if earlier:
+        far, *earlier = together(far, *earlier)
+    return [columns(h, x, 0), near, swap(far, 2, name)], earlier
+
+
+def from_heads_by_two(pieces, name):
+    own, partner, others = pieces
+    far = swap(others, 2, name)
+    return [own, swap(partner, 1, name), far[:PIECE], swap(far[PIECE:], 1, name)]
+
+
+def from_heads(pieces, name):
+    return [pieces[0]] + [swap(pieces[k], k, name) for k in (1, 2, 3)]
 
 
 def plus(x, y):
@@ -398,29 +483,36 @@
     block = positions[0] // HALF
     b = jnp.where(h < 2, block, BLOCKS - 1 - block)
     header = jnp.broadcast_to(b.astype(bf16), (HEADER, 2 * D))
-    kv = to_heads(h, key_value)
+    kv = to_heads(h, key_value, "kv")
     own = jnp.concatenate(kv + [header], axis=0)
-    q = to_heads(h, query, kv)
-    g = to_heads(h, grad_out, q)
-    before = along(own, ("inner", "outer"), 1)
-    w1 = along(own, "inner", 1)
-    w2 = along(w1, "inner", 1)
-    w3 = along(w2, "inner", 1)
-    q_rows, state, top, wo, ww2, wwb, ww1 = forward_first(h_arg, q, own, [w2, before, w1])
-    *out, ga, gb, ww3 = forward_last(h_arg, q_rows, g, own, w3, state, top)
-    out = from_heads(out)
-    d, t3 = backward("backward_a", STEP_A, h_arg, q_rows, gb, own, [w3], [ww3])
-    s2 = along(t3, "inner", -1)
-    d, t2, tb = backward("backward_b", STEP_B, h_arg, q_rows, ga, own, [w2, before], [ww2, wwb], d)
-    s1 = along(plus(t2, s2), "inner", -1)
-    back = along(tb, ("inner", "outer"), -1)
+    w1 = along(own, "inner", 1, "w_1")
+    before = along(own, ("inner", "outer"), 1, "before")
+    w2 = along(w1, "inner", 1, "w_2")
+    q = to_heads(h, query, "query")
+    g, (q[2], q[3]) = to_heads_by_two(h, grad_out, "grad_out", (q[2], q[3]))
+    q_token = token(small(before), 2, "before_token")
+    w3 = along(w2, "inner", 1, "w_3")
+    q_rows, state, top, wo, wwb, ww1 = forward_first(h_arg, q, own, [before, w1], q_token)
+    *out, factors, ww2, ww3 = forward_last(h_arg, q_rows, own, [w2, w3], state, top)
+    d, ga, t3, t2, tb = backward(
+        "backward_first", STEP_A, h_arg, q_rows, (*g, *out, factors), (1, 1, 0), own,
+        [w3, w2, before], [ww3, ww2, wwb])
+    out = from_heads_by_two(out, "out")
+    s2 = along(t3, "inner", -1, "term_3")
+    back = along(tb, ("inner", "outer"), -1, "term_before")
     *dq, t0, t1 = backward(
-        "backward_c", STEP_C, h_arg, q_rows, ga, own, [w1], [wo, ww1], d, with_own=True, last=True)
-    s0 = along(plus(t1, s1), "inner", -1)
-    dq = from_heads(dq[:1] + [after(dq[k], out[k]) for k in (1, 2, 3)])
+        "backward_last", STEP_C, h_arg, q_rows, (ga,), (0, 0), own, [w1], [wo, ww1], d, with_own=True)
+    s2, t1 = together(s2, t1)
+    s1 = along(plus(t2, s2), "inner", -1, "term_2")
+    s0 = along(plus(t1, s1), "inner", -1, "term_1")
+    (attn_out,) = placed(h_arg, (out, bf16))
     dkv = (t0.astype(f32) + s0.astype(f32) + back.astype(f32)).astype(bf16)
-    dkv = from_heads([dkv[k * PIECE : (k + 1) * PIECE] for k in range(4)])
-    return placed(h_arg, out), placed(h_arg, dq), placed(h_arg, dkv, f32)
+    far = swap(dq[2], 2, "grad_query")
+    far, attn_out = together(far, attn_out)
+    dq = [dq[0], swap(dq[1], 1, "grad_query"), far[:PIECE], swap(far[PIECE:], 1, "grad_query")]
+    dkv = from_heads([dkv[k * PIECE : (k + 1) * PIECE] for k in range(4)], "grad_kv")
+    grad_query, grad_kv = placed(h_arg, (dq, bf16), (dkv, f32))
+    return attn_out, grad_query, grad_kv
 
 
 def solution(mesh):

time: 130 us -> 107 us (0.82)
  waiting for transfers between devices: 29.7 us -> 19 us
  Pallas kernels: 44.5 us -> 34.1 us
  starting transfers between devices: 39.2 us -> 46.2 us
  local copies, waits for them, and re-layouts: 12.1 us -> 6.04 us
  between operations: 3.47 us -> 1.23 us
    ppermute x8, waiting for transfers between devices: 15.5 us -> 4.54 us  [along(): return lax.ppermute(x, axis, [(i, (i + distance) % n) for i in range(n)])]
    pallas_call x8 -> x6, Pallas kernels: 44.5 us -> 34.1 us  [the longest x4 29.5 us: call(): pl.pallas_call(body, grid_spec=pltpu.PrefetchScalarGridSpec(num_scalar_pr...]
    unnamed x40 -> x25, local copies, waits for them, and re-layouts: 10.1 us -> 1.49 us
    ppermute x18 -> x19, starting transfers between devices: 26.2 us -> 30.6 us  [swap(): return lax.ppermute(x, 'head', [(i, i ^ k) for i in range(4)])]
    ppermute x8, starting transfers between devices: 13 us -> 15.6 us  [along(): return lax.ppermute(x, axis, [(i, (i + distance) % n) for i in range(n)])]
    slice x1 -> x4, local copies, waits for them, and re-layouts: 0.65 us -> 2.16 us  [the longest x1 0.76 us: local(): far[PIECE:]]
    ppermute x18 -> x19, waiting for transfers between devices: 14.1 us -> 14.5 us  [swap(): return lax.ppermute(x, 'head', [(i, i ^ k) for i in range(4)])]
  transfers between devices with their start and end apart: 26 -> 27, of which waited for: 9 -> 10; matrix products, arithmetic and copies ran while one was open for 2% -> 4% of each run, Pallas kernels for 25% -> 30%
where the time goes in v1:
time: 107 us
  starting transfers between devices  46.2 us (43%)
  Pallas kernels  34.1 us (32%)
  waiting for transfers between devices  19 us (18%)
  local copies, waits for them, and re-layouts  6.04 us (6%)
  between operations  1.23 us (1%)
    ppermute x19, starting transfers between devices, swap(): return lax.ppermute(x, 'head', [(i, i ^ k) for i in range(4)])  30.6 us
    pallas_call x4, Pallas kernels, call(): pl.pallas_call(body, grid_spec=pltpu.PrefetchScalarGridSpec(num_scalar_pr...  29.5 us
    ppermute x8, starting transfers between devices, along(): return lax.ppermute(x, axis, [(i, (i + distance) % n) for i in range(n)])  15.6 us
    ppermute x19, waiting for transfers between devices, swap(): return lax.ppermute(x, 'head', [(i, i ^ k) for i in range(4)])  14.5 us
    pallas_call x2, Pallas kernels, placed(): pl.pallas_call(functools.partial(place_kernel, len(arrays)), in_specs=[pl...  4.59 us
    ppermute x8, waiting for transfers between devices, along(): return lax.ppermute(x, axis, [(i, (i + distance) % n) for i in range(n)])  4.54 us
    dynamic_slice x3, local copies, waits for them, and re-layouts, columns(): return lax.dynamic_slice(x, (0, (h ^ k) * width), (x.shape[0], width))  2.39 us
  transfers between devices with their start and end apart: 27, of which 10 were waited for; matrix products, arithmetic and copies ran while one was open for 4% of the time, Pallas kernels for 30%

profile of v1, /device:TPU:1, one launch (start us, length us, event | category | flops | bytes accessed | tf_op | source)
XLA Modules:
  0.0 106.9 jit_solution(2741161918595287154)
XLA Ops:
  0.7 1.0 constant_dynamic-slice_fusion.8
  1.7 4.2 %collective-permute-start.2 = (bf16[128,256]{1,0:T(8,128)(2,1)S(1)}, bf16[128,256]{1,0:T(8,128)(2,1)S(1)}, u32[]{:S(2)}, u32[]{:S(2)}) collective-permute-start(bf16[128,256]{1,0:T(8,128)(2,1)S(1)} %get-tuple-element.81), channel_id=1, source_target_pairs={{0,192},{64,128},{128,64},{192,0},{1,193},{65,129},{129,65},{193,1... | collective-permute-start | bytes 196616 | tf_op jit(solution)/shard_map/kv_3/ppermute | solution.py:440
  5.9 0.0 collective-permute-start
  5.9 2.0 %collective-permute-start.1 = (bf16[128,256]{1,0:T(8,128)(2,1)S(1)}, bf16[128,256]{1,0:T(8,128)(2,1)S(1)}, u32[]{:S(2)}, u32[]{:S(2)}) collective-permute-start(bf16[128,256]{1,0:T(8,128)(2,1)S(1)} %get-tuple-element.84), channel_id=1, source_target_pairs={{0,128},{64,192},{128,0},{192,64},{1,129},{65,193},{129,1},{193,65... | collective-permute-start | bytes 196616 | tf_op jit(solution)/shard_map/kv_2/ppermute | solution.py:440
  7.9 1.3 %constant_dynamic-slice_fusion = (bf16[128,1024]{1,0:T(8,128)(2,1)S(1)}, bf16[128,1024]{1,0:T(8,128)(2,1)S(1)}, bf16[128,1024]{1,0:T(8,128)(2,1)S(1)}, bf16[128,1024]{1,0:T(8,128)(2,1)S(1)}) fusion(bf16[128,4096]{1,0:T(8,128)(2,1)} %param.6, s32[]{:T(128)S(6)} %select_n.42, s32[]{:T(128)S(6)} %select_n.43, s32[]{:T(128)S(6)} %select_n.44, s32[]{:T(128)S(6)} %select_n.45), kind=kLoop, calls=%fused_computation.11 | loop fusion | bytes 2097168 | tf_op jit(solution)/shard_map/dynamic_slice | solution.py:451
  9.2 0.9 collective-permute-start.7
  10.3 0.0 collective-permute-done
  10.3 0.3 collective-permute-done.1
  10.6 0.0 collective-permute-done.2
  10.6 1.7 %collective-permute-start.10 = (bf16[528,256]{1,0:T(8,128)(2,1)S(1)}, bf16[528,256]{1,0:T(8,128)(2,1)S(1)}, u32[]{:S(2)}, u32[]{:S(2)}) collective-permute-start(bf16[528,256]{1,0:T(8,128)(2,1)S(1)} %constant_dynamic-update-slice_fusion.refs_5_.refs_1_), channel_id=1, source_target_pairs={{0,8},{8,16},{16,24},{24,32},{32,40},{40,48},{48,56},{56,0},{1,9},... | collective-permute-start | bytes 811016 | tf_op jit(solution)/shard_map/w_1/ppermute | solution.py:446
  12.3 0.3 collective-permute-start.3
  12.6 0.1 constant_dynamic-slice_fusion.1
  12.7 3.9 %collective-permute-start.9 = (bf16[128,1024]{1,0:T(8,128)(2,1)S(1)}, bf16[128,1024]{1,0:T(8,128)(2,1)S(1)}, u32[]{:S(2)}, u32[]{:S(2)}) collective-permute-start(bf16[128,1024]{1,0:T(8,128)(2,1)S(1)} %get-tuple-element.69), channel_id=1, source_target_pairs={{0,192},{64,128},{128,64},{192,0},{1,193},{65,129},{129,65},{193,1... | collective-permute-start | bytes 786440 | tf_op jit(solution)/shard_map/query_3/ppermute | solution.py:440
  16.7 1.2 %collective-permute-start.8 = (bf16[128,1024]{1,0:T(8,128)(2,1)S(1)}, bf16[128,1024]{1,0:T(8,128)(2,1)S(1)}, u32[]{:S(2)}, u32[]{:S(2)}) collective-permute-start(bf16[128,1024]{1,0:T(8,128)(2,1)S(1)} %get-tuple-element.72), channel_id=1, source_target_pairs={{0,128},{64,192},{128,0},{192,64},{1,129},{65,193},{129,1},{193,65... | collective-permute-start | bytes 786440 | tf_op jit(solution)/shard_map/query_2/ppermute | solution.py:440
  17.9 3.5 %collective-permute-done.10.refs_7_.refs_3_ = bf16[528,256]{1,0:T(8,128)(2,1)S(1)} collective-permute-done((bf16[528,256]{1,0:T(8,128)(2,1)S(1)}, bf16[528,256]{1,0:T(8,128)(2,1)S(1)}, u32[]{:S(2)}, u32[]{:S(2)}) %collective-permute-start.10) | collective-permute-done | bytes 270368 | tf_op jit(solution)/shard_map/w_1/ppermute | solution.py:446
  21.4 2.3 %collective-permute-start.6 = (bf16[128,1024]{1,0:T(8,128)(2,1)S(1)}, bf16[128,1024]{1,0:T(8,128)(2,1)S(1)}, u32[]{:S(2)}, u32[]{:S(2)}) collective-permute-start(bf16[128,1024]{1,0:T(8,128)(2,1)S(1)} %get-tuple-element.70), channel_id=1, source_target_pairs={{0,64},{64,0},{128,192},{192,128},{1,65},{65,1},{129,193},{193,129... | collective-permute-start | bytes 786440 | tf_op jit(solution)/shard_map/query_1/ppermute | solution.py:440
  23.7 0.0 collective-permute-done.7.refs_3_
  23.7 0.0 collective-permute-start.12
  23.8 5.7 %collective-permute-done.9.refs_4_ = bf16[128,1024]{1,0:T(8,128)(2,1)S(1)} collective-permute-done((bf16[128,1024]{1,0:T(8,128)(2,1)S(1)}, bf16[128,1024]{1,0:T(8,128)(2,1)S(1)}, u32[]{:S(2)}, u32[]{:S(2)}) %collective-permute-start.9) | collective-permute-done | bytes 262176 | tf_op jit(solution)/shard_map/query_3/ppermute | solution.py:440
  29.5 1.4 %collective-permute-done.8.refs_3_ = bf16[128,1024]{1,0:T(8,128)(2,1)S(1)} collective-permute-done((bf16[128,1024]{1,0:T(8,128)(2,1)S(1)}, bf16[128,1024]{1,0:T(8,128)(2,1)S(1)}, u32[]{:S(2)}, u32[]{:S(2)}) %collective-permute-start.8) | collective-permute-done | bytes 262176 | tf_op jit(solution)/shard_map/query_2/ppermute | solution.py:440
  30.8 1.3 %collective-permute-start.11 = (bf16[256,1024]{1,0:T(8,128)(2,1)S(1)}, bf16[256,1024]{1,0:T(8,128)(2,1)S(1)}, u32[]{:S(2)}, u32[]{:S(2)}) collective-permute-start(bf16[256,1024]{1,0:T(8,128)(2,1)S(1)} %pad_maximum_fusion.1), channel_id=1, source_target_pairs={{0,128},{64,192},{128,0},{192,64},{1,129},{65,193},{129,1},{193,65... | collective-permute-start | bytes 1572872 | tf_op jit(solution)/shard_map/grad_out_2/ppermute | solution.py:440
  32.2 0.0 collective-permute-done.3.refs_6_.refs_11_
  32.2 2.4 %collective-permute-start.4 = (bf16[16,128]{1,0:T(8,128)(2,1)S(1)}, bf16[16,128]{1,0:T(8,128)(2,1)S(1)}, u32[]{:S(2)}, u32[]{:S(2)}) collective-permute-start(bf16[16,128]{1,0:T(8,128)(2,1)S(1)} %slice_add_fusion), channel_id=1, source_target_pairs={{0,64},{64,0},{128,192},{192,128},{1,65},{65,1},{129,193},{193,129... | collective-permute-start | bytes 12296 | tf_op jit(solution)/shard_map/before_token_1/ppermute | solution.py:440
  34.6 0.0 collective-permute-done.12.refs_2_.refs_10_
  34.6 1.7 %collective-permute-start.13 = (bf16[528,256]{1,0:T(8,128)(2,1)S(1)}, bf16[528,256]{1,0:T(8,128)(2,1)S(1)}, u32[]{:S(2)}, u32[]{:S(2)}) collective-permute-start(bf16[528,256]{1,0:T(8,128)(2,1)S(1)} %collective-permute-done.12.refs_2_.refs_10_), channel_id=1, source_target_pairs={{0,8},{8,16},{16,24},{24,32},{32,40},{40,48},{48,56},{56,0},{1,9},... | collective-permute-start | bytes 811016 | tf_op jit(solution)/shard_map/w_3/ppermute | solution.py:446
  36.2 0.4 collective-permute-start.5
  36.6 0.8 collective-permute-done.5.refs_0_
  37.4 7.7 %forward_first.1 = (bf16[512,1024]{1,0:T(8,128)(2,1)S(1)}, f32[8,2,144,256]{3,2,1,0:T(8,128)S(1)}, f32[8,2,8,256]{3,2,1,0:T(8,128)S(1)}, bf16[8,3,256,256]{3,2,1...) custom-call(s32[1]{0:T(128)} %bitcast.h_ref, ...), custom_call_target="tpu_custom_call" | custom-call | flops 469762048 | bytes 65536 | tf_op jit(solution)/shard_map/forward_first/pallas_call | solution.py:221
  45.1 0.3 collective-permute-done.13.refs_3_.refs_9_
  45.4 4.5 %forward_last.1 = (bf16[128,1024]{1,0:T(8,128)(2,1)S(1)}, bf16[128,1024]{1,0:T(8,128)(2,1)S(1)}, bf16[256,1024]{1,0:T(8,128)(2,1)S(1)}, f32[8,2,16,256]{3,2,1,0:...) custom-call(s32[1]{0:T(128)} %bitcast.h_ref, ...), custom_call_target="tpu_custom_call" | custom-call | flops 268435456 | bytes 65536 | tf_op jit(solution)/shard_map/forward_last/pallas_call | solution.py:221
  49.9 0.0 copy-start
  49.9 2.2 %collective-permute-start.16 = (bf16[256,1024]{1,0:T(8,128)(2,1)S(1)}, bf16[256,1024]{1,0:T(8,128)(2,1)S(1)}, u32[]{:S(2)}, u32[]{:S(2)}) collective-permute-start(bf16[256,1024]{1,0:T(8,128)(2,1)S(1)} %get-tuple-element.42.refs_7_), channel_id=1, source_target_pairs={{0,128},{64,192},{128,0},{192,64},{1,129},{65,193},{129,1},{193,65... | collective-permute-start | bytes 1572872 | tf_op jit(solution)/shard_map/out_2/ppermute | solution.py:440
  52.1 0.0 collective-permute-done.11.refs_4_
  52.1 9.6 %backward_first.1 = (f32[8,2,128,256]{3,2,1,0:T(8,128)S(1)}, bf16[512,2048]{1,0:T(8,128)(2,1)S(1)}, bf16[512,256]{1,0:T(8,128)(2,1)S(1)}, bf16[512,256]{1,0:T(8,128)(2,1)S(1)}, bf16[512,256]{1,0:T(8,128)(2,1)S(1)}) custom-call(s32[1]{0:T(128)} %bitcast.h_ref, bf16[512,1024]{1,0:T(8,128)(2,1)S(1)} %get-tuple-element.36.refs_0_, ...), custom_call_target="tpu_custom_call" | custom-call | flops 805306368 | bytes 65536 | tf_op jit(solution)/shard_map/backward_first/pallas_call | solution.py:221
  61.7 3.0 %collective-permute-start.20 = (bf16[512,256]{1,0:T(8,128)(2,1)S(1)}, bf16[512,256]{1,0:T(8,128)(2,1)S(1)}, u32[]{:S(2)}, u32[]{:S(2)}) collective-permute-start(bf16[512,256]{1,0:T(8,128)(2,1)S(1)} %get-tuple-element.57), channel_id=1, source_target_pairs={{0,56},{8,0},{16,8},{24,16},{32,24},{40,32},{48,40},{56,48},{1,57}... | collective-permute-start | bytes 786440 | tf_op jit(solution)/shard_map/term_3/ppermute | solution.py:446
  64.7 7.7 %backward_last.1 = (bf16[128,1024]{1,0:T(8,128)(2,1)S(1)}, bf16[128,1024]{1,0:T(8,128)(2,1)S(1)}, bf16[256,1024]{1,0:T(8,128)(2,1)S(1)}, bf16[512,256]{1,0:T(8,128)(2,1)S(1)}, bf16[512,256]{1,0:T(8,128)(2,1)S(1)}) custom-call(s32[1]{0:T(128)} %bitcast.h_ref, bf16[512,1024]{1,0:T(8,128)(2,1)S(1)} %get-tuple-element.36.refs_0_, ...), custom_call_target="tpu_custom_call" | custom-call | flops 671088640 | bytes 65536 | tf_op jit(solution)/shard_map/backward_last/pallas_call | solution.py:221
  72.4 1.0 collective-permute-start.14
  73.4 0.0 collective-permute-done.20
  73.4 0.1 add_convert_fusion.2
  73.5 1.4 %collective-permute-start.21 = (bf16[512,256]{1,0:T(8,128)(2,1)S(1)}, bf16[512,256]{1,0:T(8,128)(2,1)S(1)}, u32[]{:S(2)}, u32[]{:S(2)}) collective-permute-start(bf16[512,256]{1,0:T(8,128)(2,1)S(1)} %add_convert_fusion.2), channel_id=1, source_target_pairs={{0,56},{8,0},{16,8},{24,16},{32,24},{40,32},{48,40},{56,48},{1,57}... | collective-permute-start | bytes 786440 | tf_op jit(solution)/shard_map/term_2/ppermute | solution.py:446
  74.9 1.5 %collective-permute-start.15 = (bf16[128,1024]{1,0:T(8,128)(2,1)S(1)}, bf16[128,1024]{1,0:T(8,128)(2,1)S(1)}, u32[]{:S(2)}, u32[]{:S(2)}) collective-permute-start(bf16[128,1024]{1,0:T(8,128)(2,1)S(1)} %get-tuple-element.41.refs_6_), channel_id=1, source_target_pairs={{0,64},{64,0},{128,192},{192,128},{1,65},{65,1},{129,193},{193,129... | collective-permute-start | bytes 786440 | tf_op jit(solution)/shard_map/out_1/ppermute | solution.py:440
  76.4 0.0 collective-permute-done.16
  76.4 0.7 fusion.1
  77.1 0.0 collective-permute-start.17
  77.1 6.5 %collective-permute-start.23 = (bf16[512,256]{1,0:T(8,128)(2,1)S(1)}, bf16[512,256]{1,0:T(8,128)(2,1)S(1)}, u32[]{:S(2)}, u32[]{:S(2)}) collective-permute-start(bf16[512,256]{1,0:T(8,128)(2,1)S(1)} %get-tuple-element.62), channel_id=1, source_target_pairs={{0,63},{1,0},{2,1},{3,2},{4,3},{5,4},{6,5},{7,6},{8,7},{9,8},{10,9... | collective-permute-start | bytes 786440 | tf_op jit(solution)/shard_map/term_before/ppermute | solution.py:446
  83.7 0.1 add_convert_fusion.1
  83.7 0.9 collective-permute-start.22
  84.6 1.1 collective-permute-start.18
  85.7 0.7 copy-done.6
  86.4 2.2 %placed.2 = bf16[128,4096]{1,0:T(8,128)(2,1)} custom-call(s32[1]{0:T(128)} %bitcast.h_ref, bf16[128,1024]{1,0:T(8,128)(2,1)} %copy-done, bf16[128,1024]{1,0:T(8,128)(2,1)} %copy-done.5, bf16[128,1024]{1,0:T(8,128)(2,1)} %get-tuple-element.76.refs_2_, bf16[128,1024]{1,0:T(8,128)(2,1)} %copy-done.6), custom_call_target="tpu_custom_call" | custom-call | bytes 2097152 | tf_op jit(solution)/shard_map/placed/pallas_call | solution.py:412
  88.6 3.2 %collective-permute-done.14 = bf16[256,1024]{1,0:T(8,128)(2,1)S(1)} collective-permute-done((bf16[256,1024]{1,0:T(8,128)(2,1)S(1)}, bf16[256,1024]{1,0:T(8,128)(2,1)S(1)}, u32[]{:S(2)}, u32[]{:S(2)}) %collective-permute-start.14) | collective-permute-done | bytes 524320 | tf_op jit(solution)/shard_map/grad_query_2/ppermute | solution.py:440
  91.8 0.8 fusion
  92.5 2.2 %collective-permute-start.19 = (bf16[128,1024]{1,0:T(8,128)(2,1)S(1)}, bf16[128,1024]{1,0:T(8,128)(2,1)S(1)}, u32[]{:S(2)}, u32[]{:S(2)}) collective-permute-start(bf16[128,1024]{1,0:T(8,128)(2,1)S(1)} %get-tuple-element.73), channel_id=1, source_target_pairs={{0,64},{64,0},{128,192},{192,128},{1,65},{65,1},{129,193},{193,129... | collective-permute-start | bytes 786440 | tf_op jit(solution)/shard_map/grad_query_1/ppermute | solution.py:440
  94.7 0.8 collective-permute-done.22
  95.5 0.1 add_convert_fusion
  95.6 0.6 fusion.2
  96.2 2.3 %collective-permute-start.26 = (bf16[128,256]{1,0:T(8,128)(2,1)S(1)}, bf16[128,256]{1,0:T(8,128)(2,1)S(1)}, u32[]{:S(2)}, u32[]{:S(2)}) collective-permute-start(bf16[128,256]{1,0:T(8,128)(2,1)S(1)} %get-tuple-element.77), channel_id=1, source_target_pairs={{0,192},{64,128},{128,64},{192,0},{1,193},{65,129},{129,65},{193,1... | collective-permute-start | bytes 196616 | tf_op jit(solution)/shard_map/grad_kv_3/ppermute | solution.py:440
  98.5 2.0 %collective-permute-start.25 = (bf16[128,256]{1,0:T(8,128)(2,1)S(1)}, bf16[128,256]{1,0:T(8,128)(2,1)S(1)}, u32[]{:S(2)}, u32[]{:S(2)}) collective-permute-start(bf16[128,256]{1,0:T(8,128)(2,1)S(1)} %get-tuple-element.78), channel_id=1, source_target_pairs={{0,128},{64,192},{128,0},{192,64},{1,129},{65,193},{129,1},{193,65... | collective-permute-start | bytes 196616 | tf_op jit(solution)/shard_map/grad_kv_2/ppermute | solution.py:440
  100.5 1.4 %collective-permute-done.26.refs_7_ = bf16[128,256]{1,0:T(8,128)(2,1)S(1)} collective-permute-done((bf16[128,256]{1,0:T(8,128)(2,1)S(1)}, bf16[128,256]{1,0:T(8,128)(2,1)S(1)}, u32[]{:S(2)}, u32[]{:S(2)}) %collective-permute-start.26) | collective-permute-done | bytes 65568 | tf_op jit(solution)/shard_map/grad_kv_3/ppermute | solution.py:440
  101.8 1.7 %collective-permute-done.25.refs_6_ = bf16[128,256]{1,0:T(8,128)(2,1)S(1)} collective-permute-done((bf16[128,256]{1,0:T(8,128)(2,1)S(1)}, bf16[128,256]{1,0:T(8,128)(2,1)S(1)}, u32[]{:S(2)}, u32[]{:S(2)}) %collective-permute-start.25) | collective-permute-done | bytes 65568 | tf_op jit(solution)/shard_map/grad_kv_2/ppermute | solution.py:440
  103.6 0.6 copy-done.8
  104.2 0.1 copy-done.9
  104.2 0.1 copy-done.4
  104.3 2.4 %placed.3 = (bf16[128,4096]{1,0:T(8,128)(2,1)}, f32[128,1024]{1,0:T(8,128)}) custom-call(s32[1]{0:T(128)} %bitcast.h_ref, bf16[128,1024]{1,0:T(8,128)(2,1)} %copy-done.1, bf16[128,1024]{1,0:T(8,128)(2,1)} %copy-done.3, bf16[128,1024]{1,0:T(8,128)(2,1)} %get-tuple-element.74.refs_2_, bf16[128,1024]{1,0:T(8,128)(2,1)} %copy-done.4, ...), custom_call_target="tpu_custom_call" | custom-call | bytes 2097152 | tf_op jit(solution)/shard_map/placed/pallas_call | solution.py:412
  (36 shorter events, 0.2 us)
Async XLA Ops:
  0.6 9.5 %copy-start.10 = (s32[128]{0:T(128)S(1)}, s32[128]{0:T(128)}, u32[]{:S(2)}) copy-start(s32[128]{0:T(128)} %param.7) | copy-start | bytes 1540
  0.6 12.0 %copy-start.2 = (bf16[128,4096]{1,0:T(8,128)(2,1)S(1)}, bf16[128,4096]{1,0:T(8,128)(2,1)}, u32[]{:S(2)}) copy-start(bf16[128,4096]{1,0:T(8,128)(2,1)} %param.4) | copy-start | bytes 3145732
  1.7 8.9 %collective-permute-start.2 = (bf16[128,256]{1,0:T(8,128)(2,1)S(1)}, bf16[128,256]{1,0:T(8,128)(2,1)S(1)}, u32[]{:S(2)}, u32[]{:S(2)}) collective-permute-start(bf16[128,256]{1,0:T(8,128)(2,1)S(1)} %get-tuple-element.81), channel_id=1, source_target_pairs={{0,192},{64,128},{128,64},{192,0},{1,193},{65,129},{129,65},{193,1... | collective-permute-start | bytes 196616 | tf_op jit(solution)/shard_map/kv_3/ppermute | solution.py:440
  5.9 4.3 %collective-permute-start = (bf16[128,256]{1,0:T(8,128)(2,1)S(1)}, bf16[128,256]{1,0:T(8,128)(2,1)S(1)}, u32[]{:S(2)}, u32[]{:S(2)}) collective-permute-start(bf16[128,256]{1,0:T(8,128)(2,1)S(1)} %get-tuple-element.82), channel_id=1, source_target_pairs={{0,64},{64,0},{128,192},{192,128},{1,65},{65,1},{129,193},{193,129... | collective-permute-start | bytes 196616 | tf_op jit(solution)/shard_map/kv_1/ppermute | solution.py:440
  5.9 4.6 %collective-permute-start.1 = (bf16[128,256]{1,0:T(8,128)(2,1)S(1)}, bf16[128,256]{1,0:T(8,128)(2,1)S(1)}, u32[]{:S(2)}, u32[]{:S(2)}) collective-permute-start(bf16[128,256]{1,0:T(8,128)(2,1)S(1)} %get-tuple-element.84), channel_id=1, source_target_pairs={{0,128},{64,192},{128,0},{192,64},{1,129},{65,193},{129,1},{193,65... | collective-permute-start | bytes 196616 | tf_op jit(solution)/shard_map/kv_2/ppermute | solution.py:440
  9.2 14.5 %collective-permute-start.7 = (bf16[256,1024]{1,0:T(8,128)(2,1)S(1)}, bf16[256,1024]{1,0:T(8,128)(2,1)S(1)}, u32[]{:S(2)}, u32[]{:S(2)}) collective-permute-start(bf16[256,1024]{1,0:T(8,128)(2,1)S(1)} %pad_maximum_fusion), channel_id=1, source_target_pairs={{0,64},{64,0},{128,192},{192,128},{1,65},{65,1},{129,193},{193,129... | collective-permute-start | bytes 1572872 | tf_op jit(solution)/shard_map/grad_out_1/ppermute | solution.py:440
  10.6 10.8 %collective-permute-start.10 = (bf16[528,256]{1,0:T(8,128)(2,1)S(1)}, bf16[528,256]{1,0:T(8,128)(2,1)S(1)}, u32[]{:S(2)}, u32[]{:S(2)}) collective-permute-start(bf16[528,256]{1,0:T(8,128)(2,1)S(1)} %constant_dynamic-update-slice_fusion.refs_5_.refs_1_), channel_id=1, source_target_pairs={{0,8},{8,16},{16,24},{24,32},{32,40},{40,48},{48,56},{56,0},{1,9},... | collective-permute-start | bytes 811016 | tf_op jit(solution)/shard_map/w_1/ppermute | solution.py:446
  12.3 19.9 %collective-permute-start.3 = (bf16[528,256]{1,0:T(8,128)(2,1)S(1)}, bf16[528,256]{1,0:T(8,128)(2,1)S(1)}, u32[]{:S(2)}, u32[]{:S(2)}) collective-permute-start(bf16[528,256]{1,0:T(8,128)(2,1)S(1)} %constant_dynamic-update-slice_fusion.refs_5_.refs_1_), channel_id=1, source_target_pairs={{0,1},{1,2},{2,3},{3,4},{4,5},{5,6},{6,7},{7,8},{8,9},{9,10},{10,1... | collective-permute-start | bytes 811016 | tf_op jit(solution)/shard_map/before/ppermute | solution.py:446
  12.7 16.8 %collective-permute-start.9 = (bf16[128,1024]{1,0:T(8,128)(2,1)S(1)}, bf16[128,1024]{1,0:T(8,128)(2,1)S(1)}, u32[]{:S(2)}, u32[]{:S(2)}) collective-permute-start(bf16[128,1024]{1,0:T(8,128)(2,1)S(1)} %get-tuple-element.69), channel_id=1, source_target_pairs={{0,192},{64,128},{128,64},{192,0},{1,193},{65,129},{129,65},{193,1... | collective-permute-start | bytes 786440 | tf_op jit(solution)/shard_map/query_3/ppermute | solution.py:440
  16.7 14.2 %collective-permute-start.8 = (bf16[128,1024]{1,0:T(8,128)(2,1)S(1)}, bf16[128,1024]{1,0:T(8,128)(2,1)S(1)}, u32[]{:S(2)}, u32[]{:S(2)}) collective-permute-start(bf16[128,1024]{1,0:T(8,128)(2,1)S(1)} %get-tuple-element.72), channel_id=1, source_target_pairs={{0,128},{64,192},{128,0},{192,64},{1,129},{65,193},{129,1},{193,65... | collective-permute-start | bytes 786440 | tf_op jit(solution)/shard_map/query_2/ppermute | solution.py:440
  21.4 15.2 %collective-permute-start.6 = (bf16[128,1024]{1,0:T(8,128)(2,1)S(1)}, bf16[128,1024]{1,0:T(8,128)(2,1)S(1)}, u32[]{:S(2)}, u32[]{:S(2)}) collective-permute-start(bf16[128,1024]{1,0:T(8,128)(2,1)S(1)} %get-tuple-element.70), channel_id=1, source_target_pairs={{0,64},{64,0},{128,192},{192,128},{1,65},{65,1},{129,193},{193,129... | collective-permute-start | bytes 786440 | tf_op jit(solution)/shard_map/query_1/ppermute | solution.py:440
  23.7 10.9 %collective-permute-start.12 = (bf16[528,256]{1,0:T(8,128)(2,1)S(1)}, bf16[528,256]{1,0:T(8,128)(2,1)S(1)}, u32[]{:S(2)}, u32[]{:S(2)}) collective-permute-start(bf16[528,256]{1,0:T(8,128)(2,1)S(1)} %collective-permute-done.10.refs_7_.refs_3_), channel_id=1, source_target_pairs={{0,8},{8,16},{16,24},{24,32},{32,40},{40,48},{48,56},{56,0},{1,9},... | collective-permute-start | bytes 811016 | tf_op jit(solution)/shard_map/w_2/ppermute | solution.py:446
  30.8 21.2 %collective-permute-start.11 = (bf16[256,1024]{1,0:T(8,128)(2,1)S(1)}, bf16[256,1024]{1,0:T(8,128)(2,1)S(1)}, u32[]{:S(2)}, u32[]{:S(2)}) collective-permute-start(bf16[256,1024]{1,0:T(8,128)(2,1)S(1)} %pad_maximum_fusion.1), channel_id=1, source_target_pairs={{0,128},{64,192},{128,0},{192,64},{1,129},{65,193},{129,1},{193,65... | collective-permute-start | bytes 1572872 | tf_op jit(solution)/shard_map/grad_out_2/ppermute | solution.py:440
  32.2 4.0 %collective-permute-start.4 = (bf16[16,128]{1,0:T(8,128)(2,1)S(1)}, bf16[16,128]{1,0:T(8,128)(2,1)S(1)}, u32[]{:S(2)}, u32[]{:S(2)}) collective-permute-start(bf16[16,128]{1,0:T(8,128)(2,1)S(1)} %slice_add_fusion), channel_id=1, source_target_pairs={{0,64},{64,0},{128,192},{192,128},{1,65},{65,1},{129,193},{193,129... | collective-permute-start | bytes 12296 | tf_op jit(solution)/shard_map/before_token_1/ppermute | solution.py:440
  34.6 10.8 %collective-permute-start.13 = (bf16[528,256]{1,0:T(8,128)(2,1)S(1)}, bf16[528,256]{1,0:T(8,128)(2,1)S(1)}, u32[]{:S(2)}, u32[]{:S(2)}) collective-permute-start(bf16[528,256]{1,0:T(8,128)(2,1)S(1)} %collective-permute-done.12.refs_2_.refs_10_), channel_id=1, source_target_pairs={{0,8},{8,16},{16,24},{24,32},{32,40},{40,48},{48,56},{56,0},{1,9},... | collective-permute-start | bytes 811016 | tf_op jit(solution)/shard_map/w_3/ppermute | solution.py:446
  36.2 1.2 %collective-permute-start.5 = (bf16[16,128]{1,0:T(8,128)(2,1)S(1)}, bf16[16,128]{1,0:T(8,128)(2,1)S(1)}, u32[]{:S(2)}, u32[]{:S(2)}) collective-permute-start(bf16[16,128]{1,0:T(8,128)(2,1)S(1)} %broadcast_add_fusion), channel_id=1, source_target_pairs={{0,64},{64,0},{128,192},{192,128},{1,65},{65,1},{129,193},{193,129... | collective-permute-start | bytes 12296 | tf_op jit(solution)/shard_map/before_token_1/ppermute | solution.py:440
  49.9 11.8 %copy-start = (bf16[128,1024]{1,0:T(8,128)(2,1)}, bf16[128,1024]{1,0:T(8,128)(2,1)S(1)}, u32[]{:S(2)}) copy-start(bf16[128,1024]{1,0:T(8,128)(2,1)S(1)} %get-tuple-element.40.refs_5_.refs_0_) | copy-start | bytes 786436
  49.9 26.5 %collective-permute-start.16 = (bf16[256,1024]{1,0:T(8,128)(2,1)S(1)}, bf16[256,1024]{1,0:T(8,128)(2,1)S(1)}, u32[]{:S(2)}, u32[]{:S(2)}) collective-permute-start(bf16[256,1024]{1,0:T(8,128)(2,1)S(1)} %get-tuple-element.42.refs_7_), channel_id=1, source_target_pairs={{0,128},{64,192},{128,0},{192,64},{1,129},{65,193},{129,1},{193,65... | collective-permute-start | bytes 1572872 | tf_op jit(solution)/shard_map/out_2/ppermute | solution.py:440
  61.7 11.7 %collective-permute-start.20 = (bf16[512,256]{1,0:T(8,128)(2,1)S(1)}, bf16[512,256]{1,0:T(8,128)(2,1)S(1)}, u32[]{:S(2)}, u32[]{:S(2)}) collective-permute-start(bf16[512,256]{1,0:T(8,128)(2,1)S(1)} %get-tuple-element.57), channel_id=1, source_target_pairs={{0,56},{8,0},{16,8},{24,16},{32,24},{40,32},{48,40},{56,48},{1,57}... | collective-permute-start | bytes 786440 | tf_op jit(solution)/shard_map/term_3/ppermute | solution.py:446
  72.4 4.0 %copy-start.1 = (bf16[128,1024]{1,0:T(8,128)(2,1)}, bf16[128,1024]{1,0:T(8,128)(2,1)S(1)}, u32[]{:S(2)}) copy-start(bf16[128,1024]{1,0:T(8,128)(2,1)S(1)} %get-tuple-element.53.refs_0_) | copy-start | bytes 786436
  72.4 19.4 %collective-permute-start.14 = (bf16[256,1024]{1,0:T(8,128)(2,1)S(1)}, bf16[256,1024]{1,0:T(8,128)(2,1)S(1)}, u32[]{:S(2)}, u32[]{:S(2)}) collective-permute-start(bf16[256,1024]{1,0:T(8,128)(2,1)S(1)} %get-tuple-element.51), channel_id=1, source_target_pairs={{0,128},{64,192},{128,0},{192,64},{1,129},{65,193},{129,1},{193,65... | collective-permute-start | bytes 1572872 | tf_op jit(solution)/shard_map/grad_query_2/ppermute | solution.py:440
  73.5 10.2 %collective-permute-start.21 = (bf16[512,256]{1,0:T(8,128)(2,1)S(1)}, bf16[512,256]{1,0:T(8,128)(2,1)S(1)}, u32[]{:S(2)}, u32[]{:S(2)}) collective-permute-start(bf16[512,256]{1,0:T(8,128)(2,1)S(1)} %add_convert_fusion.2), channel_id=1, source_target_pairs={{0,56},{8,0},{16,8},{24,16},{32,24},{40,32},{48,40},{56,48},{1,57}... | collective-permute-start | bytes 786440 | tf_op jit(solution)/shard_map/term_2/ppermute | solution.py:446
  74.9 9.7 %collective-permute-start.15 = (bf16[128,1024]{1,0:T(8,128)(2,1)S(1)}, bf16[128,1024]{1,0:T(8,128)(2,1)S(1)}, u32[]{:S(2)}, u32[]{:S(2)}) collective-permute-start(bf16[128,1024]{1,0:T(8,128)(2,1)S(1)} %get-tuple-element.41.refs_6_), channel_id=1, source_target_pairs={{0,64},{64,0},{128,192},{192,128},{1,65},{65,1},{129,193},{193,129... | collective-permute-start | bytes 786440 | tf_op jit(solution)/shard_map/out_1/ppermute | solution.py:440
  77.1 8.5 %collective-permute-start.17 = (bf16[128,1024]{1,0:T(8,128)(2,1)S(1)}, bf16[128,1024]{1,0:T(8,128)(2,1)S(1)}, u32[]{:S(2)}, u32[]{:S(2)}) collective-permute-start(bf16[128,1024]{1,0:T(8,128)(2,1)S(1)} %get-tuple-element.75), channel_id=1, source_target_pairs={{0,64},{64,0},{128,192},{192,128},{1,65},{65,1},{129,193},{193,129... | collective-permute-start | bytes 786440 | tf_op jit(solution)/shard_map/out_1/ppermute | solution.py:440
  77.1 17.6 %collective-permute-start.23 = (bf16[512,256]{1,0:T(8,128)(2,1)S(1)}, bf16[512,256]{1,0:T(8,128)(2,1)S(1)}, u32[]{:S(2)}, u32[]{:S(2)}) collective-permute-start(bf16[512,256]{1,0:T(8,128)(2,1)S(1)} %get-tuple-element.62), channel_id=1, source_target_pairs={{0,63},{1,0},{2,1},{3,2},{4,3},{5,4},{6,5},{7,6},{8,7},{9,8},{10,9... | collective-permute-start | bytes 786440 | tf_op jit(solution)/shard_map/term_before/ppermute | solution.py:446
  83.7 11.7 %collective-permute-start.22 = (bf16[512,256]{1,0:T(8,128)(2,1)S(1)}, bf16[512,256]{1,0:T(8,128)(2,1)S(1)}, u32[]{:S(2)}, u32[]{:S(2)}) collective-permute-start(bf16[512,256]{1,0:T(8,128)(2,1)S(1)} %add_convert_fusion.1), channel_id=1, source_target_pairs={{0,56},{8,0},{16,8},{24,16},{32,24},{40,32},{48,40},{56,48},{1,57}... | collective-permute-start | bytes 786440 | tf_op jit(solution)/shard_map/term_1/ppermute | solution.py:446
  84.6 1.1 %copy-start.5 = (bf16[128,1024]{1,0:T(8,128)(2,1)}, bf16[128,1024]{1,0:T(8,128)(2,1)S(1)}, u32[]{:S(2)}) copy-start(bf16[128,1024]{1,0:T(8,128)(2,1)S(1)} %collective-permute-done.15.refs_1_) | copy-start | bytes 786436
  84.6 15.8 %collective-permute-start.18 = (bf16[128,1024]{1,0:T(8,128)(2,1)S(1)}, bf16[128,1024]{1,0:T(8,128)(2,1)S(1)}, u32[]{:S(2)}, u32[]{:S(2)}) collective-permute-start(bf16[128,1024]{1,0:T(8,128)(2,1)S(1)} %get-tuple-element.54), channel_id=1, source_target_pairs={{0,64},{64,0},{128,192},{192,128},{1,65},{65,1},{129,193},{193,129... | collective-permute-start | bytes 786440 | tf_op jit(solution)/shard_map/grad_query_1/ppermute | solution.py:440
  85.7 0.7 copy-start.6
  92.5 11.0 %collective-permute-start.19 = (bf16[128,1024]{1,0:T(8,128)(2,1)S(1)}, bf16[128,1024]{1,0:T(8,128)(2,1)S(1)}, u32[]{:S(2)}, u32[]{:S(2)}) collective-permute-start(bf16[128,1024]{1,0:T(8,128)(2,1)S(1)} %get-tuple-element.73), channel_id=1, source_target_pairs={{0,64},{64,0},{128,192},{192,128},{1,65},{65,1},{129,193},{193,129... | collective-permute-start | bytes 786440 | tf_op jit(solution)/shard_map/grad_query_1/ppermute | solution.py:440
  96.2 5.6 %collective-permute-start.26 = (bf16[128,256]{1,0:T(8,128)(2,1)S(1)}, bf16[128,256]{1,0:T(8,128)(2,1)S(1)}, u32[]{:S(2)}, u32[]{:S(2)}) collective-permute-start(bf16[128,256]{1,0:T(8,128)(2,1)S(1)} %get-tuple-element.77), channel_id=1, source_target_pairs={{0,192},{64,128},{128,64},{192,0},{1,193},{65,129},{129,65},{193,1... | collective-permute-start | bytes 196616 | tf_op jit(solution)/shard_map/grad_kv_3/ppermute | solution.py:440
  98.5 5.1 %collective-permute-start.25 = (bf16[128,256]{1,0:T(8,128)(2,1)S(1)}, bf16[128,256]{1,0:T(8,128)(2,1)S(1)}, u32[]{:S(2)}, u32[]{:S(2)}) collective-permute-start(bf16[128,256]{1,0:T(8,128)(2,1)S(1)} %get-tuple-element.78), channel_id=1, source_target_pairs={{0,128},{64,192},{128,0},{192,64},{1,129},{65,193},{129,1},{193,65... | collective-permute-start | bytes 196616 | tf_op jit(solution)/shard_map/grad_kv_2/ppermute | solution.py:440
  100.4 3.1 %collective-permute-start.24 = (bf16[128,256]{1,0:T(8,128)(2,1)S(1)}, bf16[128,256]{1,0:T(8,128)(2,1)S(1)}, u32[]{:S(2)}, u32[]{:S(2)}) collective-permute-start(bf16[128,256]{1,0:T(8,128)(2,1)S(1)} %get-tuple-element.79), channel_id=1, source_target_pairs={{0,64},{64,0},{128,192},{192,128},{1,65},{65,1},{129,193},{193,129... | collective-permute-start | bytes 196616 | tf_op jit(solution)/shard_map/grad_kv_1/ppermute | solution.py:440
  100.4 3.1 %copy-start.3 = (bf16[128,1024]{1,0:T(8,128)(2,1)}, bf16[128,1024]{1,0:T(8,128)(2,1)S(1)}, u32[]{:S(2)}) copy-start(bf16[128,1024]{1,0:T(8,128)(2,1)S(1)} %collective-permute-done.18.refs_1_) | copy-start | bytes 786436
  101.8 1.8 %copy-start.7 = (bf16[128,256]{1,0:T(8,128)(2,1)}, bf16[128,256]{1,0:T(8,128)(2,1)S(1)}, u32[]{:S(2)}) copy-start(bf16[128,256]{1,0:T(8,128)(2,1)S(1)} %collective-permute-done.26.refs_7_) | copy-start | bytes 196612
  103.6 0.6 copy-start.8
  103.6 0.7 copy-start.9
  103.6 0.7 copy-start.4

commit v2 on v1

--- a/solution.py
+++ b/solution.py
@@ -89,9 +89,11 @@
     return ref[pl.ds(row, n), head * D : (head + 1) * D]
 
 
-def weigh_blocks(layout, heads, q_ref, mask, vt_ref, s_ref, w_refs, old):
+def weigh_blocks(layout, heads, q_ref, mask, vt_ref, s_ref, w_refs, old, piped):
     tops = [[None, None] if old is None else list(old[a]) for a in range(heads)]
-    for a in range(heads):
+    acc = [[None, None] for _ in range(heads)]
+
+    def scores(a):
         for n, (keys, key_row, query_row, first, masked) in enumerate(layout.blocks):
             s = dot(keys[pl.ds(key_row, HALF), :D], cols(q_ref, query_row, HALF, a), NT)
             if masked:
@@ -105,8 +107,8 @@
                 if first is not True and first is not False:
                     t = jnp.where(first if half == 0 else jnp.logical_not(first), top, -1e30)
                 tops[a][half] = t if tops[a][half] is None else jnp.maximum(tops[a][half], t)
-    acc = [[None, None] for _ in range(heads)]
-    for a in range(heads):
+
+    def sums(a):
         for n, (keys, key_row, query_row, first, masked) in enumerate(layout.blocks):
             if first is True:
                 m = tops[a][0]
@@ -120,6 +122,13 @@
                 w_ref[r : r + STRIP, :] = jnp.exp2((x - m) * EXP2_SCALE).astype(bf16)
             for half, x in enumerate(split(first, dot(vt_ref[n], w_ref[...], NN))):
                 acc[a][half] = add(acc[a][half], x)
+
+    for a in range(heads):
+        scores(a)
+        if piped and a:
+            sums(a - 1)
+    for a in range(heads - 1 if piped else 0, heads):
+        sums(a)
     return tops, acc
 
 
@@ -142,7 +151,7 @@
     load_vt(layout, vt_ref)
     for k, piece in enumerate((q0, q1, q2, q3)):
         q_out[k * PIECE : (k + 1) * PIECE, :] = piece[...]
-    tops, acc = weigh_blocks(layout, heads, q_out, causal(h), vt_ref, s_ref, w_refs, None)
+    tops, acc = weigh_blocks(layout, heads, q_out, causal(h), vt_ref, s_ref, w_refs, None, True)
     for a in range(heads):
         for half in range(2):
             state_ref[a, half] = acc[a][half]
@@ -158,7 +167,7 @@
     layout = Layout(h, own, windows, False)
     load_vt(layout, vt_ref)
     old = [[top_in[a, half, :1, :] for half in range(2)] for a in range(heads)]
-    tops, acc = weigh_blocks(layout, heads, q_ref, None, vt_ref, s_ref, w_refs, old)
+    tops, acc = weigh_blocks(layout, heads, q_ref, None, vt_ref, s_ref, w_refs, old, False)
     for a in range(heads):
         for half, row in enumerate((layout.q_early, layout.q_late)):
             shrink = jnp.exp2((old[a][half] - tops[a][half]) * EXP2_SCALE)
@@ -234,7 +243,7 @@
     return jax.ShapeDtypeStruct(dims, dtype)
 
 
-STEP_FIRST, STEP_LAST, STEP_A, STEP_C = 2, 4, 2, 2
+STEP_FIRST, STEP_LAST, STEP_A, STEP_C = 4, 4, 4, 4
 
 
 def forward_first(h, q, own, windows, token=None):

time: 107 us -> 104 us (0.972)
  Pallas kernels: 34.1 us -> 31.3 us
    pallas_call x4, Pallas kernels: 29.5 us -> 26.7 us  [call(): pl.pallas_call(body, grid_spec=pltpu.PrefetchScalarGridSpec(num_scalar_pr...]
    ppermute x19, waiting for transfers between devices: 14.5 us -> 13.4 us  [swap(): return lax.ppermute(x, 'head', [(i, i ^ k) for i in range(4)])]
  transfers between devices with their start and end apart: 27 -> 27, of which waited for: 10 -> 10; matrix products, arithmetic and copies ran while one was open for 4% -> 4% of each run, Pallas kernels for 30% -> 28%
where the time goes in v2:
time: 104 us
  starting transfers between devices  46.5 us (45%)
  Pallas kernels  31.3 us (30%)
  waiting for transfers between devices  18.9 us (18%)
  local copies, waits for them, and re-layouts  6.04 us (6%)
  between operations  1.23 us (1%)
    ppermute x19, starting transfers between devices, swap(): return lax.ppermute(x, 'head', [(i, i ^ k) for i in range(4)])  30.7 us
    pallas_call x4, Pallas kernels, call(): pl.pallas_call(body, grid_spec=pltpu.PrefetchScalarGridSpec(num_scalar_pr...  26.7 us
    ppermute x8, starting transfers between devices, along(): return lax.ppermute(x, axis, [(i, (i + distance) % n) for i in range(n)])  15.8 us
    ppermute x19, waiting for transfers between devices, swap(): return lax.ppermute(x, 'head', [(i, i ^ k) for i in range(4)])  13.4 us
    ppermute x8, waiting for transfers between devices, along(): return lax.ppermute(x, axis, [(i, (i + distance) % n) for i in range(n)])  5.53 us
    pallas_call x2, Pallas kernels, placed(): pl.pallas_call(functools.partial(place_kernel, len(arrays)), in_specs=[pl...  4.59 us
    dynamic_slice x3, local copies, waits for them, and re-layouts, columns(): return lax.dynamic_slice(x, (0, (h ^ k) * width), (x.shape[0], width))  2.39 us
  transfers between devices with their start and end apart: 27, of which 10 were waited for; matrix products, arithmetic and copies ran while one was open for 4% of the time, Pallas kernels for 28%

profile of v2, /device:TPU:1, one launch (start us, length us, event | category | flops | bytes accessed | tf_op | source)
XLA Modules:
  0.0 104.3 jit_solution(15703026561875044716)
XLA Ops:
  0.7 1.0 %constant_dynamic-slice_fusion.8 = (bf16[128,256]{1,0:T(8,128)(2,1)S(1)}, bf16[128,256]{1,0:T(8,128)(2,1)S(1)}, bf16[528,256]{1,0:T(8,128)(2,1)S(1)}, bf16[128,256]{1,0:T(8,128)(2,1)S(1)}) fusion(bf16[128,1024]{1,0:T(8,128)(2,1)} %param.5, s32[]{:T(128)S(6)} %select_n.39, s32[]{:T(128)S(6)} %select_n.37, s32[]{:T(128)S(6)} %select_n.36, s32[]{:T(128)S(6)} %select_n.38), kind=kLoop, calls=%fused_computation.19 | loop fusion | bytes 524304 | tf_op jit(solution)/shard_map/dynamic_slice | solution.py:460
  1.7 4.2 %collective-permute-start.2 = (bf16[128,256]{1,0:T(8,128)(2,1)S(1)}, bf16[128,256]{1,0:T(8,128)(2,1)S(1)}, u32[]{:S(2)}, u32[]{:S(2)}) collective-permute-start(bf16[128,256]{1,0:T(8,128)(2,1)S(1)} %get-tuple-element.81), channel_id=1, source_target_pairs={{0,192},{64,128},{128,64},{192,0},{1,193},{65,129},{129,65},{193,1... | collective-permute-start | bytes 196616 | tf_op jit(solution)/shard_map/kv_3/ppermute | solution.py:449
  5.9 2.0 %collective-permute-start.1 = (bf16[128,256]{1,0:T(8,128)(2,1)S(1)}, bf16[128,256]{1,0:T(8,128)(2,1)S(1)}, u32[]{:S(2)}, u32[]{:S(2)}) collective-permute-start(bf16[128,256]{1,0:T(8,128)(2,1)S(1)} %get-tuple-element.84), channel_id=1, source_target_pairs={{0,128},{64,192},{128,0},{192,64},{1,129},{65,193},{129,1},{193,65... | collective-permute-start | bytes 196616 | tf_op jit(solution)/shard_map/kv_2/ppermute | solution.py:449
  7.9 1.3 %constant_dynamic-slice_fusion = (bf16[128,1024]{1,0:T(8,128)(2,1)S(1)}, bf16[128,1024]{1,0:T(8,128)(2,1)S(1)}, bf16[128,1024]{1,0:T(8,128)(2,1)S(1)}, bf16[128,1024]{1,0:T(8,128)(2,1)S(1)}) fusion(bf16[128,4096]{1,0:T(8,128)(2,1)} %param.6, s32[]{:T(128)S(6)} %select_n.42, s32[]{:T(128)S(6)} %select_n.43, s32[]{:T(128)S(6)} %select_n.44, s32[]{:T(128)S(6)} %select_n.45), kind=kLoop, calls=%fused_computation.11 | loop fusion | bytes 2097168 | tf_op jit(solution)/shard_map/dynamic_slice | solution.py:460
  9.2 0.9 collective-permute-start.7
  10.3 0.0 collective-permute-done
  10.3 0.3 collective-permute-done.1
  10.6 1.7 %collective-permute-start.10 = (bf16[528,256]{1,0:T(8,128)(2,1)S(1)}, bf16[528,256]{1,0:T(8,128)(2,1)S(1)}, u32[]{:S(2)}, u32[]{:S(2)}) collective-permute-start(bf16[528,256]{1,0:T(8,128)(2,1)S(1)} %constant_dynamic-update-slice_fusion.refs_5_.refs_1_), channel_id=1, source_target_pairs={{0,8},{8,16},{16,24},{24,32},{32,40},{40,48},{48,56},{56,0},{1,9},... | collective-permute-start | bytes 811016 | tf_op jit(solution)/shard_map/w_1/ppermute | solution.py:455
  12.3 0.3 collective-permute-start.3
  12.6 0.1 constant_dynamic-slice_fusion.1
  12.7 3.9 %collective-permute-start.9 = (bf16[128,1024]{1,0:T(8,128)(2,1)S(1)}, bf16[128,1024]{1,0:T(8,128)(2,1)S(1)}, u32[]{:S(2)}, u32[]{:S(2)}) collective-permute-start(bf16[128,1024]{1,0:T(8,128)(2,1)S(1)} %get-tuple-element.69), channel_id=1, source_target_pairs={{0,192},{64,128},{128,64},{192,0},{1,193},{65,129},{129,65},{193,1... | collective-permute-start | bytes 786440 | tf_op jit(solution)/shard_map/query_3/ppermute | solution.py:449
  16.7 1.2 %collective-permute-start.8 = (bf16[128,1024]{1,0:T(8,128)(2,1)S(1)}, bf16[128,1024]{1,0:T(8,128)(2,1)S(1)}, u32[]{:S(2)}, u32[]{:S(2)}) collective-permute-start(bf16[128,1024]{1,0:T(8,128)(2,1)S(1)} %get-tuple-element.72), channel_id=1, source_target_pairs={{0,128},{64,192},{128,0},{192,64},{1,129},{65,193},{129,1},{193,65... | collective-permute-start | bytes 786440 | tf_op jit(solution)/shard_map/query_2/ppermute | solution.py:449
  17.9 3.5 %collective-permute-done.10.refs_7_.refs_3_ = bf16[528,256]{1,0:T(8,128)(2,1)S(1)} collective-permute-done((bf16[528,256]{1,0:T(8,128)(2,1)S(1)}, bf16[528,256]{1,0:T(8,128)(2,1)S(1)}, u32[]{:S(2)}, u32[]{:S(2)}) %collective-permute-start.10) | collective-permute-done | bytes 270368 | tf_op jit(solution)/shard_map/w_1/ppermute | solution.py:455
  21.4 2.3 %collective-permute-start.6 = (bf16[128,1024]{1,0:T(8,128)(2,1)S(1)}, bf16[128,1024]{1,0:T(8,128)(2,1)S(1)}, u32[]{:S(2)}, u32[]{:S(2)}) collective-permute-start(bf16[128,1024]{1,0:T(8,128)(2,1)S(1)} %get-tuple-element.70), channel_id=1, source_target_pairs={{0,64},{64,0},{128,192},{192,128},{1,65},{65,1},{129,193},{193,129... | collective-permute-start | bytes 786440 | tf_op jit(solution)/shard_map/query_1/ppermute | solution.py:449
  23.7 0.0 collective-permute-start.12
  23.8 5.7 %collective-permute-done.9.refs_4_ = bf16[128,1024]{1,0:T(8,128)(2,1)S(1)} collective-permute-done((bf16[128,1024]{1,0:T(8,128)(2,1)S(1)}, bf16[128,1024]{1,0:T(8,128)(2,1)S(1)}, u32[]{:S(2)}, u32[]{:S(2)}) %collective-permute-start.9) | collective-permute-done | bytes 262176 | tf_op jit(solution)/shard_map/query_3/ppermute | solution.py:449
  29.5 1.4 %collective-permute-done.8.refs_3_ = bf16[128,1024]{1,0:T(8,128)(2,1)S(1)} collective-permute-done((bf16[128,1024]{1,0:T(8,128)(2,1)S(1)}, bf16[128,1024]{1,0:T(8,128)(2,1)S(1)}, u32[]{:S(2)}, u32[]{:S(2)}) %collective-permute-start.8) | collective-permute-done | bytes 262176 | tf_op jit(solution)/shard_map/query_2/ppermute | solution.py:449
  30.8 1.3 %collective-permute-start.11 = (bf16[256,1024]{1,0:T(8,128)(2,1)S(1)}, bf16[256,1024]{1,0:T(8,128)(2,1)S(1)}, u32[]{:S(2)}, u32[]{:S(2)}) collective-permute-start(bf16[256,1024]{1,0:T(8,128)(2,1)S(1)} %pad_maximum_fusion.1), channel_id=1, source_target_pairs={{0,128},{64,192},{128,0},{192,64},{1,129},{65,193},{129,1},{193,65... | collective-permute-start | bytes 1572872 | tf_op jit(solution)/shard_map/grad_out_2/ppermute | solution.py:449
  32.2 2.4 %collective-permute-start.4 = (bf16[16,128]{1,0:T(8,128)(2,1)S(1)}, bf16[16,128]{1,0:T(8,128)(2,1)S(1)}, u32[]{:S(2)}, u32[]{:S(2)}) collective-permute-start(bf16[16,128]{1,0:T(8,128)(2,1)S(1)} %slice_add_fusion), channel_id=1, source_target_pairs={{0,64},{64,0},{128,192},{192,128},{1,65},{65,1},{129,193},{193,129... | collective-permute-start | bytes 12296 | tf_op jit(solution)/shard_map/before_token_1/ppermute | solution.py:449
  34.6 0.0 collective-permute-done.12.refs_2_.refs_10_
  34.6 1.7 %collective-permute-start.13 = (bf16[528,256]{1,0:T(8,128)(2,1)S(1)}, bf16[528,256]{1,0:T(8,128)(2,1)S(1)}, u32[]{:S(2)}, u32[]{:S(2)}) collective-permute-start(bf16[528,256]{1,0:T(8,128)(2,1)S(1)} %collective-permute-done.12.refs_2_.refs_10_), channel_id=1, source_target_pairs={{0,8},{8,16},{16,24},{24,32},{32,40},{40,48},{48,56},{56,0},{1,9},... | collective-permute-start | bytes 811016 | tf_op jit(solution)/shard_map/w_3/ppermute | solution.py:455
  36.2 0.0 collective-permute-done.4
  36.2 0.4 collective-permute-start.5
  36.6 0.0 collective-permute-done.6.refs_2_
  36.6 0.8 collective-permute-done.5.refs_0_
  37.4 6.7 %forward_first.1 = (bf16[512,1024]{1,0:T(8,128)(2,1)S(1)}, f32[8,2,144,256]{3,2,1,0:T(8,128)S(1)}, f32[8,2,8,256]{3,2,1,0:T(8,128)S(1)}, bf16[8,3,256,256]{3,2,1...) custom-call(s32[1]{0:T(128)} %bitcast.h_ref, ...), custom_call_target="tpu_custom_call" | custom-call | flops 469762048 | bytes 65536 | tf_op jit(solution)/shard_map/forward_first/pallas_call | solution.py:230
  44.1 1.2 %collective-permute-done.13.refs_3_.refs_9_ = bf16[528,256]{1,0:T(8,128)(2,1)S(1)} collective-permute-done((bf16[528,256]{1,0:T(8,128)(2,1)S(1)}, bf16[528,256]{1,0:T(8,128)(2,1)S(1)}, u32[]{:S(2)}, u32[]{:S(2)}) %collective-permute-start.13) | collective-permute-done | bytes 270368 | tf_op jit(solution)/shard_map/w_3/ppermute | solution.py:455
  45.4 4.5 %forward_last.1 = (bf16[128,1024]{1,0:T(8,128)(2,1)S(1)}, bf16[128,1024]{1,0:T(8,128)(2,1)S(1)}, bf16[256,1024]{1,0:T(8,128)(2,1)S(1)}, f32[8,2,16,256]{3,2,1,0:...) custom-call(s32[1]{0:T(128)} %bitcast.h_ref, ...), custom_call_target="tpu_custom_call" | custom-call | flops 268435456 | bytes 65536 | tf_op jit(solution)/shard_map/forward_last/pallas_call | solution.py:230
  49.9 0.0 copy-start
  49.9 2.2 %collective-permute-start.16 = (bf16[256,1024]{1,0:T(8,128)(2,1)S(1)}, bf16[256,1024]{1,0:T(8,128)(2,1)S(1)}, u32[]{:S(2)}, u32[]{:S(2)}) collective-permute-start(bf16[256,1024]{1,0:T(8,128)(2,1)S(1)} %get-tuple-element.42.refs_7_), channel_id=1, source_target_pairs={{0,128},{64,192},{128,0},{192,64},{1,129},{65,193},{129,1},{193,65... | collective-permute-start | bytes 1572872 | tf_op jit(solution)/shard_map/out_2/ppermute | solution.py:449
  52.1 8.7 %backward_first.1 = (f32[8,2,128,256]{3,2,1,0:T(8,128)S(1)}, bf16[512,2048]{1,0:T(8,128)(2,1)S(1)}, bf16[512,256]{1,0:T(8,128)(2,1)S(1)}, bf16[512,256]{1,0:T(8,128)(2,1)S(1)}, bf16[512,256]{1,0:T(8,128)(2,1)S(1)}) custom-call(s32[1]{0:T(128)} %bitcast.h_ref, bf16[512,1024]{1,0:T(8,128)(2,1)S(1)} %get-tuple-element.36.refs_0_, ...), custom_call_target="tpu_custom_call" | custom-call | flops 805306368 | bytes 65536 | tf_op jit(solution)/shard_map/backward_first/pallas_call | solution.py:230
  60.8 2.3 %collective-permute-start.20 = (bf16[512,256]{1,0:T(8,128)(2,1)S(1)}, bf16[512,256]{1,0:T(8,128)(2,1)S(1)}, u32[]{:S(2)}, u32[]{:S(2)}) collective-permute-start(bf16[512,256]{1,0:T(8,128)(2,1)S(1)} %get-tuple-element.57), channel_id=1, source_target_pairs={{0,56},{8,0},{16,8},{24,16},{32,24},{40,32},{48,40},{56,48},{1,57}... | collective-permute-start | bytes 786440 | tf_op jit(solution)/shard_map/term_3/ppermute | solution.py:455
  63.0 6.7 %backward_last.1 = (bf16[128,1024]{1,0:T(8,128)(2,1)S(1)}, bf16[128,1024]{1,0:T(8,128)(2,1)S(1)}, bf16[256,1024]{1,0:T(8,128)(2,1)S(1)}, bf16[512,256]{1,0:T(8,128)(2,1)S(1)}, bf16[512,256]{1,0:T(8,128)(2,1)S(1)}) custom-call(s32[1]{0:T(128)} %bitcast.h_ref, bf16[512,1024]{1,0:T(8,128)(2,1)S(1)} %get-tuple-element.36.refs_0_, ...), custom_call_target="tpu_custom_call" | custom-call | flops 671088640 | bytes 65536 | tf_op jit(solution)/shard_map/backward_last/pallas_call | solution.py:230
  69.8 1.0 collective-permute-start.14
  70.8 0.1 add_convert_fusion.2
  70.9 1.5 %collective-permute-start.21 = (bf16[512,256]{1,0:T(8,128)(2,1)S(1)}, bf16[512,256]{1,0:T(8,128)(2,1)S(1)}, u32[]{:S(2)}, u32[]{:S(2)}) collective-permute-start(bf16[512,256]{1,0:T(8,128)(2,1)S(1)} %add_convert_fusion.2), channel_id=1, source_target_pairs={{0,56},{8,0},{16,8},{24,16},{32,24},{40,32},{48,40},{56,48},{1,57}... | collective-permute-start | bytes 786440 | tf_op jit(solution)/shard_map/term_2/ppermute | solution.py:455
  72.4 1.4 %collective-permute-start.15 = (bf16[128,1024]{1,0:T(8,128)(2,1)S(1)}, bf16[128,1024]{1,0:T(8,128)(2,1)S(1)}, u32[]{:S(2)}, u32[]{:S(2)}) collective-permute-start(bf16[128,1024]{1,0:T(8,128)(2,1)S(1)} %get-tuple-element.41.refs_6_), channel_id=1, source_target_pairs={{0,64},{64,0},{128,192},{192,128},{1,65},{65,1},{129,193},{193,129... | collective-permute-start | bytes 786440 | tf_op jit(solution)/shard_map/out_1/ppermute | solution.py:449
  73.8 0.0 collective-permute-done.16
  73.8 0.7 fusion.1
  74.5 0.0 collective-permute-start.17
  74.5 6.5 %collective-permute-start.23 = (bf16[512,256]{1,0:T(8,128)(2,1)S(1)}, bf16[512,256]{1,0:T(8,128)(2,1)S(1)}, u32[]{:S(2)}, u32[]{:S(2)}) collective-permute-start(bf16[512,256]{1,0:T(8,128)(2,1)S(1)} %get-tuple-element.62), channel_id=1, source_target_pairs={{0,63},{1,0},{2,1},{3,2},{4,3},{5,4},{6,5},{7,6},{8,7},{9,8},{10,9... | collective-permute-start | bytes 786440 | tf_op jit(solution)/shard_map/term_before/ppermute | solution.py:455
  81.1 0.1 add_convert_fusion.1
  81.1 1.8 %collective-permute-start.22 = (bf16[512,256]{1,0:T(8,128)(2,1)S(1)}, bf16[512,256]{1,0:T(8,128)(2,1)S(1)}, u32[]{:S(2)}, u32[]{:S(2)}) collective-permute-start(bf16[512,256]{1,0:T(8,128)(2,1)S(1)} %add_convert_fusion.1), channel_id=1, source_target_pairs={{0,56},{8,0},{16,8},{24,16},{32,24},{40,32},{48,40},{56,48},{1,57}... | collective-permute-start | bytes 786440 | tf_op jit(solution)/shard_map/term_1/ppermute | solution.py:455
  83.0 0.0 collective-permute-done.15.refs_1_
  83.0 1.1 %collective-permute-start.18 = (bf16[128,1024]{1,0:T(8,128)(2,1)S(1)}, bf16[128,1024]{1,0:T(8,128)(2,1)S(1)}, u32[]{:S(2)}, u32[]{:S(2)}) collective-permute-start(bf16[128,1024]{1,0:T(8,128)(2,1)S(1)} %get-tuple-element.54), channel_id=1, source_target_pairs={{0,64},{64,0},{128,192},{192,128},{1,65},{65,1},{129,193},{193,129... | collective-permute-start | bytes 786440 | tf_op jit(solution)/shard_map/grad_query_1/ppermute | solution.py:449
  84.1 0.0 collective-permute-done.17.refs_3_
  84.1 0.7 copy-done.6
  84.8 2.2 %placed.2 = bf16[128,4096]{1,0:T(8,128)(2,1)} custom-call(s32[1]{0:T(128)} %bitcast.h_ref, bf16[128,1024]{1,0:T(8,128)(2,1)} %copy-done, bf16[128,1024]{1,0:T(8,128)(2,1)} %copy-done.5, bf16[128,1024]{1,0:T(8,128)(2,1)} %get-tuple-element.76.refs_2_, bf16[128,1024]{1,0:T(8,128)(2,1)} %copy-done.6), custom_call_target="tpu_custom_call" | custom-call | bytes 2097152 | tf_op jit(solution)/shard_map/placed/pallas_call | solution.py:421
  87.0 2.1 %collective-permute-done.14 = bf16[256,1024]{1,0:T(8,128)(2,1)S(1)} collective-permute-done((bf16[256,1024]{1,0:T(8,128)(2,1)S(1)}, bf16[256,1024]{1,0:T(8,128)(2,1)S(1)}, u32[]{:S(2)}, u32[]{:S(2)}) %collective-permute-start.14) | collective-permute-done | bytes 524320 | tf_op jit(solution)/shard_map/grad_query_2/ppermute | solution.py:449
  89.1 0.8 fusion
  89.8 2.3 %collective-permute-start.19 = (bf16[128,1024]{1,0:T(8,128)(2,1)S(1)}, bf16[128,1024]{1,0:T(8,128)(2,1)S(1)}, u32[]{:S(2)}, u32[]{:S(2)}) collective-permute-start(bf16[128,1024]{1,0:T(8,128)(2,1)S(1)} %get-tuple-element.73), channel_id=1, source_target_pairs={{0,64},{64,0},{128,192},{192,128},{1,65},{65,1},{129,193},{193,129... | collective-permute-start | bytes 786440 | tf_op jit(solution)/shard_map/grad_query_1/ppermute | solution.py:449
  92.1 0.8 collective-permute-done.22
  92.9 0.1 add_convert_fusion
  93.0 0.6 fusion.2
  93.6 2.3 %collective-permute-start.26 = (bf16[128,256]{1,0:T(8,128)(2,1)S(1)}, bf16[128,256]{1,0:T(8,128)(2,1)S(1)}, u32[]{:S(2)}, u32[]{:S(2)}) collective-permute-start(bf16[128,256]{1,0:T(8,128)(2,1)S(1)} %get-tuple-element.77), channel_id=1, source_target_pairs={{0,192},{64,128},{128,64},{192,0},{1,193},{65,129},{129,65},{193,1... | collective-permute-start | bytes 196616 | tf_op jit(solution)/shard_map/grad_kv_3/ppermute | solution.py:449
  95.9 1.9 %collective-permute-start.25 = (bf16[128,256]{1,0:T(8,128)(2,1)S(1)}, bf16[128,256]{1,0:T(8,128)(2,1)S(1)}, u32[]{:S(2)}, u32[]{:S(2)}) collective-permute-start(bf16[128,256]{1,0:T(8,128)(2,1)S(1)} %get-tuple-element.78), channel_id=1, source_target_pairs={{0,128},{64,192},{128,0},{192,64},{1,129},{65,193},{129,1},{193,65... | collective-permute-start | bytes 196616 | tf_op jit(solution)/shard_map/grad_kv_2/ppermute | solution.py:449
  97.8 0.0 collective-permute-done.18.refs_1_
  97.9 1.4 %collective-permute-done.26.refs_7_ = bf16[128,256]{1,0:T(8,128)(2,1)S(1)} collective-permute-done((bf16[128,256]{1,0:T(8,128)(2,1)S(1)}, bf16[128,256]{1,0:T(8,128)(2,1)S(1)}, u32[]{:S(2)}, u32[]{:S(2)}) %collective-permute-start.26) | collective-permute-done | bytes 65568 | tf_op jit(solution)/shard_map/grad_kv_3/ppermute | solution.py:449
  99.2 1.7 %collective-permute-done.25.refs_6_ = bf16[128,256]{1,0:T(8,128)(2,1)S(1)} collective-permute-done((bf16[128,256]{1,0:T(8,128)(2,1)S(1)}, bf16[128,256]{1,0:T(8,128)(2,1)S(1)}, u32[]{:S(2)}, u32[]{:S(2)}) %collective-permute-start.25) | collective-permute-done | bytes 65568 | tf_op jit(solution)/shard_map/grad_kv_2/ppermute | solution.py:449
  100.9 0.0 collective-permute-done.24.refs_5_
  101.0 0.6 copy-done.8
  101.6 0.1 copy-done.9
  101.6 0.1 copy-done.4
  101.7 2.4 %placed.3 = (bf16[128,4096]{1,0:T(8,128)(2,1)}, f32[128,1024]{1,0:T(8,128)}) custom-call(s32[1]{0:T(128)} %bitcast.h_ref, bf16[128,1024]{1,0:T(8,128)(2,1)} %copy-done.1, bf16[128,1024]{1,0:T(8,128)(2,1)} %copy-done.3, bf16[128,1024]{1,0:T(8,128)(2,1)} %get-tuple-element.74.refs_2_, bf16[128,1024]{1,0:T(8,128)(2,1)} %copy-done.4, ...), custom_call_target="tpu_custom_call" | custom-call | bytes 2097152 | tf_op jit(solution)/shard_map/placed/pallas_call | solution.py:421
  (36 shorter events, 0.2 us)
Async XLA Ops:
  0.6 9.5 %copy-start.10 = (s32[128]{0:T(128)S(1)}, s32[128]{0:T(128)}, u32[]{:S(2)}) copy-start(s32[128]{0:T(128)} %param.7) | copy-start | bytes 1540
  0.6 12.0 %copy-start.2 = (bf16[128,4096]{1,0:T(8,128)(2,1)S(1)}, bf16[128,4096]{1,0:T(8,128)(2,1)}, u32[]{:S(2)}) copy-start(bf16[128,4096]{1,0:T(8,128)(2,1)} %param.4) | copy-start | bytes 3145732
  1.7 8.9 %collective-permute-start.2 = (bf16[128,256]{1,0:T(8,128)(2,1)S(1)}, bf16[128,256]{1,0:T(8,128)(2,1)S(1)}, u32[]{:S(2)}, u32[]{:S(2)}) collective-permute-start(bf16[128,256]{1,0:T(8,128)(2,1)S(1)} %get-tuple-element.81), channel_id=1, source_target_pairs={{0,192},{64,128},{128,64},{192,0},{1,193},{65,129},{129,65},{193,1... | collective-permute-start | bytes 196616 | tf_op jit(solution)/shard_map/kv_3/ppermute | solution.py:449
  5.9 4.3 %collective-permute-start = (bf16[128,256]{1,0:T(8,128)(2,1)S(1)}, bf16[128,256]{1,0:T(8,128)(2,1)S(1)}, u32[]{:S(2)}, u32[]{:S(2)}) collective-permute-start(bf16[128,256]{1,0:T(8,128)(2,1)S(1)} %get-tuple-element.82), channel_id=1, source_target_pairs={{0,64},{64,0},{128,192},{192,128},{1,65},{65,1},{129,193},{193,129... | collective-permute-start | bytes 196616 | tf_op jit(solution)/shard_map/kv_1/ppermute | solution.py:449
  5.9 4.6 %collective-permute-start.1 = (bf16[128,256]{1,0:T(8,128)(2,1)S(1)}, bf16[128,256]{1,0:T(8,128)(2,1)S(1)}, u32[]{:S(2)}, u32[]{:S(2)}) collective-permute-start(bf16[128,256]{1,0:T(8,128)(2,1)S(1)} %get-tuple-element.84), channel_id=1, source_target_pairs={{0,128},{64,192},{128,0},{192,64},{1,129},{65,193},{129,1},{193,65... | collective-permute-start | bytes 196616 | tf_op jit(solution)/shard_map/kv_2/ppermute | solution.py:449
  9.2 14.5 %collective-permute-start.7 = (bf16[256,1024]{1,0:T(8,128)(2,1)S(1)}, bf16[256,1024]{1,0:T(8,128)(2,1)S(1)}, u32[]{:S(2)}, u32[]{:S(2)}) collective-permute-start(bf16[256,1024]{1,0:T(8,128)(2,1)S(1)} %pad_maximum_fusion), channel_id=1, source_target_pairs={{0,64},{64,0},{128,192},{192,128},{1,65},{65,1},{129,193},{193,129... | collective-permute-start | bytes 1572872 | tf_op jit(solution)/shard_map/grad_out_1/ppermute | solution.py:449
  10.6 10.8 %collective-permute-start.10 = (bf16[528,256]{1,0:T(8,128)(2,1)S(1)}, bf16[528,256]{1,0:T(8,128)(2,1)S(1)}, u32[]{:S(2)}, u32[]{:S(2)}) collective-permute-start(bf16[528,256]{1,0:T(8,128)(2,1)S(1)} %constant_dynamic-update-slice_fusion.refs_5_.refs_1_), channel_id=1, source_target_pairs={{0,8},{8,16},{16,24},{24,32},{32,40},{40,48},{48,56},{56,0},{1,9},... | collective-permute-start | bytes 811016 | tf_op jit(solution)/shard_map/w_1/ppermute | solution.py:455
  12.3 19.9 %collective-permute-start.3 = (bf16[528,256]{1,0:T(8,128)(2,1)S(1)}, bf16[528,256]{1,0:T(8,128)(2,1)S(1)}, u32[]{:S(2)}, u32[]{:S(2)}) collective-permute-start(bf16[528,256]{1,0:T(8,128)(2,1)S(1)} %constant_dynamic-update-slice_fusion.refs_5_.refs_1_), channel_id=1, source_target_pairs={{0,1},{1,2},{2,3},{3,4},{4,5},{5,6},{6,7},{7,8},{8,9},{9,10},{10,1... | collective-permute-start | bytes 811016 | tf_op jit(solution)/shard_map/before/ppermute | solution.py:455
  12.7 16.8 %collective-permute-start.9 = (bf16[128,1024]{1,0:T(8,128)(2,1)S(1)}, bf16[128,1024]{1,0:T(8,128)(2,1)S(1)}, u32[]{:S(2)}, u32[]{:S(2)}) collective-permute-start(bf16[128,1024]{1,0:T(8,128)(2,1)S(1)} %get-tuple-element.69), channel_id=1, source_target_pairs={{0,192},{64,128},{128,64},{192,0},{1,193},{65,129},{129,65},{193,1... | collective-permute-start | bytes 786440 | tf_op jit(solution)/shard_map/query_3/ppermute | solution.py:449
  16.7 14.2 %collective-permute-start.8 = (bf16[128,1024]{1,0:T(8,128)(2,1)S(1)}, bf16[128,1024]{1,0:T(8,128)(2,1)S(1)}, u32[]{:S(2)}, u32[]{:S(2)}) collective-permute-start(bf16[128,1024]{1,0:T(8,128)(2,1)S(1)} %get-tuple-element.72), channel_id=1, source_target_pairs={{0,128},{64,192},{128,0},{192,64},{1,129},{65,193},{129,1},{193,65... | collective-permute-start | bytes 786440 | tf_op jit(solution)/shard_map/query_2/ppermute | solution.py:449
  21.4 15.2 %collective-permute-start.6 = (bf16[128,1024]{1,0:T(8,128)(2,1)S(1)}, bf16[128,1024]{1,0:T(8,128)(2,1)S(1)}, u32[]{:S(2)}, u32[]{:S(2)}) collective-permute-start(bf16[128,1024]{1,0:T(8,128)(2,1)S(1)} %get-tuple-element.70), channel_id=1, source_target_pairs={{0,64},{64,0},{128,192},{192,128},{1,65},{65,1},{129,193},{193,129... | collective-permute-start | bytes 786440 | tf_op jit(solution)/shard_map/query_1/ppermute | solution.py:449
  23.7 10.9 %collective-permute-start.12 = (bf16[528,256]{1,0:T(8,128)(2,1)S(1)}, bf16[528,256]{1,0:T(8,128)(2,1)S(1)}, u32[]{:S(2)}, u32[]{:S(2)}) collective-permute-start(bf16[528,256]{1,0:T(8,128)(2,1)S(1)} %collective-permute-done.10.refs_7_.refs_3_), channel_id=1, source_target_pairs={{0,8},{8,16},{16,24},{24,32},{32,40},{40,48},{48,56},{56,0},{1,9},... | collective-permute-start | bytes 811016 | tf_op jit(solution)/shard_map/w_2/ppermute | solution.py:455
  30.8 21.2 %collective-permute-start.11 = (bf16[256,1024]{1,0:T(8,128)(2,1)S(1)}, bf16[256,1024]{1,0:T(8,128)(2,1)S(1)}, u32[]{:S(2)}, u32[]{:S(2)}) collective-permute-start(bf16[256,1024]{1,0:T(8,128)(2,1)S(1)} %pad_maximum_fusion.1), channel_id=1, source_target_pairs={{0,128},{64,192},{128,0},{192,64},{1,129},{65,193},{129,1},{193,65... | collective-permute-start | bytes 1572872 | tf_op jit(solution)/shard_map/grad_out_2/ppermute | solution.py:449
  32.2 4.0 %collective-permute-start.4 = (bf16[16,128]{1,0:T(8,128)(2,1)S(1)}, bf16[16,128]{1,0:T(8,128)(2,1)S(1)}, u32[]{:S(2)}, u32[]{:S(2)}) collective-permute-start(bf16[16,128]{1,0:T(8,128)(2,1)S(1)} %slice_add_fusion), channel_id=1, source_target_pairs={{0,64},{64,0},{128,192},{192,128},{1,65},{65,1},{129,193},{193,129... | collective-permute-start | bytes 12296 | tf_op jit(solution)/shard_map/before_token_1/ppermute | solution.py:449
  34.6 10.8 %collective-permute-start.13 = (bf16[528,256]{1,0:T(8,128)(2,1)S(1)}, bf16[528,256]{1,0:T(8,128)(2,1)S(1)}, u32[]{:S(2)}, u32[]{:S(2)}) collective-permute-start(bf16[528,256]{1,0:T(8,128)(2,1)S(1)} %collective-permute-done.12.refs_2_.refs_10_), channel_id=1, source_target_pairs={{0,8},{8,16},{16,24},{24,32},{32,40},{40,48},{48,56},{56,0},{1,9},... | collective-permute-start | bytes 811016 | tf_op jit(solution)/shard_map/w_3/ppermute | solution.py:455
  36.2 1.2 %collective-permute-start.5 = (bf16[16,128]{1,0:T(8,128)(2,1)S(1)}, bf16[16,128]{1,0:T(8,128)(2,1)S(1)}, u32[]{:S(2)}, u32[]{:S(2)}) collective-permute-start(bf16[16,128]{1,0:T(8,128)(2,1)S(1)} %broadcast_add_fusion), channel_id=1, source_target_pairs={{0,64},{64,0},{128,192},{192,128},{1,65},{65,1},{129,193},{193,129... | collective-permute-start | bytes 12296 | tf_op jit(solution)/shard_map/before_token_1/ppermute | solution.py:449
  49.9 10.9 %copy-start = (bf16[128,1024]{1,0:T(8,128)(2,1)}, bf16[128,1024]{1,0:T(8,128)(2,1)S(1)}, u32[]{:S(2)}) copy-start(bf16[128,1024]{1,0:T(8,128)(2,1)S(1)} %get-tuple-element.40.refs_5_.refs_0_) | copy-start | bytes 786436
  49.9 23.9 %collective-permute-start.16 = (bf16[256,1024]{1,0:T(8,128)(2,1)S(1)}, bf16[256,1024]{1,0:T(8,128)(2,1)S(1)}, u32[]{:S(2)}, u32[]{:S(2)}) collective-permute-start(bf16[256,1024]{1,0:T(8,128)(2,1)S(1)} %get-tuple-element.42.refs_7_), channel_id=1, source_target_pairs={{0,128},{64,192},{128,0},{192,64},{1,129},{65,193},{129,1},{193,65... | collective-permute-start | bytes 1572872 | tf_op jit(solution)/shard_map/out_2/ppermute | solution.py:449
  60.8 10.0 %collective-permute-start.20 = (bf16[512,256]{1,0:T(8,128)(2,1)S(1)}, bf16[512,256]{1,0:T(8,128)(2,1)S(1)}, u32[]{:S(2)}, u32[]{:S(2)}) collective-permute-start(bf16[512,256]{1,0:T(8,128)(2,1)S(1)} %get-tuple-element.57), channel_id=1, source_target_pairs={{0,56},{8,0},{16,8},{24,16},{32,24},{40,32},{48,40},{56,48},{1,57}... | collective-permute-start | bytes 786440 | tf_op jit(solution)/shard_map/term_3/ppermute | solution.py:455
  69.8 4.0 %copy-start.1 = (bf16[128,1024]{1,0:T(8,128)(2,1)}, bf16[128,1024]{1,0:T(8,128)(2,1)S(1)}, u32[]{:S(2)}) copy-start(bf16[128,1024]{1,0:T(8,128)(2,1)S(1)} %get-tuple-element.53.refs_0_) | copy-start | bytes 786436
  69.8 19.3 %collective-permute-start.14 = (bf16[256,1024]{1,0:T(8,128)(2,1)S(1)}, bf16[256,1024]{1,0:T(8,128)(2,1)S(1)}, u32[]{:S(2)}, u32[]{:S(2)}) collective-permute-start(bf16[256,1024]{1,0:T(8,128)(2,1)S(1)} %get-tuple-element.51), channel_id=1, source_target_pairs={{0,128},{64,192},{128,0},{192,64},{1,129},{65,193},{129,1},{193,65... | collective-permute-start | bytes 1572872 | tf_op jit(solution)/shard_map/grad_query_2/ppermute | solution.py:449
  70.9 10.2 %collective-permute-start.21 = (bf16[512,256]{1,0:T(8,128)(2,1)S(1)}, bf16[512,256]{1,0:T(8,128)(2,1)S(1)}, u32[]{:S(2)}, u32[]{:S(2)}) collective-permute-start(bf16[512,256]{1,0:T(8,128)(2,1)S(1)} %add_convert_fusion.2), channel_id=1, source_target_pairs={{0,56},{8,0},{16,8},{24,16},{32,24},{40,32},{48,40},{56,48},{1,57}... | collective-permute-start | bytes 786440 | tf_op jit(solution)/shard_map/term_2/ppermute | solution.py:455
  72.4 10.6 %collective-permute-start.15 = (bf16[128,1024]{1,0:T(8,128)(2,1)S(1)}, bf16[128,1024]{1,0:T(8,128)(2,1)S(1)}, u32[]{:S(2)}, u32[]{:S(2)}) collective-permute-start(bf16[128,1024]{1,0:T(8,128)(2,1)S(1)} %get-tuple-element.41.refs_6_), channel_id=1, source_target_pairs={{0,64},{64,0},{128,192},{192,128},{1,65},{65,1},{129,193},{193,129... | collective-permute-start | bytes 786440 | tf_op jit(solution)/shard_map/out_1/ppermute | solution.py:449
  74.5 9.5 %collective-permute-start.17 = (bf16[128,1024]{1,0:T(8,128)(2,1)S(1)}, bf16[128,1024]{1,0:T(8,128)(2,1)S(1)}, u32[]{:S(2)}, u32[]{:S(2)}) collective-permute-start(bf16[128,1024]{1,0:T(8,128)(2,1)S(1)} %get-tuple-element.75), channel_id=1, source_target_pairs={{0,64},{64,0},{128,192},{192,128},{1,65},{65,1},{129,193},{193,129... | collective-permute-start | bytes 786440 | tf_op jit(solution)/shard_map/out_1/ppermute | solution.py:449
  74.5 17.6 %collective-permute-start.23 = (bf16[512,256]{1,0:T(8,128)(2,1)S(1)}, bf16[512,256]{1,0:T(8,128)(2,1)S(1)}, u32[]{:S(2)}, u32[]{:S(2)}) collective-permute-start(bf16[512,256]{1,0:T(8,128)(2,1)S(1)} %get-tuple-element.62), channel_id=1, source_target_pairs={{0,63},{1,0},{2,1},{3,2},{4,3},{5,4},{6,5},{7,6},{8,7},{9,8},{10,9... | collective-permute-start | bytes 786440 | tf_op jit(solution)/shard_map/term_before/ppermute | solution.py:455
  81.1 11.7 %collective-permute-start.22 = (bf16[512,256]{1,0:T(8,128)(2,1)S(1)}, bf16[512,256]{1,0:T(8,128)(2,1)S(1)}, u32[]{:S(2)}, u32[]{:S(2)}) collective-permute-start(bf16[512,256]{1,0:T(8,128)(2,1)S(1)} %add_convert_fusion.1), channel_id=1, source_target_pairs={{0,56},{8,0},{16,8},{24,16},{32,24},{40,32},{48,40},{56,48},{1,57}... | collective-permute-start | bytes 786440 | tf_op jit(solution)/shard_map/term_1/ppermute | solution.py:455
  83.0 1.1 %copy-start.5 = (bf16[128,1024]{1,0:T(8,128)(2,1)}, bf16[128,1024]{1,0:T(8,128)(2,1)S(1)}, u32[]{:S(2)}) copy-start(bf16[128,1024]{1,0:T(8,128)(2,1)S(1)} %collective-permute-done.15.refs_1_) | copy-start | bytes 786436
  83.0 14.9 %collective-permute-start.18 = (bf16[128,1024]{1,0:T(8,128)(2,1)S(1)}, bf16[128,1024]{1,0:T(8,128)(2,1)S(1)}, u32[]{:S(2)}, u32[]{:S(2)}) collective-permute-start(bf16[128,1024]{1,0:T(8,128)(2,1)S(1)} %get-tuple-element.54), channel_id=1, source_target_pairs={{0,64},{64,0},{128,192},{192,128},{1,65},{65,1},{129,193},{193,129... | collective-permute-start | bytes 786440 | tf_op jit(solution)/shard_map/grad_query_1/ppermute | solution.py:449
  84.1 0.7 copy-start.6
  89.8 11.1 %collective-permute-start.19 = (bf16[128,1024]{1,0:T(8,128)(2,1)S(1)}, bf16[128,1024]{1,0:T(8,128)(2,1)S(1)}, u32[]{:S(2)}, u32[]{:S(2)}) collective-permute-start(bf16[128,1024]{1,0:T(8,128)(2,1)S(1)} %get-tuple-element.73), channel_id=1, source_target_pairs={{0,64},{64,0},{128,192},{192,128},{1,65},{65,1},{129,193},{193,129... | collective-permute-start | bytes 786440 | tf_op jit(solution)/shard_map/grad_query_1/ppermute | solution.py:449
  93.6 5.6 %collective-permute-start.26 = (bf16[128,256]{1,0:T(8,128)(2,1)S(1)}, bf16[128,256]{1,0:T(8,128)(2,1)S(1)}, u32[]{:S(2)}, u32[]{:S(2)}) collective-permute-start(bf16[128,256]{1,0:T(8,128)(2,1)S(1)} %get-tuple-element.77), channel_id=1, source_target_pairs={{0,192},{64,128},{128,64},{192,0},{1,193},{65,129},{129,65},{193,1... | collective-permute-start | bytes 196616 | tf_op jit(solution)/shard_map/grad_kv_3/ppermute | solution.py:449
  95.9 5.0 %collective-permute-start.25 = (bf16[128,256]{1,0:T(8,128)(2,1)S(1)}, bf16[128,256]{1,0:T(8,128)(2,1)S(1)}, u32[]{:S(2)}, u32[]{:S(2)}) collective-permute-start(bf16[128,256]{1,0:T(8,128)(2,1)S(1)} %get-tuple-element.78), channel_id=1, source_target_pairs={{0,128},{64,192},{128,0},{192,64},{1,129},{65,193},{129,1},{193,65... | collective-permute-start | bytes 196616 | tf_op jit(solution)/shard_map/grad_kv_2/ppermute | solution.py:449
  97.8 3.1 %collective-permute-start.24 = (bf16[128,256]{1,0:T(8,128)(2,1)S(1)}, bf16[128,256]{1,0:T(8,128)(2,1)S(1)}, u32[]{:S(2)}, u32[]{:S(2)}) collective-permute-start(bf16[128,256]{1,0:T(8,128)(2,1)S(1)} %get-tuple-element.79), channel_id=1, source_target_pairs={{0,64},{64,0},{128,192},{192,128},{1,65},{65,1},{129,193},{193,129... | collective-permute-start | bytes 196616 | tf_op jit(solution)/shard_map/grad_kv_1/ppermute | solution.py:449
  97.9 3.1 %copy-start.3 = (bf16[128,1024]{1,0:T(8,128)(2,1)}, bf16[128,1024]{1,0:T(8,128)(2,1)S(1)}, u32[]{:S(2)}) copy-start(bf16[128,1024]{1,0:T(8,128)(2,1)S(1)} %collective-permute-done.18.refs_1_) | copy-start | bytes 786436
  99.2 1.8 %copy-start.7 = (bf16[128,256]{1,0:T(8,128)(2,1)}, bf16[128,256]{1,0:T(8,128)(2,1)S(1)}, u32[]{:S(2)}) copy-start(bf16[128,256]{1,0:T(8,128)(2,1)S(1)} %collective-permute-done.26.refs_7_) | copy-start | bytes 196612
  100.9 0.6 copy-start.8
  100.9 0.7 copy-start.9
  101.0 0.7 copy-start.4

commit v3 on v2

--- a/solution.py
+++ b/solution.py
@@ -392,6 +392,9 @@
         int(heads * n * 2 * HALF * HALF * D))
 
 
+PARTS = 4
+
+
 def place_kernel(n, h_ref, *refs):
     pieces, outs, held, sems = refs[: 4 * n], refs[4 * n : 5 * n], refs[5 * n : -1], refs[-1]
     copies = []
@@ -403,9 +406,13 @@
                 held[0][k] = piece[...].astype(out.dtype)
                 piece = held[0].at[k]
             column = pl.multiple_of((h_ref[0] ^ k) * width, width)
-            copy = pltpu.make_async_copy(piece, out.at[:, pl.ds(column, width)], sems.at[4 * i + k])
-            copy.start()
-            copies.append(copy)
+            for part in range(PARTS):
+                rows = pl.ds(part * (PIECE // PARTS), PIECE // PARTS)
+                copy = pltpu.make_async_copy(
+                    piece.at[rows], out.at[rows, pl.ds(column, width)],
+                    sems.at[(4 * i + k) * PARTS + part])
+                copy.start()
+                copies.append(copy)
     for copy in copies:
         copy.wait()
 
@@ -424,7 +431,7 @@
         + [pl.BlockSpec(memory_space=pltpu.VMEM)] * len(ins),
         out_specs=[pl.BlockSpec(memory_space=pl.ANY)] * len(outs),
         out_shape=outs,
-        scratch_shapes=held + [pltpu.SemaphoreType.DMA((len(ins),))],
+        scratch_shapes=held + [pltpu.SemaphoreType.DMA((len(ins) * PARTS,))],
         cost_estimate=pl.CostEstimate(flops=0, bytes_accessed=2**21, transcendentals=0),
         name="placed",
     )(h, *ins)

time: 104 us -> 105 us (level)
  no operation moved by 1% of the time
where the time goes in v3:
time: 105 us; the launch traced here: 104 us
  starting transfers between devices  46.5 us (44%)
  Pallas kernels  31.5 us (30%)
  waiting for transfers between devices  18.8 us (18%)
  local copies, waits for them, and re-layouts  6.04 us (6%)
  between operations  1.23 us (1%)
    ppermute x19, starting transfers between devices, swap(): return lax.ppermute(x, 'head', [(i, i ^ k) for i in range(4)])  30.7 us
    pallas_call x4, Pallas kernels, call(): pl.pallas_call(body, grid_spec=pltpu.PrefetchScalarGridSpec(num_scalar_pr...  26.7 us
    ppermute x8, starting transfers between devices, along(): return lax.ppermute(x, axis, [(i, (i + distance) % n) for i in range(n)])  15.8 us
    ppermute x19, waiting for transfers between devices, swap(): return lax.ppermute(x, 'head', [(i, i ^ k) for i in range(4)])  13.3 us
    ppermute x8, waiting for transfers between devices, along(): return lax.ppermute(x, axis, [(i, (i + distance) % n) for i in range(n)])  5.53 us
    pallas_call x2, Pallas kernels, placed(): pl.pallas_call(functools.partial(place_kernel, len(arrays)), in_specs=[pl...  4.88 us
    dynamic_slice x3, local copies, waits for them, and re-layouts, columns(): return lax.dynamic_slice(x, (0, (h ^ k) * width), (x.shape[0], width))  2.39 us
  transfers between devices with their start and end apart: 27, of which 10 were waited for; matrix products, arithmetic and copies ran while one was open for 4% of the time, Pallas kernels for 28%

profile of v3, /device:TPU:1, one launch (start us, length us, event | category | flops | bytes accessed | tf_op | source)
XLA Modules:
  0.0 104.5 jit_solution(10116301318483584511)
XLA Ops:
  0.7 1.0 %constant_dynamic-slice_fusion.8 = (bf16[128,256]{1,0:T(8,128)(2,1)S(1)}, bf16[128,256]{1,0:T(8,128)(2,1)S(1)}, bf16[528,256]{1,0:T(8,128)(2,1)S(1)}, bf16[128,256]{1,0:T(8,128)(2,1)S(1)}) fusion(bf16[128,1024]{1,0:T(8,128)(2,1)} %param.5, s32[]{:T(128)S(6)} %select_n.39, s32[]{:T(128)S(6)} %select_n.37, s32[]{:T(128)S(6)} %select_n.36, s32[]{:T(128)S(6)} %select_n.38), kind=kLoop, calls=%fused_computation.19 | loop fusion | bytes 524304 | tf_op jit(solution)/shard_map/dynamic_slice | solution.py:467
  1.7 4.2 %collective-permute-start.2 = (bf16[128,256]{1,0:T(8,128)(2,1)S(1)}, bf16[128,256]{1,0:T(8,128)(2,1)S(1)}, u32[]{:S(2)}, u32[]{:S(2)}) collective-permute-start(bf16[128,256]{1,0:T(8,128)(2,1)S(1)} %get-tuple-element.81), channel_id=1, source_target_pairs={{0,192},{64,128},{128,64},{192,0},{1,193},{65,129},{129,65},{193,1... | collective-permute-start | bytes 196616 | tf_op jit(solution)/shard_map/kv_3/ppermute | solution.py:456
  5.9 2.0 %collective-permute-start.1 = (bf16[128,256]{1,0:T(8,128)(2,1)S(1)}, bf16[128,256]{1,0:T(8,128)(2,1)S(1)}, u32[]{:S(2)}, u32[]{:S(2)}) collective-permute-start(bf16[128,256]{1,0:T(8,128)(2,1)S(1)} %get-tuple-element.84), channel_id=1, source_target_pairs={{0,128},{64,192},{128,0},{192,64},{1,129},{65,193},{129,1},{193,65... | collective-permute-start | bytes 196616 | tf_op jit(solution)/shard_map/kv_2/ppermute | solution.py:456
  7.9 1.3 %constant_dynamic-slice_fusion = (bf16[128,1024]{1,0:T(8,128)(2,1)S(1)}, bf16[128,1024]{1,0:T(8,128)(2,1)S(1)}, bf16[128,1024]{1,0:T(8,128)(2,1)S(1)}, bf16[128,1024]{1,0:T(8,128)(2,1)S(1)}) fusion(bf16[128,4096]{1,0:T(8,128)(2,1)} %param.6, s32[]{:T(128)S(6)} %select_n.42, s32[]{:T(128)S(6)} %select_n.43, s32[]{:T(128)S(6)} %select_n.44, s32[]{:T(128)S(6)} %select_n.45), kind=kLoop, calls=%fused_computation.11 | loop fusion | bytes 2097168 | tf_op jit(solution)/shard_map/dynamic_slice | solution.py:467
  9.2 0.9 collective-permute-start.7
  10.3 0.0 collective-permute-done
  10.3 0.3 collective-permute-done.1
  10.6 1.7 %collective-permute-start.10 = (bf16[528,256]{1,0:T(8,128)(2,1)S(1)}, bf16[528,256]{1,0:T(8,128)(2,1)S(1)}, u32[]{:S(2)}, u32[]{:S(2)}) collective-permute-start(bf16[528,256]{1,0:T(8,128)(2,1)S(1)} %constant_dynamic-update-slice_fusion.refs_5_.refs_1_), channel_id=1, source_target_pairs={{0,8},{8,16},{16,24},{24,32},{32,40},{40,48},{48,56},{56,0},{1,9},... | collective-permute-start | bytes 811016 | tf_op jit(solution)/shard_map/w_1/ppermute | solution.py:462
  12.3 0.3 collective-permute-start.3
  12.6 0.1 constant_dynamic-slice_fusion.1
  12.7 3.9 %collective-permute-start.9 = (bf16[128,1024]{1,0:T(8,128)(2,1)S(1)}, bf16[128,1024]{1,0:T(8,128)(2,1)S(1)}, u32[]{:S(2)}, u32[]{:S(2)}) collective-permute-start(bf16[128,1024]{1,0:T(8,128)(2,1)S(1)} %get-tuple-element.69), channel_id=1, source_target_pairs={{0,192},{64,128},{128,64},{192,0},{1,193},{65,129},{129,65},{193,1... | collective-permute-start | bytes 786440 | tf_op jit(solution)/shard_map/query_3/ppermute | solution.py:456
  16.7 1.2 %collective-permute-start.8 = (bf16[128,1024]{1,0:T(8,128)(2,1)S(1)}, bf16[128,1024]{1,0:T(8,128)(2,1)S(1)}, u32[]{:S(2)}, u32[]{:S(2)}) collective-permute-start(bf16[128,1024]{1,0:T(8,128)(2,1)S(1)} %get-tuple-element.72), channel_id=1, source_target_pairs={{0,128},{64,192},{128,0},{192,64},{1,129},{65,193},{129,1},{193,65... | collective-permute-start | bytes 786440 | tf_op jit(solution)/shard_map/query_2/ppermute | solution.py:456
  17.9 3.5 %collective-permute-done.10.refs_7_.refs_3_ = bf16[528,256]{1,0:T(8,128)(2,1)S(1)} collective-permute-done((bf16[528,256]{1,0:T(8,128)(2,1)S(1)}, bf16[528,256]{1,0:T(8,128)(2,1)S(1)}, u32[]{:S(2)}, u32[]{:S(2)}) %collective-permute-start.10) | collective-permute-done | bytes 270368 | tf_op jit(solution)/shard_map/w_1/ppermute | solution.py:462
  21.4 2.3 %collective-permute-start.6 = (bf16[128,1024]{1,0:T(8,128)(2,1)S(1)}, bf16[128,1024]{1,0:T(8,128)(2,1)S(1)}, u32[]{:S(2)}, u32[]{:S(2)}) collective-permute-start(bf16[128,1024]{1,0:T(8,128)(2,1)S(1)} %get-tuple-element.70), channel_id=1, source_target_pairs={{0,64},{64,0},{128,192},{192,128},{1,65},{65,1},{129,193},{193,129... | collective-permute-start | bytes 786440 | tf_op jit(solution)/shard_map/query_1/ppermute | solution.py:456
  23.7 0.0 collective-permute-start.12
  23.8 5.7 %collective-permute-done.9.refs_4_ = bf16[128,1024]{1,0:T(8,128)(2,1)S(1)} collective-permute-done((bf16[128,1024]{1,0:T(8,128)(2,1)S(1)}, bf16[128,1024]{1,0:T(8,128)(2,1)S(1)}, u32[]{:S(2)}, u32[]{:S(2)}) %collective-permute-start.9) | collective-permute-done | bytes 262176 | tf_op jit(solution)/shard_map/query_3/ppermute | solution.py:456
  29.5 1.4 %collective-permute-done.8.refs_3_ = bf16[128,1024]{1,0:T(8,128)(2,1)S(1)} collective-permute-done((bf16[128,1024]{1,0:T(8,128)(2,1)S(1)}, bf16[128,1024]{1,0:T(8,128)(2,1)S(1)}, u32[]{:S(2)}, u32[]{:S(2)}) %collective-permute-start.8) | collective-permute-done | bytes 262176 | tf_op jit(solution)/shard_map/query_2/ppermute | solution.py:456
  30.8 1.3 %collective-permute-start.11 = (bf16[256,1024]{1,0:T(8,128)(2,1)S(1)}, bf16[256,1024]{1,0:T(8,128)(2,1)S(1)}, u32[]{:S(2)}, u32[]{:S(2)}) collective-permute-start(bf16[256,1024]{1,0:T(8,128)(2,1)S(1)} %pad_maximum_fusion.1), channel_id=1, source_target_pairs={{0,128},{64,192},{128,0},{192,64},{1,129},{65,193},{129,1},{193,65... | collective-permute-start | bytes 1572872 | tf_op jit(solution)/shard_map/grad_out_2/ppermute | solution.py:456
  32.2 2.4 %collective-permute-start.4 = (bf16[16,128]{1,0:T(8,128)(2,1)S(1)}, bf16[16,128]{1,0:T(8,128)(2,1)S(1)}, u32[]{:S(2)}, u32[]{:S(2)}) collective-permute-start(bf16[16,128]{1,0:T(8,128)(2,1)S(1)} %slice_add_fusion), channel_id=1, source_target_pairs={{0,64},{64,0},{128,192},{192,128},{1,65},{65,1},{129,193},{193,129... | collective-permute-start | bytes 12296 | tf_op jit(solution)/shard_map/before_token_1/ppermute | solution.py:456
  34.6 0.0 collective-permute-done.12.refs_2_.refs_10_
  34.6 1.7 %collective-permute-start.13 = (bf16[528,256]{1,0:T(8,128)(2,1)S(1)}, bf16[528,256]{1,0:T(8,128)(2,1)S(1)}, u32[]{:S(2)}, u32[]{:S(2)}) collective-permute-start(bf16[528,256]{1,0:T(8,128)(2,1)S(1)} %collective-permute-done.12.refs_2_.refs_10_), channel_id=1, source_target_pairs={{0,8},{8,16},{16,24},{24,32},{32,40},{40,48},{48,56},{56,0},{1,9},... | collective-permute-start | bytes 811016 | tf_op jit(solution)/shard_map/w_3/ppermute | solution.py:462
  36.2 0.0 collective-permute-done.4
  36.2 0.4 collective-permute-start.5
  36.6 0.0 collective-permute-done.6.refs_2_
  36.6 0.8 collective-permute-done.5.refs_0_
  37.4 6.7 %forward_first.1 = (bf16[512,1024]{1,0:T(8,128)(2,1)S(1)}, f32[8,2,144,256]{3,2,1,0:T(8,128)S(1)}, f32[8,2,8,256]{3,2,1,0:T(8,128)S(1)}, bf16[8,3,256,256]{3,2,1...) custom-call(s32[1]{0:T(128)} %bitcast.h_ref, ...), custom_call_target="tpu_custom_call" | custom-call | flops 469762048 | bytes 65536 | tf_op jit(solution)/shard_map/forward_first/pallas_call | solution.py:230
  44.1 1.2 %collective-permute-done.13.refs_3_.refs_9_ = bf16[528,256]{1,0:T(8,128)(2,1)S(1)} collective-permute-done((bf16[528,256]{1,0:T(8,128)(2,1)S(1)}, bf16[528,256]{1,0:T(8,128)(2,1)S(1)}, u32[]{:S(2)}, u32[]{:S(2)}) %collective-permute-start.13) | collective-permute-done | bytes 270368 | tf_op jit(solution)/shard_map/w_3/ppermute | solution.py:462
  45.4 4.5 %forward_last.1 = (bf16[128,1024]{1,0:T(8,128)(2,1)S(1)}, bf16[128,1024]{1,0:T(8,128)(2,1)S(1)}, bf16[256,1024]{1,0:T(8,128)(2,1)S(1)}, f32[8,2,16,256]{3,2,1,0:...) custom-call(s32[1]{0:T(128)} %bitcast.h_ref, ...), custom_call_target="tpu_custom_call" | custom-call | flops 268435456 | bytes 65536 | tf_op jit(solution)/shard_map/forward_last/pallas_call | solution.py:230
  49.9 0.0 copy-start
  49.9 2.2 %collective-permute-start.16 = (bf16[256,1024]{1,0:T(8,128)(2,1)S(1)}, bf16[256,1024]{1,0:T(8,128)(2,1)S(1)}, u32[]{:S(2)}, u32[]{:S(2)}) collective-permute-start(bf16[256,1024]{1,0:T(8,128)(2,1)S(1)} %get-tuple-element.42.refs_7_), channel_id=1, source_target_pairs={{0,128},{64,192},{128,0},{192,64},{1,129},{65,193},{129,1},{193,65... | collective-permute-start | bytes 1572872 | tf_op jit(solution)/shard_map/out_2/ppermute | solution.py:456
  52.1 8.7 %backward_first.1 = (f32[8,2,128,256]{3,2,1,0:T(8,128)S(1)}, bf16[512,2048]{1,0:T(8,128)(2,1)S(1)}, bf16[512,256]{1,0:T(8,128)(2,1)S(1)}, bf16[512,256]{1,0:T(8,128)(2,1)S(1)}, bf16[512,256]{1,0:T(8,128)(2,1)S(1)}) custom-call(s32[1]{0:T(128)} %bitcast.h_ref, bf16[512,1024]{1,0:T(8,128)(2,1)S(1)} %get-tuple-element.36.refs_0_, ...), custom_call_target="tpu_custom_call" | custom-call | flops 805306368 | bytes 65536 | tf_op jit(solution)/shard_map/backward_first/pallas_call | solution.py:230
  60.8 2.3 %collective-permute-start.20 = (bf16[512,256]{1,0:T(8,128)(2,1)S(1)}, bf16[512,256]{1,0:T(8,128)(2,1)S(1)}, u32[]{:S(2)}, u32[]{:S(2)}) collective-permute-start(bf16[512,256]{1,0:T(8,128)(2,1)S(1)} %get-tuple-element.57), channel_id=1, source_target_pairs={{0,56},{8,0},{16,8},{24,16},{32,24},{40,32},{48,40},{56,48},{1,57}... | collective-permute-start | bytes 786440 | tf_op jit(solution)/shard_map/term_3/ppermute | solution.py:462
  63.0 6.7 %backward_last.1 = (bf16[128,1024]{1,0:T(8,128)(2,1)S(1)}, bf16[128,1024]{1,0:T(8,128)(2,1)S(1)}, bf16[256,1024]{1,0:T(8,128)(2,1)S(1)}, bf16[512,256]{1,0:T(8,128)(2,1)S(1)}, bf16[512,256]{1,0:T(8,128)(2,1)S(1)}) custom-call(s32[1]{0:T(128)} %bitcast.h_ref, bf16[512,1024]{1,0:T(8,128)(2,1)S(1)} %get-tuple-element.36.refs_0_, ...), custom_call_target="tpu_custom_call" | custom-call | flops 671088640 | bytes 65536 | tf_op jit(solution)/shard_map/backward_last/pallas_call | solution.py:230
  69.8 1.0 collective-permute-start.14
  70.8 0.1 add_convert_fusion.2
  70.9 1.5 %collective-permute-start.21 = (bf16[512,256]{1,0:T(8,128)(2,1)S(1)}, bf16[512,256]{1,0:T(8,128)(2,1)S(1)}, u32[]{:S(2)}, u32[]{:S(2)}) collective-permute-start(bf16[512,256]{1,0:T(8,128)(2,1)S(1)} %add_convert_fusion.2), channel_id=1, source_target_pairs={{0,56},{8,0},{16,8},{24,16},{32,24},{40,32},{48,40},{56,48},{1,57}... | collective-permute-start | bytes 786440 | tf_op jit(solution)/shard_map/term_2/ppermute | solution.py:462
  72.4 1.4 %collective-permute-start.15 = (bf16[128,1024]{1,0:T(8,128)(2,1)S(1)}, bf16[128,1024]{1,0:T(8,128)(2,1)S(1)}, u32[]{:S(2)}, u32[]{:S(2)}) collective-permute-start(bf16[128,1024]{1,0:T(8,128)(2,1)S(1)} %get-tuple-element.41.refs_6_), channel_id=1, source_target_pairs={{0,64},{64,0},{128,192},{192,128},{1,65},{65,1},{129,193},{193,129... | collective-permute-start | bytes 786440 | tf_op jit(solution)/shard_map/out_1/ppermute | solution.py:456
  73.8 0.0 collective-permute-done.16
  73.8 0.7 fusion.1
  74.5 0.0 collective-permute-start.17
  74.5 6.5 %collective-permute-start.23 = (bf16[512,256]{1,0:T(8,128)(2,1)S(1)}, bf16[512,256]{1,0:T(8,128)(2,1)S(1)}, u32[]{:S(2)}, u32[]{:S(2)}) collective-permute-start(bf16[512,256]{1,0:T(8,128)(2,1)S(1)} %get-tuple-element.62), channel_id=1, source_target_pairs={{0,63},{1,0},{2,1},{3,2},{4,3},{5,4},{6,5},{7,6},{8,7},{9,8},{10,9... | collective-permute-start | bytes 786440 | tf_op jit(solution)/shard_map/term_before/ppermute | solution.py:462
  81.1 0.1 add_convert_fusion.1
  81.1 1.8 %collective-permute-start.22 = (bf16[512,256]{1,0:T(8,128)(2,1)S(1)}, bf16[512,256]{1,0:T(8,128)(2,1)S(1)}, u32[]{:S(2)}, u32[]{:S(2)}) collective-permute-start(bf16[512,256]{1,0:T(8,128)(2,1)S(1)} %add_convert_fusion.1), channel_id=1, source_target_pairs={{0,56},{8,0},{16,8},{24,16},{32,24},{40,32},{48,40},{56,48},{1,57}... | collective-permute-start | bytes 786440 | tf_op jit(solution)/shard_map/term_1/ppermute | solution.py:462
  83.0 0.0 collective-permute-done.15.refs_1_
  83.0 1.1 %collective-permute-start.18 = (bf16[128,1024]{1,0:T(8,128)(2,1)S(1)}, bf16[128,1024]{1,0:T(8,128)(2,1)S(1)}, u32[]{:S(2)}, u32[]{:S(2)}) collective-permute-start(bf16[128,1024]{1,0:T(8,128)(2,1)S(1)} %get-tuple-element.54), channel_id=1, source_target_pairs={{0,64},{64,0},{128,192},{192,128},{1,65},{65,1},{129,193},{193,129... | collective-permute-start | bytes 786440 | tf_op jit(solution)/shard_map/grad_query_1/ppermute | solution.py:456
  84.1 0.0 collective-permute-done.17.refs_3_
  84.1 0.7 copy-done.6
  84.8 2.3 %placed.2 = bf16[128,4096]{1,0:T(8,128)(2,1)} custom-call(s32[1]{0:T(128)} %bitcast.h_ref, bf16[128,1024]{1,0:T(8,128)(2,1)} %copy-done, bf16[128,1024]{1,0:T(8,128)(2,1)} %copy-done.5, bf16[128,1024]{1,0:T(8,128)(2,1)} %get-tuple-element.76.refs_2_, bf16[128,1024]{1,0:T(8,128)(2,1)} %copy-done.6), custom_call_target="tpu_custom_call" | custom-call | bytes 2097152 | tf_op jit(solution)/shard_map/placed/pallas_call | solution.py:428
  87.1 2.0 %collective-permute-done.14 = bf16[256,1024]{1,0:T(8,128)(2,1)S(1)} collective-permute-done((bf16[256,1024]{1,0:T(8,128)(2,1)S(1)}, bf16[256,1024]{1,0:T(8,128)(2,1)S(1)}, u32[]{:S(2)}, u32[]{:S(2)}) %collective-permute-start.14) | collective-permute-done | bytes 524320 | tf_op jit(solution)/shard_map/grad_query_2/ppermute | solution.py:456
  89.1 0.8 fusion
  89.8 2.3 %collective-permute-start.19 = (bf16[128,1024]{1,0:T(8,128)(2,1)S(1)}, bf16[128,1024]{1,0:T(8,128)(2,1)S(1)}, u32[]{:S(2)}, u32[]{:S(2)}) collective-permute-start(bf16[128,1024]{1,0:T(8,128)(2,1)S(1)} %get-tuple-element.73), channel_id=1, source_target_pairs={{0,64},{64,0},{128,192},{192,128},{1,65},{65,1},{129,193},{193,129... | collective-permute-start | bytes 786440 | tf_op jit(solution)/shard_map/grad_query_1/ppermute | solution.py:456
  92.1 0.8 collective-permute-done.22
  92.9 0.1 add_convert_fusion
  93.0 0.6 fusion.2
  93.6 2.3 %collective-permute-start.26 = (bf16[128,256]{1,0:T(8,128)(2,1)S(1)}, bf16[128,256]{1,0:T(8,128)(2,1)S(1)}, u32[]{:S(2)}, u32[]{:S(2)}) collective-permute-start(bf16[128,256]{1,0:T(8,128)(2,1)S(1)} %get-tuple-element.77), channel_id=1, source_target_pairs={{0,192},{64,128},{128,64},{192,0},{1,193},{65,129},{129,65},{193,1... | collective-permute-start | bytes 196616 | tf_op jit(solution)/shard_map/grad_kv_3/ppermute | solution.py:456
  95.9 1.9 %collective-permute-start.25 = (bf16[128,256]{1,0:T(8,128)(2,1)S(1)}, bf16[128,256]{1,0:T(8,128)(2,1)S(1)}, u32[]{:S(2)}, u32[]{:S(2)}) collective-permute-start(bf16[128,256]{1,0:T(8,128)(2,1)S(1)} %get-tuple-element.78), channel_id=1, source_target_pairs={{0,128},{64,192},{128,0},{192,64},{1,129},{65,193},{129,1},{193,65... | collective-permute-start | bytes 196616 | tf_op jit(solution)/shard_map/grad_kv_2/ppermute | solution.py:456
  97.8 0.0 collective-permute-done.18.refs_1_
  97.9 1.4 %collective-permute-done.26.refs_7_ = bf16[128,256]{1,0:T(8,128)(2,1)S(1)} collective-permute-done((bf16[128,256]{1,0:T(8,128)(2,1)S(1)}, bf16[128,256]{1,0:T(8,128)(2,1)S(1)}, u32[]{:S(2)}, u32[]{:S(2)}) %collective-permute-start.26) | collective-permute-done | bytes 65568 | tf_op jit(solution)/shard_map/grad_kv_3/ppermute | solution.py:456
  99.2 1.7 %collective-permute-done.25.refs_6_ = bf16[128,256]{1,0:T(8,128)(2,1)S(1)} collective-permute-done((bf16[128,256]{1,0:T(8,128)(2,1)S(1)}, bf16[128,256]{1,0:T(8,128)(2,1)S(1)}, u32[]{:S(2)}, u32[]{:S(2)}) %collective-permute-start.25) | collective-permute-done | bytes 65568 | tf_op jit(solution)/shard_map/grad_kv_2/ppermute | solution.py:456
  100.9 0.0 collective-permute-done.24.refs_5_
  101.0 0.6 copy-done.8
  101.6 0.1 copy-done.9
  101.6 0.1 copy-done.4
  101.7 2.6 %placed.3 = (bf16[128,4096]{1,0:T(8,128)(2,1)}, f32[128,1024]{1,0:T(8,128)}) custom-call(s32[1]{0:T(128)} %bitcast.h_ref, bf16[128,1024]{1,0:T(8,128)(2,1)} %copy-done.1, bf16[128,1024]{1,0:T(8,128)(2,1)} %copy-done.3, bf16[128,1024]{1,0:T(8,128)(2,1)} %get-tuple-element.74.refs_2_, bf16[128,1024]{1,0:T(8,128)(2,1)} %copy-done.4, ...), custom_call_target="tpu_custom_call" | custom-call | bytes 2097152 | tf_op jit(solution)/shard_map/placed/pallas_call | solution.py:428
  (36 shorter events, 0.2 us)
Async XLA Ops:
  0.6 9.5 %copy-start.10 = (s32[128]{0:T(128)S(1)}, s32[128]{0:T(128)}, u32[]{:S(2)}) copy-start(s32[128]{0:T(128)} %param.7) | copy-start | bytes 1540
  0.6 12.0 %copy-start.2 = (bf16[128,4096]{1,0:T(8,128)(2,1)S(1)}, bf16[128,4096]{1,0:T(8,128)(2,1)}, u32[]{:S(2)}) copy-start(bf16[128,4096]{1,0:T(8,128)(2,1)} %param.4) | copy-start | bytes 3145732
  1.7 8.9 %collective-permute-start.2 = (bf16[128,256]{1,0:T(8,128)(2,1)S(1)}, bf16[128,256]{1,0:T(8,128)(2,1)S(1)}, u32[]{:S(2)}, u32[]{:S(2)}) collective-permute-start(bf16[128,256]{1,0:T(8,128)(2,1)S(1)} %get-tuple-element.81), channel_id=1, source_target_pairs={{0,192},{64,128},{128,64},{192,0},{1,193},{65,129},{129,65},{193,1... | collective-permute-start | bytes 196616 | tf_op jit(solution)/shard_map/kv_3/ppermute | solution.py:456
  5.9 4.3 %collective-permute-start = (bf16[128,256]{1,0:T(8,128)(2,1)S(1)}, bf16[128,256]{1,0:T(8,128)(2,1)S(1)}, u32[]{:S(2)}, u32[]{:S(2)}) collective-permute-start(bf16[128,256]{1,0:T(8,128)(2,1)S(1)} %get-tuple-element.82), channel_id=1, source_target_pairs={{0,64},{64,0},{128,192},{192,128},{1,65},{65,1},{129,193},{193,129... | collective-permute-start | bytes 196616 | tf_op jit(solution)/shard_map/kv_1/ppermute | solution.py:456
  5.9 4.6 %collective-permute-start.1 = (bf16[128,256]{1,0:T(8,128)(2,1)S(1)}, bf16[128,256]{1,0:T(8,128)(2,1)S(1)}, u32[]{:S(2)}, u32[]{:S(2)}) collective-permute-start(bf16[128,256]{1,0:T(8,128)(2,1)S(1)} %get-tuple-element.84), channel_id=1, source_target_pairs={{0,128},{64,192},{128,0},{192,64},{1,129},{65,193},{129,1},{193,65... | collective-permute-start | bytes 196616 | tf_op jit(solution)/shard_map/kv_2/ppermute | solution.py:456
  9.2 14.5 %collective-permute-start.7 = (bf16[256,1024]{1,0:T(8,128)(2,1)S(1)}, bf16[256,1024]{1,0:T(8,128)(2,1)S(1)}, u32[]{:S(2)}, u32[]{:S(2)}) collective-permute-start(bf16[256,1024]{1,0:T(8,128)(2,1)S(1)} %pad_maximum_fusion), channel_id=1, source_target_pairs={{0,64},{64,0},{128,192},{192,128},{1,65},{65,1},{129,193},{193,129... | collective-permute-start | bytes 1572872 | tf_op jit(solution)/shard_map/grad_out_1/ppermute | solution.py:456
  10.6 10.8 %collective-permute-start.10 = (bf16[528,256]{1,0:T(8,128)(2,1)S(1)}, bf16[528,256]{1,0:T(8,128)(2,1)S(1)}, u32[]{:S(2)}, u32[]{:S(2)}) collective-permute-start(bf16[528,256]{1,0:T(8,128)(2,1)S(1)} %constant_dynamic-update-slice_fusion.refs_5_.refs_1_), channel_id=1, source_target_pairs={{0,8},{8,16},{16,24},{24,32},{32,40},{40,48},{48,56},{56,0},{1,9},... | collective-permute-start | bytes 811016 | tf_op jit(solution)/shard_map/w_1/ppermute | solution.py:462
  12.3 19.9 %collective-permute-start.3 = (bf16[528,256]{1,0:T(8,128)(2,1)S(1)}, bf16[528,256]{1,0:T(8,128)(2,1)S(1)}, u32[]{:S(2)}, u32[]{:S(2)}) collective-permute-start(bf16[528,256]{1,0:T(8,128)(2,1)S(1)} %constant_dynamic-update-slice_fusion.refs_5_.refs_1_), channel_id=1, source_target_pairs={{0,1},{1,2},{2,3},{3,4},{4,5},{5,6},{6,7},{7,8},{8,9},{9,10},{10,1... | collective-permute-start | bytes 811016 | tf_op jit(solution)/shard_map/before/ppermute | solution.py:462
  12.7 16.8 %collective-permute-start.9 = (bf16[128,1024]{1,0:T(8,128)(2,1)S(1)}, bf16[128,1024]{1,0:T(8,128)(2,1)S(1)}, u32[]{:S(2)}, u32[]{:S(2)}) collective-permute-start(bf16[128,1024]{1,0:T(8,128)(2,1)S(1)} %get-tuple-element.69), channel_id=1, source_target_pairs={{0,192},{64,128},{128,64},{192,0},{1,193},{65,129},{129,65},{193,1... | collective-permute-start | bytes 786440 | tf_op jit(solution)/shard_map/query_3/ppermute | solution.py:456
  16.7 14.2 %collective-permute-start.8 = (bf16[128,1024]{1,0:T(8,128)(2,1)S(1)}, bf16[128,1024]{1,0:T(8,128)(2,1)S(1)}, u32[]{:S(2)}, u32[]{:S(2)}) collective-permute-start(bf16[128,1024]{1,0:T(8,128)(2,1)S(1)} %get-tuple-element.72), channel_id=1, source_target_pairs={{0,128},{64,192},{128,0},{192,64},{1,129},{65,193},{129,1},{193,65... | collective-permute-start | bytes 786440 | tf_op jit(solution)/shard_map/query_2/ppermute | solution.py:456
  21.4 15.2 %collective-permute-start.6 = (bf16[128,1024]{1,0:T(8,128)(2,1)S(1)}, bf16[128,1024]{1,0:T(8,128)(2,1)S(1)}, u32[]{:S(2)}, u32[]{:S(2)}) collective-permute-start(bf16[128,1024]{1,0:T(8,128)(2,1)S(1)} %get-tuple-element.70), channel_id=1, source_target_pairs={{0,64},{64,0},{128,192},{192,128},{1,65},{65,1},{129,193},{193,129... | collective-permute-start | bytes 786440 | tf_op jit(solution)/shard_map/query_1/ppermute | solution.py:456
  23.7 10.9 %collective-permute-start.12 = (bf16[528,256]{1,0:T(8,128)(2,1)S(1)}, bf16[528,256]{1,0:T(8,128)(2,1)S(1)}, u32[]{:S(2)}, u32[]{:S(2)}) collective-permute-start(bf16[528,256]{1,0:T(8,128)(2,1)S(1)} %collective-permute-done.10.refs_7_.refs_3_), channel_id=1, source_target_pairs={{0,8},{8,16},{16,24},{24,32},{32,40},{40,48},{48,56},{56,0},{1,9},... | collective-permute-start | bytes 811016 | tf_op jit(solution)/shard_map/w_2/ppermute | solution.py:462
  30.8 21.2 %collective-permute-start.11 = (bf16[256,1024]{1,0:T(8,128)(2,1)S(1)}, bf16[256,1024]{1,0:T(8,128)(2,1)S(1)}, u32[]{:S(2)}, u32[]{:S(2)}) collective-permute-start(bf16[256,1024]{1,0:T(8,128)(2,1)S(1)} %pad_maximum_fusion.1), channel_id=1, source_target_pairs={{0,128},{64,192},{128,0},{192,64},{1,129},{65,193},{129,1},{193,65... | collective-permute-start | bytes 1572872 | tf_op jit(solution)/shard_map/grad_out_2/ppermute | solution.py:456
  32.2 4.0 %collective-permute-start.4 = (bf16[16,128]{1,0:T(8,128)(2,1)S(1)}, bf16[16,128]{1,0:T(8,128)(2,1)S(1)}, u32[]{:S(2)}, u32[]{:S(2)}) collective-permute-start(bf16[16,128]{1,0:T(8,128)(2,1)S(1)} %slice_add_fusion), channel_id=1, source_target_pairs={{0,64},{64,0},{128,192},{192,128},{1,65},{65,1},{129,193},{193,129... | collective-permute-start | bytes 12296 | tf_op jit(solution)/shard_map/before_token_1/ppermute | solution.py:456
  34.6 10.8 %collective-permute-start.13 = (bf16[528,256]{1,0:T(8,128)(2,1)S(1)}, bf16[528,256]{1,0:T(8,128)(2,1)S(1)}, u32[]{:S(2)}, u32[]{:S(2)}) collective-permute-start(bf16[528,256]{1,0:T(8,128)(2,1)S(1)} %collective-permute-done.12.refs_2_.refs_10_), channel_id=1, source_target_pairs={{0,8},{8,16},{16,24},{24,32},{32,40},{40,48},{48,56},{56,0},{1,9},... | collective-permute-start | bytes 811016 | tf_op jit(solution)/shard_map/w_3/ppermute | solution.py:462
  36.2 1.2 %collective-permute-start.5 = (bf16[16,128]{1,0:T(8,128)(2,1)S(1)}, bf16[16,128]{1,0:T(8,128)(2,1)S(1)}, u32[]{:S(2)}, u32[]{:S(2)}) collective-permute-start(bf16[16,128]{1,0:T(8,128)(2,1)S(1)} %broadcast_add_fusion), channel_id=1, source_target_pairs={{0,64},{64,0},{128,192},{192,128},{1,65},{65,1},{129,193},{193,129... | collective-permute-start | bytes 12296 | tf_op jit(solution)/shard_map/before_token_1/ppermute | solution.py:456
  49.9 10.9 %copy-start = (bf16[128,1024]{1,0:T(8,128)(2,1)}, bf16[128,1024]{1,0:T(8,128)(2,1)S(1)}, u32[]{:S(2)}) copy-start(bf16[128,1024]{1,0:T(8,128)(2,1)S(1)} %get-tuple-element.40.refs_5_.refs_0_) | copy-start | bytes 786436
  49.9 23.9 %collective-permute-start.16 = (bf16[256,1024]{1,0:T(8,128)(2,1)S(1)}, bf16[256,1024]{1,0:T(8,128)(2,1)S(1)}, u32[]{:S(2)}, u32[]{:S(2)}) collective-permute-start(bf16[256,1024]{1,0:T(8,128)(2,1)S(1)} %get-tuple-element.42.refs_7_), channel_id=1, source_target_pairs={{0,128},{64,192},{128,0},{192,64},{1,129},{65,193},{129,1},{193,65... | collective-permute-start | bytes 1572872 | tf_op jit(solution)/shard_map/out_2/ppermute | solution.py:456
  60.8 10.0 %collective-permute-start.20 = (bf16[512,256]{1,0:T(8,128)(2,1)S(1)}, bf16[512,256]{1,0:T(8,128)(2,1)S(1)}, u32[]{:S(2)}, u32[]{:S(2)}) collective-permute-start(bf16[512,256]{1,0:T(8,128)(2,1)S(1)} %get-tuple-element.57), channel_id=1, source_target_pairs={{0,56},{8,0},{16,8},{24,16},{32,24},{40,32},{48,40},{56,48},{1,57}... | collective-permute-start | bytes 786440 | tf_op jit(solution)/shard_map/term_3/ppermute | solution.py:462
  69.8 4.0 %copy-start.1 = (bf16[128,1024]{1,0:T(8,128)(2,1)}, bf16[128,1024]{1,0:T(8,128)(2,1)S(1)}, u32[]{:S(2)}) copy-start(bf16[128,1024]{1,0:T(8,128)(2,1)S(1)} %get-tuple-element.53.refs_0_) | copy-start | bytes 786436
  69.8 19.3 %collective-permute-start.14 = (bf16[256,1024]{1,0:T(8,128)(2,1)S(1)}, bf16[256,1024]{1,0:T(8,128)(2,1)S(1)}, u32[]{:S(2)}, u32[]{:S(2)}) collective-permute-start(bf16[256,1024]{1,0:T(8,128)(2,1)S(1)} %get-tuple-element.51), channel_id=1, source_target_pairs={{0,128},{64,192},{128,0},{192,64},{1,129},{65,193},{129,1},{193,65... | collective-permute-start | bytes 1572872 | tf_op jit(solution)/shard_map/grad_query_2/ppermute | solution.py:456
  70.9 10.2 %collective-permute-start.21 = (bf16[512,256]{1,0:T(8,128)(2,1)S(1)}, bf16[512,256]{1,0:T(8,128)(2,1)S(1)}, u32[]{:S(2)}, u32[]{:S(2)}) collective-permute-start(bf16[512,256]{1,0:T(8,128)(2,1)S(1)} %add_convert_fusion.2), channel_id=1, source_target_pairs={{0,56},{8,0},{16,8},{24,16},{32,24},{40,32},{48,40},{56,48},{1,57}... | collective-permute-start | bytes 786440 | tf_op jit(solution)/shard_map/term_2/ppermute | solution.py:462
  72.4 10.6 %collective-permute-start.15 = (bf16[128,1024]{1,0:T(8,128)(2,1)S(1)}, bf16[128,1024]{1,0:T(8,128)(2,1)S(1)}, u32[]{:S(2)}, u32[]{:S(2)}) collective-permute-start(bf16[128,1024]{1,0:T(8,128)(2,1)S(1)} %get-tuple-element.41.refs_6_), channel_id=1, source_target_pairs={{0,64},{64,0},{128,192},{192,128},{1,65},{65,1},{129,193},{193,129... | collective-permute-start | bytes 786440 | tf_op jit(solution)/shard_map/out_1/ppermute | solution.py:456
  74.5 9.5 %collective-permute-start.17 = (bf16[128,1024]{1,0:T(8,128)(2,1)S(1)}, bf16[128,1024]{1,0:T(8,128)(2,1)S(1)}, u32[]{:S(2)}, u32[]{:S(2)}) collective-permute-start(bf16[128,1024]{1,0:T(8,128)(2,1)S(1)} %get-tuple-element.75), channel_id=1, source_target_pairs={{0,64},{64,0},{128,192},{192,128},{1,65},{65,1},{129,193},{193,129... | collective-permute-start | bytes 786440 | tf_op jit(solution)/shard_map/out_1/ppermute | solution.py:456
  74.5 17.6 %collective-permute-start.23 = (bf16[512,256]{1,0:T(8,128)(2,1)S(1)}, bf16[512,256]{1,0:T(8,128)(2,1)S(1)}, u32[]{:S(2)}, u32[]{:S(2)}) collective-permute-start(bf16[512,256]{1,0:T(8,128)(2,1)S(1)} %get-tuple-element.62), channel_id=1, source_target_pairs={{0,63},{1,0},{2,1},{3,2},{4,3},{5,4},{6,5},{7,6},{8,7},{9,8},{10,9... | collective-permute-start | bytes 786440 | tf_op jit(solution)/shard_map/term_before/ppermute | solution.py:462
  81.1 11.7 %collective-permute-start.22 = (bf16[512,256]{1,0:T(8,128)(2,1)S(1)}, bf16[512,256]{1,0:T(8,128)(2,1)S(1)}, u32[]{:S(2)}, u32[]{:S(2)}) collective-permute-start(bf16[512,256]{1,0:T(8,128)(2,1)S(1)} %add_convert_fusion.1), channel_id=1, source_target_pairs={{0,56},{8,0},{16,8},{24,16},{32,24},{40,32},{48,40},{56,48},{1,57}... | collective-permute-start | bytes 786440 | tf_op jit(solution)/shard_map/term_1/ppermute | solution.py:462
  83.0 1.1 %copy-start.5 = (bf16[128,1024]{1,0:T(8,128)(2,1)}, bf16[128,1024]{1,0:T(8,128)(2,1)S(1)}, u32[]{:S(2)}) copy-start(bf16[128,1024]{1,0:T(8,128)(2,1)S(1)} %collective-permute-done.15.refs_1_) | copy-start | bytes 786436
  83.0 14.9 %collective-permute-start.18 = (bf16[128,1024]{1,0:T(8,128)(2,1)S(1)}, bf16[128,1024]{1,0:T(8,128)(2,1)S(1)}, u32[]{:S(2)}, u32[]{:S(2)}) collective-permute-start(bf16[128,1024]{1,0:T(8,128)(2,1)S(1)} %get-tuple-element.54), channel_id=1, source_target_pairs={{0,64},{64,0},{128,192},{192,128},{1,65},{65,1},{129,193},{193,129... | collective-permute-start | bytes 786440 | tf_op jit(solution)/shard_map/grad_query_1/ppermute | solution.py:456
  84.1 0.7 copy-start.6
  89.8 11.1 %collective-permute-start.19 = (bf16[128,1024]{1,0:T(8,128)(2,1)S(1)}, bf16[128,1024]{1,0:T(8,128)(2,1)S(1)}, u32[]{:S(2)}, u32[]{:S(2)}) collective-permute-start(bf16[128,1024]{1,0:T(8,128)(2,1)S(1)} %get-tuple-element.73), channel_id=1, source_target_pairs={{0,64},{64,0},{128,192},{192,128},{1,65},{65,1},{129,193},{193,129... | collective-permute-start | bytes 786440 | tf_op jit(solution)/shard_map/grad_query_1/ppermute | solution.py:456
  93.6 5.6 %collective-permute-start.26 = (bf16[128,256]{1,0:T(8,128)(2,1)S(1)}, bf16[128,256]{1,0:T(8,128)(2,1)S(1)}, u32[]{:S(2)}, u32[]{:S(2)}) collective-permute-start(bf16[128,256]{1,0:T(8,128)(2,1)S(1)} %get-tuple-element.77), channel_id=1, source_target_pairs={{0,192},{64,128},{128,64},{192,0},{1,193},{65,129},{129,65},{193,1... | collective-permute-start | bytes 196616 | tf_op jit(solution)/shard_map/grad_kv_3/ppermute | solution.py:456
  95.9 5.0 %collective-permute-start.25 = (bf16[128,256]{1,0:T(8,128)(2,1)S(1)}, bf16[128,256]{1,0:T(8,128)(2,1)S(1)}, u32[]{:S(2)}, u32[]{:S(2)}) collective-permute-start(bf16[128,256]{1,0:T(8,128)(2,1)S(1)} %get-tuple-element.78), channel_id=1, source_target_pairs={{0,128},{64,192},{128,0},{192,64},{1,129},{65,193},{129,1},{193,65... | collective-permute-start | bytes 196616 | tf_op jit(solution)/shard_map/grad_kv_2/ppermute | solution.py:456
  97.8 3.1 %collective-permute-start.24 = (bf16[128,256]{1,0:T(8,128)(2,1)S(1)}, bf16[128,256]{1,0:T(8,128)(2,1)S(1)}, u32[]{:S(2)}, u32[]{:S(2)}) collective-permute-start(bf16[128,256]{1,0:T(8,128)(2,1)S(1)} %get-tuple-element.79), channel_id=1, source_target_pairs={{0,64},{64,0},{128,192},{192,128},{1,65},{65,1},{129,193},{193,129... | collective-permute-start | bytes 196616 | tf_op jit(solution)/shard_map/grad_kv_1/ppermute | solution.py:456
  97.9 3.1 %copy-start.3 = (bf16[128,1024]{1,0:T(8,128)(2,1)}, bf16[128,1024]{1,0:T(8,128)(2,1)S(1)}, u32[]{:S(2)}) copy-start(bf16[128,1024]{1,0:T(8,128)(2,1)S(1)} %collective-permute-done.18.refs_1_) | copy-start | bytes 786436
  99.2 1.8 %copy-start.7 = (bf16[128,256]{1,0:T(8,128)(2,1)}, bf16[128,256]{1,0:T(8,128)(2,1)S(1)}, u32[]{:S(2)}) copy-start(bf16[128,256]{1,0:T(8,128)(2,1)S(1)} %collective-permute-done.26.refs_7_) | copy-start | bytes 196612
  100.9 0.6 copy-start.8
  100.9 0.7 copy-start.9
  101.0 0.7 copy-start.4
